TPU v7x, 32 devices: a whole 2x2x4 slice. The times are simulated.
32 devices in a mesh: dp: 4 (over y, x), fsdp: 8 (over z, core).
Axes of the slice: x: 2, y: 2, z: 4, core: 2. Of those that a mesh axis runs over, the one named last changes fastest.
Arguments:
- tokens: bfloat16 [128, 196, 768], P(('dp', 'fsdp')), may hold values from -6 to 6
- image_counts: int32 [32], P(('dp', 'fsdp')), may hold values from 1 to 4, as said below
- skip_mask: int32 [128, 2, 2], P(('dp', 'fsdp')), may hold values 0 or 1
- norm1_gain: bfloat16 [2, 768], P(None, 'fsdp'), may hold values from 0.5 to 1.5
- norm1_bias: bfloat16 [2, 768], P(None, 'fsdp'), may hold values from -2 to 2
- token_in: bfloat16 [2, 196, 384], P(None, None, 'fsdp'), may hold values from -0.4375 to 0.4375
- token_in_bias: bfloat16 [2, 384], P(None, 'fsdp'), may hold values from -2 to 2
- token_out: bfloat16 [2, 384, 196], P(None, 'fsdp'), may hold values from -0.3125 to 0.3125
- token_out_bias: bfloat16 [2, 196], replicated, may hold values from -2 to 2
- norm2_gain: bfloat16 [2, 768], P(None, 'fsdp'), may hold values from 0.5 to 1.5
- norm2_bias: bfloat16 [2, 768], P(None, 'fsdp'), may hold values from -2 to 2
- channel_in: bfloat16 [2, 768, 3072], P(None, 'fsdp'), may hold values from -0.21875 to 0.21875
- channel_in_bias: bfloat16 [2, 3072], P(None, 'fsdp'), may hold values from -2 to 2
- channel_out: bfloat16 [2, 3072, 768], P(None, 'fsdp'), may hold values from -0.109375 to 0.109375
- channel_out_bias: bfloat16 [2, 768], P(None, 'fsdp'), may hold values from -2 to 2
- cotangent: bfloat16 [128, 196, 768], P(('dp', 'fsdp')), may hold values from -6 to 6
Outputs:
- output: bfloat16 [128, 196, 768], P(('dp', 'fsdp'))
- input_grad: float32 [128, 196, 768], P(('dp', 'fsdp'))
- grad_norm1_gain: float32 [2, 768], P(None, 'fsdp')
- grad_norm1_bias: float32 [2, 768], P(None, 'fsdp')
- grad_token_in: float32 [2, 196, 384], P(None, None, 'fsdp')
- grad_token_in_bias: float32 [2, 384], P(None, 'fsdp')
- grad_token_out: float32 [2, 384, 196], P(None, 'fsdp')
- grad_token_out_bias: float32 [2, 196], replicated
- grad_norm2_gain: float32 [2, 768], P(None, 'fsdp')
- grad_norm2_bias: float32 [2, 768], P(None, 'fsdp')
- grad_channel_in: float32 [2, 768, 3072], P(None, 'fsdp')
- grad_channel_in_bias: float32 [2, 3072], P(None, 'fsdp')
- grad_channel_out: float32 [2, 3072, 768], P(None, 'fsdp')
- grad_channel_out_bias: float32 [2, 768], P(None, 'fsdp')
Inputs may be any that keep to these rules, and one draw needn't show every extreme that they name: `image_counts`: some device holds 4 live images.
All inputs are finite; a program needn't handle non-finite values. No bound on the sum of `skip_mask` on one device may be relied on, other than what follows from the above.
Results may differ from a plain program's by a relative error of at most 0.014.
Values may be sent and summed in bfloat16 or wider, within the bound.
No kernel may reach another device: no remote copies, remote signals or barrier semaphores. Data moves between devices by JAX's collectives and lax.ppermute only.
A program may use at most 256 MiB of HBM per device.

v0:
```python
import jax
import jax.numpy as jnp
from jax import lax
from jax.sharding import PartitionSpec as P

EPSILON = 1e-06


def as_sent(shard):

    def short(part):
        return part.astype(jnp.bfloat16) if part.dtype == jnp.float32 else part

    return jax.tree.map(short, shard)


def layer_norm(values, gain, shift):
    center = values - jnp.mean(values, -1, keepdims=True)
    inv_std = lax.rsqrt(jnp.mean(center * center, -1, keepdims=True) + EPSILON)
    normed = center * inv_std
    return (normed * gain + shift, normed, inv_std)


def norm_back(grad_out, normed, inv_std, gain):
    grad_gain = jnp.sum(grad_out * normed, axis=(0, 1))
    grad_shift = jnp.sum(grad_out, axis=(0, 1))
    scaled = grad_out * gain
    grad_in = inv_std * (
        scaled
        - jnp.mean(scaled, -1, keepdims=True)
        - normed * jnp.mean(scaled * normed, -1, keepdims=True)
    )
    return (grad_in, grad_gain, grad_shift)


def gelu_back(pre_act, grad_out):
    return jax.vjp(jax.nn.gelu, pre_act)[1](grad_out)[0]


def fetch_forward(pieces):
    return (
        lax.all_gather(pieces[0], "fsdp", axis=0, tiled=True),
        lax.all_gather(pieces[1], "fsdp", axis=0, tiled=True),
        lax.all_gather(pieces[2], "fsdp", axis=1, tiled=True),
        lax.all_gather(pieces[3], "fsdp", axis=0, tiled=True),
        lax.all_gather(pieces[4], "fsdp", axis=0, tiled=True),
        lax.all_gather(pieces[5], "fsdp", axis=0, tiled=True),
        lax.all_gather(pieces[6], "fsdp", axis=0, tiled=True),
        lax.all_gather(pieces[7], "fsdp", axis=0, tiled=True),
        lax.all_gather(pieces[8], "fsdp", axis=0, tiled=True),
        lax.all_gather(pieces[9], "fsdp", axis=0, tiled=True),
        lax.all_gather(pieces[10], "fsdp", axis=0, tiled=True),
    )


def fetch_backward(pieces):
    return (
        lax.all_gather(pieces[0], "fsdp", axis=0, tiled=True),
        lax.all_gather(pieces[1], "fsdp", axis=0, tiled=True),
        lax.all_gather(pieces[2], "fsdp", axis=1, tiled=True),
        lax.all_gather(pieces[3], "fsdp", axis=0, tiled=True),
        lax.all_gather(pieces[4], "fsdp", axis=0, tiled=True),
        lax.all_gather(pieces[5], "fsdp", axis=0, tiled=True),
        lax.all_gather(pieces[6], "fsdp", axis=0, tiled=True),
        lax.all_gather(pieces[7], "fsdp", axis=0, tiled=True),
        lax.all_gather(pieces[8], "fsdp", axis=0, tiled=True),
        lax.all_gather(pieces[9], "fsdp", axis=0, tiled=True),
        lax.all_gather(pieces[10], "fsdp", axis=0, tiled=True),
    )


def shards(
    tokens,
    image_counts,
    skip_mask,
    norm1_gain,
    norm1_bias,
    token_in,
    token_in_bias,
    token_out,
    token_out_bias,
    norm2_gain,
    norm2_bias,
    channel_in,
    channel_in_bias,
    channel_out,
    channel_out_bias,
    cotangent,
):
    f32 = jnp.float32
    bf16 = jnp.bfloat16
    slots = tokens.shape[0]
    layers = norm1_gain.shape[0]
    live = (jnp.arange(slots, dtype=jnp.int32) < image_counts[0]).astype(f32)
    branch_scale = live[:, None, None] * skip_mask.astype(f32)

    def layer_pieces(index):
        return (
            norm1_gain[index],
            norm1_bias[index],
            token_in[index],
            token_in_bias[index],
            token_out[index],
            norm2_gain[index],
            norm2_bias[index],
            channel_in[index],
            channel_in_bias[index],
            channel_out[index],
            channel_out_bias[index],
        )

    values = tokens.astype(f32)
    saved = []
    kept_weights = []
    for index in range(layers):
        weights = fetch_forward(layer_pieces(index))
        kept_weights.append(weights)
        gain1, shift1, w_tin, b_tin, w_tout, gain2, shift2, w_cin, b_cin, w_cout, b_cout = weights
        tok_bias = token_out_bias[index].astype(f32)
        normed1, plain1, inv1 = layer_norm(values, gain1.astype(f32), shift1.astype(f32))
        normed1 = normed1.astype(bf16)
        pre_tok = jnp.einsum(
            "isd,sk->idk", normed1, w_tin, preferred_element_type=f32
        ) + b_tin.astype(f32)
        hidden1 = jax.nn.gelu(pre_tok).astype(bf16)
        branch = (
            jnp.einsum("idk,ks->isd", hidden1, w_tout, preferred_element_type=f32)
            + tok_bias[None, :, None]
        )
        middle = values + branch_scale[:, index, 0][:, None, None] * branch
        normed2, plain2, inv2 = layer_norm(middle, gain2.astype(f32), shift2.astype(f32))
        normed2 = normed2.astype(bf16)
        pre_chan = jnp.einsum(
            "isd,df->isf", normed2, w_cin, preferred_element_type=f32
        ) + b_cin.astype(f32)
        hidden2 = jax.nn.gelu(pre_chan).astype(bf16)
        branch = jnp.einsum(
            "isf,fd->isd", hidden2, w_cout, preferred_element_type=f32
        ) + b_cout.astype(f32)
        values = middle + branch_scale[:, index, 1][:, None, None] * branch
        saved.append(
            (normed1, plain1, inv1, pre_tok, hidden1, normed2, plain2, inv2, pre_chan, hidden2)
        )
    output = values.astype(bf16)
    grad = cotangent.astype(f32)
    local_grads = [None] * layers
    bias_grads = [None] * layers
    for index in reversed(range(layers)):
        weights = fetch_backward(layer_pieces(index))
        gain1, shift1, w_tin, b_tin, w_tout, gain2, shift2, w_cin, b_cin, w_cout, b_cout = weights
        normed1, plain1, inv1, pre_tok, hidden1, normed2, plain2, inv2, pre_chan, hidden2 = saved[
            index
        ]
        out_chan = branch_scale[:, index, 1][:, None, None] * grad
        grad_b_cout = jnp.sum(out_chan, axis=(0, 1))
        low_chan = out_chan.astype(bf16)
        grad_w_cout = jnp.einsum("isf,isd->fd", hidden2, low_chan, preferred_element_type=f32)
        back_hidden = jnp.einsum("isd,fd->isf", low_chan, w_cout, preferred_element_type=f32)
        pre_grad = gelu_back(pre_chan, back_hidden)
        grad_b_cin = jnp.sum(pre_grad, axis=(0, 1))
        low_pre = pre_grad.astype(bf16)
        grad_w_cin = jnp.einsum("isd,isf->df", normed2, low_pre, preferred_element_type=f32)
        back_norm = jnp.einsum("isf,df->isd", low_pre, w_cin, preferred_element_type=f32)
        norm_in, grad_gain2, grad_shift2 = norm_back(back_norm, plain2, inv2, gain2.astype(f32))
        grad_mid = grad + norm_in
        out_tok = branch_scale[:, index, 0][:, None, None] * grad_mid
        bias_grads[index] = jnp.sum(out_tok, axis=(0, 2))
        low_tok = out_tok.astype(bf16)
        grad_w_tout = jnp.einsum("idk,isd->ks", hidden1, low_tok, preferred_element_type=f32)
        back_hidden = jnp.einsum("isd,ks->idk", low_tok, w_tout, preferred_element_type=f32)
        pre_grad = gelu_back(pre_tok, back_hidden)
        grad_b_tin = jnp.sum(pre_grad, axis=(0, 1))
        low_pre = pre_grad.astype(bf16)
        grad_w_tin = jnp.einsum("isd,idk->sk", normed1, low_pre, preferred_element_type=f32)
        back_norm = jnp.einsum("idk,sk->isd", low_pre, w_tin, preferred_element_type=f32)
        norm_in, grad_gain1, grad_shift1 = norm_back(back_norm, plain1, inv1, gain1.astype(f32))
        grad = grad_mid + norm_in
        local = (
            grad_gain1,
            grad_shift1,
            grad_w_tin,
            grad_b_tin,
            grad_w_tout,
            grad_gain2,
            grad_shift2,
            grad_w_cin,
            grad_b_cin,
            grad_w_cout,
            grad_b_cout,
        )
        local_grads[index] = local
    token_bias_total = lax.psum(jnp.stack(bias_grads), ("dp", "fsdp"))
    joined = tuple(
        (
            jnp.stack([local_grads[index][position] for index in range(layers)])
            for position in range(11)
        )
    )
    owned = (
        lax.psum_scatter(joined[0], "fsdp", scatter_dimension=1, tiled=True),
        lax.psum_scatter(joined[1], "fsdp", scatter_dimension=1, tiled=True),
        lax.psum_scatter(joined[2], "fsdp", scatter_dimension=2, tiled=True),
        lax.psum_scatter(joined[3], "fsdp", scatter_dimension=1, tiled=True),
        lax.psum_scatter(joined[4], "fsdp", scatter_dimension=1, tiled=True),
        lax.psum_scatter(joined[5], "fsdp", scatter_dimension=1, tiled=True),
        lax.psum_scatter(joined[6], "fsdp", scatter_dimension=1, tiled=True),
        lax.psum_scatter(joined[7], "fsdp", scatter_dimension=1, tiled=True),
        lax.psum_scatter(joined[8], "fsdp", scatter_dimension=1, tiled=True),
        lax.psum_scatter(joined[9], "fsdp", scatter_dimension=1, tiled=True),
        lax.psum_scatter(joined[10], "fsdp", scatter_dimension=1, tiled=True),
    )
    results = jax.tree.map(lambda part: part.astype(jnp.float32), lax.psum(as_sent(owned), "dp"))
    return (
        output,
        grad,
        results[0],
        results[1],
        results[2],
        results[3],
        results[4],
        token_bias_total,
        results[5],
        results[6],
        results[7],
        results[8],
        results[9],
        results[10],
    )


def solution(mesh):
    in_specs = (
        P(("dp", "fsdp"), None, None),
        P(("dp", "fsdp")),
        P(("dp", "fsdp"), None, None),
        P(None, "fsdp"),
        P(None, "fsdp"),
        P(None, None, "fsdp"),
        P(None, "fsdp"),
        P(None, "fsdp", None),
        P(),
        P(None, "fsdp"),
        P(None, "fsdp"),
        P(None, "fsdp", None),
        P(None, "fsdp"),
        P(None, "fsdp", None),
        P(None, "fsdp"),
        P(("dp", "fsdp"), None, None),
    )
    out_specs = (
        P(("dp", "fsdp"), None, None),
        P(("dp", "fsdp"), None, None),
        P(None, "fsdp"),
        P(None, "fsdp"),
        P(None, None, "fsdp"),
        P(None, "fsdp"),
        P(None, "fsdp", None),
        P(),
        P(None, "fsdp"),
        P(None, "fsdp"),
        P(None, "fsdp", None),
        P(None, "fsdp"),
        P(None, "fsdp", None),
        P(None, "fsdp"),
    )
    return jax.shard_map(shards, mesh=mesh, in_specs=in_specs, out_specs=out_specs, check_vma=False)
```

profile of v0, /device:TPU:0, one launch (start us, length us, event | category | flops | bytes accessed | tf_op | source)
XLA Modules:
  0.0 1040.8 jit_solution(1570142752944004867)
XLA Ops:
  7.2 2.4 fusion.93
  17.6 32.2 %all-reduce.15 = (bf16[768]{0:T(1024)(128)(2,1)S(1)}, bf16[768]{0:T(1024)(128)(2,1)S(1)}, bf16[384]{0:T(512)(128)(2,1)S(1)}, bf16[768]{0:T(1024)(128)(2,1)S(1)},...) all-reduce(bf16[768]{0:T(1024)(128)(2,1)S(1)} %dynamic-update-slice, ...), channel_id=3, replica_groups=mesh['dp'=4,'fsdp'=8] {'fsdp'}, use_global_device_ids=true, to_apply=%add.1 | all-reduce | flops 8448 | bytes 33792
  50.8 12.9 %all-gather.19 = bf16[1,3072]{1,0:T(2,128)(2,1)S(1)} all-gather(bf16[1,384]{1,0:T(2,128)(2,1)S(1)} %get-tuple-element.100), channel_id=21, replica_groups=mesh['dp'=4,'fsdp'=8] {'fsdp'}, dimensions={1}, use_global_device_ids=true | all-gather | bytes 6912 | tf_op jit(solution)/shard_map/all_gather | solution.py:50
  63.7 12.7 %all-gather.8 = bf16[1,3072]{1,0:T(2,128)(2,1)S(1)} all-gather(bf16[1,384]{1,0:T(2,128)(2,1)S(1)} %get-tuple-element.101), channel_id=10, replica_groups=mesh['dp'=4,'fsdp'=8] {'fsdp'}, dimensions={1}, use_global_device_ids=true | all-gather | bytes 6912 | tf_op jit(solution)/shard_map/all_gather | solution.py:50
  76.4 14.8 %all-gather.4 = bf16[1,384,196]{2,1,0:T(8,128)(2,1)S(1)} all-gather(bf16[1,48,196]{2,1,0:T(8,128)(2,1)S(1)} %get-tuple-element.95), channel_id=6, replica_groups=mesh['dp'=4,'fsdp'=8] {'fsdp'}, dimensions={1}, use_global_device_ids=true | all-gather | bytes 169344 | tf_op jit(solution)/shard_map/all_gather | solution.py:46
  91.2 14.9 %all-gather.2 = bf16[1,196,384]{1,2,0:T(8,128)(2,1)S(1)} all-gather(bf16[1,196,48]{1,2,0:T(8,128)(2,1)S(1)} %get-tuple-element.93), channel_id=4, replica_groups=mesh['dp'=4,'fsdp'=8] {'fsdp'}, dimensions={2}, use_global_device_ids=true | all-gather | bytes 169344 | tf_op jit(solution)/shard_map/all_gather | solution.py:44
  106.1 1.6 fusion.78
  107.8 2.3 fusion.99
  110.1 14.6 %all-gather.15 = bf16[1,384,196]{2,1,0:T(8,128)(2,1)S(1)} all-gather(bf16[1,48,196]{2,1,0:T(8,128)(2,1)S(1)} %get-tuple-element.94), channel_id=17, replica_groups=mesh['dp'=4,'fsdp'=8] {'fsdp'}, dimensions={1}, use_global_device_ids=true | all-gather | bytes 169344 | tf_op jit(solution)/shard_map/all_gather | solution.py:46
  124.7 14.6 %all-gather.13 = bf16[1,196,384]{1,2,0:T(8,128)(2,1)S(1)} all-gather(bf16[1,196,48]{1,2,0:T(8,128)(2,1)S(1)} %get-tuple-element.92), channel_id=15, replica_groups=mesh['dp'=4,'fsdp'=8] {'fsdp'}, dimensions={2}, use_global_device_ids=true | all-gather | bytes 169344 | tf_op jit(solution)/shard_map/all_gather | solution.py:44
  139.9 9.5 fusion.38
  149.4 12.4 %fusion.100 = (f32[4,196]{1,0:T(4,128)S(1)}, f32[4,196,768]{2,1,0:T(8,128)S(1)}) fusion(f32[4,196,768]{2,1,0:T(8,128)} %copy-done.4, f32[768]{0:T(1024)S(1)} %convert_element_type.281, bf16[1,3072,768]{2,1,0:T(8,128)(2,1)} %all-gather.29.cloned.1.call-done, f32[4,196,3072]{2,1,0:T(8,128)} %fusion.38, f32[3072]{0:T(1024)S(1)} %bitcast.221, ...), kind=kOutput, calls=%fused_computation.193 | convolution fusion | flops 3725868288 | bytes 19187792 | tf_op jit(solution)/shard_map/isf,fd->isd/dot_general | solution.py:137
  162.3 1.6 fusion.87
  163.8 2.4 fusion.101
  166.2 1.4 copy-done
  168.1 7.1 all-gather.31.cloned.1.call-done
  175.2 7.3 fusion.30
  182.5 3.9 copy-done.51
  186.4 9.9 convolution_bitcast_fusion
  196.3 31.6 %all-gather.33.cloned.1.call-done = bf16[1,3072,768]{2,1,0:T(8,128)(2,1)} async-done(((bf16[1,384,768]{2,1,0:T(8,128)(2,1)}), bf16[1,3072,768]{2,1,0:T(8,128)(2,1)}) %all-gather.33.cloned.1.call-update) | async-done | bytes 4718608 | tf_op jit(solution)/shard_map/all_gather | solution.py:51
  227.9 13.5 %fusion.104 = (f32[3072]{0:T(1024)S(1)}, bf16[4,196,3072]{2,1,0:T(8,128)(2,1)S(1)}) fusion(f32[4,196,3072]{2,1,0:T(8,128)} %copy-done.51, f32[3072]{0:T(1024)S(1)} %bitcast.219, bf16[1,3072,768]{2,1,0:T(8,128)(2,1)} %all-gather.33.cloned.1.call-done, f32[4]{0:T(128)S(1)} %get-tuple-element.96, bf16[4,196,768]{2,0,1:T(4,128)(2,1)} %param.31), kind=kOutput, calls=%fused_computation.197 | convolution fusion | flops 3754165248 | bytes 20398096 | tf_op jit(solution)/shard_map/isd,fd->isf/dot_general | solution.py:158
  241.5 8.7 multiply_reduce_fusion
  250.3 1.6 multiply_reduce_fusion.10
  251.9 6.8 fusion.102
  258.7 2.8 fusion.60
  261.5 1.9 reduce_sum.307
  263.4 2.9 multiply_reduce_fusion.9
  266.4 12.8 %convolution_bitcast_fusion.1 = f32[1,3072,768]{2,1,0:T(8,128)} fusion(f32[4,196,768]{2,1,0:T(8,128)S(1)} %get-tuple-element.86, f32[4]{0:T(128)S(1)} %get-tuple-element.98, f32[4,196,3072]{2,1,0:T(8,128)} %fusion.38, f32[3072]{0:T(1024)S(1)} %bitcast.222), kind=kOutput, calls=%fused_computation.25 | convolution fusion | flops 3724664832 | bytes 21491728 | tf_op jit(solution)/shard_map/isf,isd->fd/dot_general | solution.py:157
  279.2 13.7 %fusion.105 = (f32[3072]{0:T(1024)S(1)}, bf16[4,196,3072]{2,1,0:T(8,128)(2,1)S(1)}) fusion(f32[4,196,3072]{2,1,0:T(8,128)} %fusion.38, f32[3072]{0:T(1024)S(1)} %bitcast.223, bf16[1,3072,768]{2,1,0:T(8,128)(2,1)} %all-gather.29.cloned.1.call-done, f32[4,196,768]{2,1,0:T(8,128)S(1)} %get-tuple-element.86, f32[4]{0:T(128)S(1)} %get-tuple-element.98), kind=kOutput, calls=%fused_computation.198 | convolution fusion | flops 3753563136 | bytes 21602320 | tf_op jit(solution)/shard_map/isd,fd->isf/dot_general | solution.py:158
  293.0 4.7 multiply_reduce_fusion.1
  299.1 5.4 fusion.103
  305.5 4.9 fusion.58
  310.4 1.9 reduce_sum.306
  317.7 1.7 copy.62
  319.4 14.7 %pad_maximum_fusion.1 = f32[2,3072,768]{2,1,0:T(8,128)} fusion(f32[1,3072,768]{2,1,0:T(8,128)} %convolution_bitcast_fusion, f32[1,3072,768]{2,1,0:T(8,128)} %convolution_bitcast_fusion.1), kind=kLoop, calls=%fused_computation.1 | loop fusion | flops 4718592 | bytes 37748736 | tf_op jit(solution)/shard_map/stack | solution.py:195
  334.8 8.6 convolution_bitcast_fusion.3
  343.4 7.7 convolution_bitcast_fusion.2
  351.1 6.9 pad_maximum_fusion
  359.0 5.2 convolution_bitcast_fusion.4
  364.2 4.3 convolution_bitcast_fusion.5
  369.4 1.6 copy.47
  371.0 3.2 convolution_bitcast_fusion.7
  376.0 60.2 %all-reduce.25 = (bf16[2,196,384]{1,0,2:T(2,128)(2,1)S(1)}, bf16[2,384,196]{2,0,1:T(2,128)(2,1)S(1)}) all-reduce(f32[2,196,384]{1,0,2:T(2,128)S(1)} %copy.46, f32[2,384,196]{2,0,1:T(2,128)S(1)} %copy.47), channel_id=26, replica_groups=mesh['dp'=4,'fsdp'=8] {'fsdp'}, use_global_device_ids=true, to_apply=%region_24.0.clone | all-reduce | flops 301056 | bytes 1806336
  438.8 1.4 copy.55
  440.2 1.4 copy.53
  441.6 1.4 copy.61
  443.0 17.2 %reduce-scatter.34.cloned.1.call-done = f32[96,2]{1,0:T(8,128)} async-done(((f32[768,2]{1,0:T(8,128)}), f32[96,2]{1,0:T(8,128)}) %reduce-scatter.34.cloned.1.call-update) | async-done | bytes 784
  460.2 1.4 copy.59
  461.6 29.6 %reduce-scatter.40.cloned.1.call-done = f32[96,2]{1,0:T(8,128)} async-done(((f32[768,2]{1,0:T(8,128)}), f32[96,2]{1,0:T(8,128)}) %reduce-scatter.40.cloned.1.call-update) | async-done | bytes 784
  492.6 33.9 %reduce-scatter.38.cloned.1.call-done = f32[384,2]{1,0:T(8,128)} async-done(((f32[3072,2]{1,0:T(8,128)}), f32[384,2]{1,0:T(8,128)}) %reduce-scatter.38.cloned.1.call-update) | async-done | bytes 3088
  526.5 1.6 copy.63
  528.5 186.3 %reduce-scatter.26.cloned.1.call-done = f32[2,384,768]{2,1,0:T(8,128)} async-done(((f32[2,3072,768]{2,1,0:T(8,128)}), f32[2,384,768]{2,1,0:T(8,128)}) %reduce-scatter.26.cloned.1.call-update) | async-done | bytes 2359312 | tf_op jit(solution)/shard_map/reduce_scatter | solution.py:209
  714.7 2.8 convert_element_type.256
  717.5 185.9 %reduce-scatter.24.cloned.1.call-done = f32[2,96,3072]{2,1,0:T(8,128)} async-done(((f32[2,768,3072]{2,1,0:T(8,128)}), f32[2,96,3072]{2,1,0:T(8,128)}) %reduce-scatter.24.cloned.1.call-update) | async-done | bytes 2359312 | tf_op jit(solution)/shard_map/reduce_scatter | solution.py:207
  903.4 2.8 convert_element_type.252
  906.3 11.5 %add_convert_fusion = bf16[4,196,768]{2,1,0:T(8,128)(2,1)S(1)} fusion(f32[4,196,768]{2,1,0:T(8,128)S(1)} %copy-done.3, bf16[1,3072,768]{2,1,0:T(8,128)(2,1)} %all-gather.33.cloned.1.call-done, f32[768]{0:T(1024)S(1)} %convert_element_type.287, f32[4]{0:T(128)S(1)} %get-tuple-element.96, f32[4,196,3072]{2,1,0:T(8,128)} %copy-done.51, f32[3072]{0:T(1024)S(1)} %bitcast.220), kind=kOutput, calls=%fused_computation.95 | convolution fusion | flops 3725869056 | bytes 17980432 | tf_op jit(solution)/shard_map/isf,fd->isd/dot_general | solution.py:137
  917.8 1.5 copy.48
  920.3 2.4 copy.49
  922.7 37.8 %psum.89 = f32[2,196]{1,0:T(2,128)} all-reduce(f32[2,196]{1,0:T(2,128)S(1)} %pad_maximum_fusion.11), channel_id=1, replica_groups=mesh['dp'=4,'fsdp'=8] {'dp','fsdp'}, use_global_device_ids=true, to_apply=%region_34.0 | all-reduce | flops 392 | bytes 3136 | tf_op jit(solution)/shard_map/psum | solution.py:192
  969.0 1.4 copy.50
  970.4 1.4 copy.51
  971.9 57.3 %all-reduce.24.cloned.1.call-done = (bf16[2,96,3072]{2,1,0:T(8,128)(2,1)}, bf16[2,384,768]{2,1,0:T(8,128)(2,1)}) async-done(((bf16[2,96,3072]{2,1,0:T(8,128)(2,1)}, bf16[2,384,768]{2,1,0:T(8,128)(2,1)}), (bf16[2,96,3072]{2,1,0:T(8,128)(2,1)}, bf16[2,384,768]{2,1,0:T(8,128)(2,1)})) %all-reduce.24.cloned.1.call-update) | async-done | bytes 2359312 | tf_op jit(solution)/shard_map/psum | solution.py:212
  1029.2 3.0 convert_element_type.253
  1032.2 1.6 convert_element_type.257
  (265 shorter events, 33.0 us)
Async XLA Ops:
  7.2 2.6 copy-start.23
  7.2 132.6 %all-gather.27.cloned.1.call-start = ((), (), s32[]{:S(2)}) async-start(), calls=%async_computation.11 | async-start | bytes 5308416 | tf_op jit(solution)/shard_map/all_gather | solution.py:49
  9.6 3.3 copy-start.43
  9.7 5.2 copy-start.45
  9.7 5.3 copy-start.46
  9.7 5.3 copy-start.47
  9.7 5.3 copy-start.48
  9.7 5.3 copy-start.49
  9.7 5.3 copy-start.50
  9.7 5.3 copy-start.44
  9.7 40.1 %copy-start.41 = (bf16[2,196]{1,0:T(2,128)(2,1)S(1)}, bf16[2,196]{1,0:T(2,128)(2,1)}, u32[]{:S(2)}) copy-start(bf16[2,196]{1,0:T(2,128)(2,1)} %param.24) | copy-start | bytes 2356
  9.7 40.2 %copy-start.40 = (bf16[2,384]{1,0:T(2,128)(2,1)S(1)}, bf16[2,384]{1,0:T(2,128)(2,1)}, u32[]{:S(2)}) copy-start(bf16[2,384]{1,0:T(2,128)(2,1)} %param.28) | copy-start | bytes 4612
  9.7 40.3 %copy-start.6 = (bf16[4,196,768]{2,0,1:T(4,128)(2,1)S(1)}, bf16[4,196,768]{2,0,1:T(4,128)(2,1)}, u32[]{:S(2)}) copy-start(bf16[4,196,768]{2,0,1:T(4,128)(2,1)} %param.16) | copy-start | bytes 3612676
  9.8 139.6 %all-gather.29.cloned.1.call-start = ((), (), s32[]{:S(2)}) async-start(), calls=%async_computation.12 | async-start | bytes 5308416 | tf_op jit(solution)/shard_map/all_gather | solution.py:51
  10.9 65.5 %copy-start.30 = (bf16[2,196,48]{1,2,0:T(8,128)(2,1)S(1)}, bf16[2,196,48]{1,2,0:T(8,128)(2,1)}, u32[]{:S(2)}) copy-start(bf16[2,196,48]{1,2,0:T(8,128)(2,1)} %param.21) | copy-start | bytes 112900
  10.9 65.5 %copy-start.31 = (bf16[2,48,196]{2,1,0:T(8,128)(2,1)S(1)}, bf16[2,48,196]{2,1,0:T(8,128)(2,1)}, u32[]{:S(2)}) copy-start(bf16[2,48,196]{2,1,0:T(8,128)(2,1)} %param.23) | copy-start | bytes 112900
  10.9 164.3 %all-gather.31.cloned.1.call-start = ((), (), s32[]{:S(2)}) async-start(), calls=%async_computation.13 | async-start | bytes 5308416 | tf_op jit(solution)/shard_map/all_gather | solution.py:49
  11.7 216.2 %all-gather.33.cloned.1.call-start = ((), (), s32[]{:S(2)}) async-start(), calls=%async_computation.14 | async-start | bytes 5308416 | tf_op jit(solution)/shard_map/all_gather | solution.py:51
  12.3 425.2 %reduce-scatter.32.cloned.1.call-start = ((), (), s32[]{:S(2)}) async-start(), calls=%async_computation.17 | async-start | bytes 221184
  49.9 57.9 %copy-start.38 = (f32[768]{0:T(1024)}, f32[768]{0:T(1024)S(1)}, u32[]{:S(2)}) copy-start(f32[768]{0:T(1024)S(1)} %convert_element_type.277) | copy-start | bytes 9220
  49.9 57.8 %copy-start.32 = (f32[768]{0:T(1024)}, f32[768]{0:T(1024)S(1)}, u32[]{:S(2)}) copy-start(f32[768]{0:T(1024)S(1)} %convert_element_type.276) | copy-start | bytes 9220
  50.0 89.9 %copy-start.26 = (f32[768]{0:T(1024)}, f32[768]{0:T(1024)S(1)}, u32[]{:S(2)}) copy-start(f32[768]{0:T(1024)S(1)} %convert_element_type.280) | copy-start | bytes 9220
  50.0 112.3 %copy-start.36 = (f32[768]{0:T(1024)}, f32[768]{0:T(1024)S(1)}, u32[]{:S(2)}) copy-start(f32[768]{0:T(1024)S(1)} %convert_element_type.283) | copy-start | bytes 9220
  50.3 57.5 %copy-start.28 = (f32[4,196]{1,0:T(4,128)}, f32[4,196]{1,0:T(4,128)S(1)}, u32[]{:S(2)}) copy-start(f32[4,196]{1,0:T(4,128)S(1)} %broadcast_multiply_fusion.11) | copy-start | bytes 9412
  50.8 57.0 %copy-start.34 = (f32[4,196]{1,0:T(4,128)}, f32[4,196]{1,0:T(4,128)S(1)}, u32[]{:S(2)}) copy-start(f32[4,196]{1,0:T(4,128)S(1)} %add_rsqrt_fusion.3) | copy-start | bytes 9412
  110.1 39.3 %copy-start.4 = (f32[4,196,768]{2,1,0:T(8,128)}, f32[4,196,768]{2,1,0:T(8,128)S(1)}, u32[]{:S(2)}) copy-start(f32[4,196,768]{2,1,0:T(8,128)S(1)} %get-tuple-element.119) | copy-start | bytes 7225348
  175.2 11.2 %copy-start.20 = (bf16[4,196,768]{2,0,1:T(4,128)(2,1)S(1)}, bf16[4,196,768]{2,0,1:T(4,128)(2,1)}, u32[]{:S(2)}) copy-start(bf16[4,196,768]{2,0,1:T(4,128)(2,1)} %param.31) | copy-start | bytes 3612676
  182.5 3.9 copy-start.51
  227.9 13.6 %copy-start.1 = (f32[4,196,768]{2,1,0:T(8,128)S(1)}, f32[4,196,768]{2,1,0:T(8,128)}, u32[]{:S(2)}) copy-start(f32[4,196,768]{2,1,0:T(8,128)} %copy-done) | copy-start | bytes 7225348
  241.5 8.7 copy-start.14
  241.5 8.7 copy-start.21
  251.8 6.8 copy-start.13
  258.7 2.9 copy-start.18
  266.4 26.6 %slice-start.2 = ((s8[4718592]{0:T(1024)(128)(4,1)}), s8[4194304]{0:T(1024)(128)(4,1)S(1)}, s32[]{:S(2)}) async-start(s8[4718592]{0:T(1024)(128)(4,1)} %bitcast.230), calls=%async_computation.26 | async-start | bytes 8388608
  266.4 32.7 %slice-start = ((s8[4718592]{0:T(1024)(128)(4,1)}), s8[4194304]{0:T(1024)(128)(4,1)S(1)}, s32[]{:S(2)}) async-start(s8[4718592]{0:T(1024)(128)(4,1)} %bitcast.203), calls=%async_computation.24 | async-start | bytes 8388608
  279.2 13.8 %copy-start.5 = (f32[4,196,768]{2,1,0:T(8,128)S(1)}, f32[4,196,768]{2,1,0:T(8,128)}, u32[]{:S(2)}) copy-start(f32[4,196,768]{2,1,0:T(8,128)} %copy-done.4) | copy-start | bytes 7225348
  279.2 13.8 %slice-start.3 = ((s8[4718592]{0:T(1024)(128)(4,1)}), s8[524288]{0:T(1024)(128)(4,1)S(1)}, s32[]{:S(2)}) async-start(s8[4718592]{0:T(1024)(128)(4,1)} %bitcast.230), calls=%async_computation.27 | async-start | bytes 1048576
  279.2 19.9 %slice-start.1 = ((s8[4718592]{0:T(1024)(128)(4,1)}), s8[524288]{0:T(1024)(128)(4,1)S(1)}, s32[]{:S(2)}) async-start(s8[4718592]{0:T(1024)(128)(4,1)} %bitcast.203), calls=%async_computation.25 | async-start | bytes 1048576
  292.9 4.7 copy-start.15
  299.1 5.5 copy-start.9
  299.1 6.4 copy-start.25
  299.1 6.4 copy-start.29
  299.1 6.4 copy-start.33
  299.1 6.4 copy-start.35
  305.5 133.4 %reduce-scatter.30.cloned.1.call-start = ((), (), s32[]{:S(2)}) async-start(), calls=%async_computation.16 | async-start | bytes 442368
  313.3 126.9 %reduce-scatter.28.cloned.1.call-start = ((), (), s32[]{:S(2)}) async-start(), calls=%async_computation.15 | async-start | bytes 442368
  314.4 127.2 %reduce-scatter.36.cloned.1.call-start = ((), (), s32[]{:S(2)}) async-start(), calls=%async_computation.19 | async-start | bytes 442368
  315.5 144.7 %reduce-scatter.34.cloned.1.call-start = ((), (), s32[]{:S(2)}) async-start(), calls=%async_computation.18 | async-start | bytes 442368
  316.5 174.7 %reduce-scatter.40.cloned.1.call-start = ((), (), s32[]{:S(2)}) async-start(), calls=%async_computation.21 | async-start | bytes 442368
  317.6 208.9 %reduce-scatter.38.cloned.1.call-start = ((), (), s32[]{:S(2)}) async-start(), calls=%async_computation.20 | async-start | bytes 1769472
  319.3 395.4 %reduce-scatter.26.cloned.1.call-start = ((), (), s32[]{:S(2)}) async-start(), calls=%async_computation.10 | async-start | bytes 21233664 | tf_op jit(solution)/shard_map/reduce_scatter | solution.py:209
  334.1 569.3 %reduce-scatter.24.cloned.1.call-start = ((), (), s32[]{:S(2)}) async-start(), calls=%async_computation.9 | async-start | bytes 21233664 | tf_op jit(solution)/shard_map/reduce_scatter | solution.py:207
  334.8 8.6 copy-start.2
  358.1 602.5 %all-reduce.22.cloned.1.call-start = ((), (), s32[]{:S(2)}) async-start(), calls=%async_computation.22 | async-start | bytes 205824 | tf_op jit(solution)/shard_map/psum | solution.py:212
  359.0 5.2 copy-start.10
  368.5 2.4 copy-start.39
  371.0 3.2 copy-start.19
  371.0 3.2 copy-start.37
  375.2 153.2 %copy-start.42 = (bf16[768]{0:T(1024)(128)(2,1)S(1)}, bf16[768]{0:T(1024)(128)(2,1)}, u32[]{:S(2)}) copy-start(bf16[768]{0:T(1024)(128)(2,1)} %get-tuple-element.69) | copy-start | bytes 4612
  528.1 501.1 %all-reduce.24.cloned.1.call-start = ((), (), s32[]{:S(2)}) async-start(), calls=%async_computation.23 | async-start | bytes 4718592 | tf_op jit(solution)/shard_map/psum | solution.py:212
  717.5 188.8 %copy-start.3 = (f32[4,196,768]{2,1,0:T(8,128)S(1)}, f32[4,196,768]{2,1,0:T(8,128)}, u32[]{:S(2)}) copy-start(f32[4,196,768]{2,1,0:T(8,128)} %copy-done) | copy-start | bytes 7225348
  906.3 13.0 %copy-start.11 = (f32[4,196,768]{2,1,0:T(8,128)S(1)}, f32[4,196,768]{2,1,0:T(8,128)}, u32[]{:S(2)}) copy-start(f32[4,196,768]{2,1,0:T(8,128)} %copy-done.9) | copy-start | bytes 7225348
  906.3 13.0 %copy-start.12 = (f32[4,768,196]{1,2,0:T(8,128)S(1)}, f32[4,768,196]{1,2,0:T(8,128)}, u32[]{:S(2)}) copy-start(f32[4,768,196]{1,2,0:T(8,128)} %get-tuple-element.127) | copy-start | bytes 7225348
  1029.2 3.0 copy-start.22
  (7 other events, 11.7 us)
Sparse Core Ops, SparseCore 0:
  10.2 54.9 all-gather.26
  67.5 54.6 all-gather.28
  124.4 50.7 all-gather.30
  177.3 50.6 all-gather.32
  305.6 29.0 reduce-scatter.31
  336.9 28.7 reduce-scatter.29
  368.0 29.0 reduce-scatter.27
  399.4 29.6 reduce-scatter.35
  431.3 28.8 reduce-scatter.33
  462.4 28.7 reduce-scatter.39
  494.1 32.3 reduce-scatter.37
  528.7 185.9 reduce-scatter.25
  717.1 186.3 reduce-scatter.23
  908.2 41.7 all-reduce.21
  953.9 75.2 all-reduce.23
where the time goes:
time: 1050 us; the launch traced here: 1040 us
  waiting for transfers between devices  550 us (52%)
  blocking collectives  215 us (20%)
  matrix products  162 us (15%)
  other arithmetic  54.1 us (5%)
  local copies, waits for them, and re-layouts  40.3 us (4%)
  between operations  18.2 us (2%)
    reduce_scatter x1, waiting for transfers between devices, shards(): lax.psum_scatter(joined[9], 'fsdp', scatter_dimension=1, tiled=True)  186 us
    reduce_scatter x1, waiting for transfers between devices, shards(): lax.psum_scatter(joined[7], 'fsdp', scatter_dimension=1, tiled=True)  186 us
    unnamed x2, blocking collectives  92.4 us
    unnamed x22, waiting for transfers between devices  82.2 us
    psum x2, waiting for transfers between devices, shards(): lax.psum(as_sent(owned), 'dp')  57.3 us
    psum x1, blocking collectives, shards(): token_bias_total = lax.psum(jnp.stack(bias_grads), ('dp', 'fsdp'))  37.8 us
    unnamed x161, local copies, waits for them, and re-layouts  33.2 us
    all_gather x2, waiting for transfers between devices, fetch_forward(): lax.all_gather(pieces[9], 'fsdp', axis=0, tiled=True)  31.6 us
  transfers between devices with their start and end apart: 15, of which 8 were waited for; matrix products, arithmetic and copies ran while one was open for 16% of the time, Pallas kernels for 0%

commit v1 on v0

--- a/solution.py
+++ b/solution.py
@@ -1,9 +1,18 @@
+import functools
+import math
+
 import jax
 import jax.numpy as jnp
 from jax import lax
+from jax.experimental import pallas as pl
+from jax.experimental.pallas import tpu as pltpu
 from jax.sharding import PartitionSpec as P
 
 EPSILON = 1e-06
+GELU_A = math.sqrt(2.0 / math.pi)
+GELU_B = 0.044715 * GELU_A
+IMAGES = 2
+VMEM_BYTES = 60 * 2**20
 
 
 def as_sent(shard):
@@ -228,6 +237,1075 @@
     )
 
 
+def norm_parts(values):
+    center = values - jnp.mean(values, -1, keepdims=True)
+    inv_std = lax.rsqrt(jnp.mean(center * center, -1, keepdims=True) + EPSILON)
+    return center * inv_std, inv_std
+
+
+def norm_input_grad(grad, normed, inv_std):
+    return inv_std * (
+        grad
+        - jnp.mean(grad, -1, keepdims=True)
+        - normed * jnp.mean(grad * normed, -1, keepdims=True)
+    )
+
+
+def gelu_pair(value):
+    square = value * value
+    gate = 0.5 + 0.5 * jnp.tanh(value * (GELU_A + GELU_B * square))
+    result = value * gate
+    slope = gate + result * (1.0 - gate) * (2.0 * GELU_A + 6.0 * GELU_B * square)
+    return result.astype(jnp.bfloat16), slope.astype(jnp.bfloat16)
+
+
+def dot(left, right, left_dim, right_dim):
+    return lax.dot_general(
+        left, right, (((left_dim,), (right_dim,)), ((), ())), preferred_element_type=jnp.float32
+    )
+
+
+def chunks(size, count):
+    return [slice(k * size // count, (k + 1) * size // count) for k in range(count)]
+
+
+def position(copy):
+    odd = copy & 1
+    return 2 * odd + (odd ^ (copy >> 1))
+
+
+def clear(first, *refs):
+    @pl.when(first)
+    def _():
+        for ref in refs:
+            ref[...] = jnp.zeros_like(ref)
+
+
+def unpack_small(place, own, other, *refs):
+    vectors = refs[-1]
+    z, c = place[0], place[1]
+    lines, rows, _ = own.shape
+    layers, extra, wide = vectors.shape[1:]
+    keys = rows // layers
+    for layer in range(layers):
+        w_in, w_in_t, w_out, w_out_t, *rest = refs[10 * layer : 10 * layer + 10]
+        base = layer * keys
+        for source, side in ((own, c), (other, 1 - c)):
+            for i in range(lines):
+                shard = 2 * (i ^ z) + side
+                start = pl.multiple_of(shard * keys, keys)
+                w_in[pl.ds(start, keys)] = source[i, base : base + keys, :wide]
+                w_out[pl.ds(start, keys)] = source[i, base : base + keys, wide : 2 * wide]
+                vectors[shard, layer] = source[i, base : base + extra, 2 * wide :]
+        w_in_t[...] = w_in[...].T
+        w_out_t[...] = w_out[...].T
+        held = [vectors[shard, layer].astype(jnp.float32) for shard in range(vectors.shape[0])]
+        for row, target in enumerate(rest[:5]):
+            size = target.shape[1] // len(held)
+            target[...] = jnp.concatenate([part[row : row + 1, :size] for part in held], axis=1)
+        biases = rest[5]
+        size = biases.shape[1] // len(held)
+        for shard, part in enumerate(held):
+            whole = jnp.concatenate([part[5:6], part[6:7]], axis=1)
+            biases[:, shard * size : (shard + 1) * size] = whole[:, :size]
+
+
+def token_branch(values, scale, small, b_out, u_out, hidden_out, slope_out):
+    gain1, shift1, w_in, w_out, gain2, shift2 = small
+    rows, wide = values.shape[0], w_in.shape[1]
+    normed, _ = norm_parts(values)
+    u_out[:rows] = (normed * gain1[...] + shift1[...]).astype(jnp.bfloat16)
+    below = lax.broadcasted_iota(jnp.int32, (wide - rows, values.shape[1]), 0)
+    u_out[rows:] = jnp.where(below == 0, 1.0, 0.0).astype(jnp.bfloat16)
+    hidden, slope = gelu_pair(dot(w_in[...], u_out[...], 1, 0))
+    hidden_out[...] = hidden
+    slope_out[...] = slope
+    middle = values + scale * (dot(w_out[:rows], hidden, 1, 0) + b_out[0, :rows])
+    normed, _ = norm_parts(middle)
+    return middle, (normed * gain2[...] + shift2[...]).astype(jnp.bfloat16)
+
+
+def token_forward(place, scale, x, b_out, *rest, layer):
+    small, (u_out, hidden_out, slope_out, middle_out, v_out) = rest[:6], rest[6:]
+    count, rows = x.shape[:2]
+    for k in range(count):
+        part = scale[count * pl.program_id(0) + k, 2 * layer]
+        middle, v = token_branch(
+            x[k].astype(jnp.float32), part, small, b_out, u_out.at[k], hidden_out.at[k], slope_out.at[k]
+        )
+        middle_out[k] = middle
+        v_out[k * rows : (k + 1) * rows] = v
+
+
+def token_grads(scale, grad, back_v, middle, x, u, hidden, slope, w_in, w_out, gain1, gain2, padded):
+    rows, width = grad.shape
+    normed, inv_std = norm_parts(middle)
+    moved = back_v * normed
+    sums = [jnp.sum(moved, 0, keepdims=True), jnp.sum(back_v, 0, keepdims=True)]
+    grad_mid = grad + norm_input_grad(back_v * gain2[...], normed, inv_std)
+    padded[:rows] = (scale * grad_mid).astype(jnp.bfloat16)
+    low = padded[...]
+    b_out = dot(jnp.ones((8, width), jnp.bfloat16), low, 1, 1)[:1]
+    w_out_grad = dot(hidden, low, 1, 1)
+    pre = (dot(w_out[...], low, 1, 0) * slope.astype(jnp.float32)).astype(jnp.bfloat16)
+    w_in_grad = dot(pre, u, 1, 1)
+    back = dot(w_in[:rows], pre, 1, 0)
+    normed, inv_std = norm_parts(x)
+    sums = [jnp.sum(back * normed, 0, keepdims=True), jnp.sum(back, 0, keepdims=True)] + sums
+    return grad_mid + norm_input_grad(back * gain1[...], normed, inv_std), sums, b_out, w_in_grad, w_out_grad
+
+
+def token_blocks(place, w_in_grad, w_out_grad, whole, put):
+    z, c = place[0], place[1]
+    keys = whole.shape[1] // 8
+    for which, total in ((0, w_in_grad), (1, w_out_grad)):
+        whole[which] = total[...].astype(jnp.bfloat16)
+        for i in range(4):
+            for side, core in ((0, c), (1, 1 - c)):
+                start = pl.multiple_of((2 * (i ^ z) + core) * keys, keys)
+                put(which, i, side, whole[which, pl.ds(start, keys)])
+
+
+def token_backward(place, scale, grad, back_v, middle, x, u, hidden, slope, w_in, w_out, gain1, gain2, *rest):
+    image = pl.program_id(0)
+    g_cout, g_cin = rest[:2]
+    last = len(rest) == 2 + 6 + 4
+    if last:
+        grad_out, mine_out, other_out, vector, low_out, above_grad = rest[2:8]
+        layer = 1
+    else:
+        earlier, grad_out, mine_out, other_out, vector = rest[2:5], *rest[7:11]
+        layer = 0
+    padded, w_in_grad, w_out_grad, whole = rest[-4:]
+    count, rows = x.shape[:2]
+    first = image == 0
+    clear(first, padded, vector, w_in_grad, w_out_grad)
+
+    @pl.when(first)
+    def _():
+        vector[4:5] = g_cout[...]
+        for j in range(g_cin.shape[0]):
+            vector[8 + j : 9 + j] = g_cin[j]
+        if not last:
+            vector[16:] = earlier[2][...]
+
+    if last:
+        clear(first, above_grad)
+    found = []
+    for k in range(count):
+        part = slice(k * rows, (k + 1) * rows)
+        result, *sums = token_grads(
+            scale[count * image + k, 2 * layer], grad[k].astype(jnp.float32), back_v[part], middle[k],
+            x[k].astype(jnp.float32), u[k], hidden[k], slope[k], w_in, w_out, gain1, gain2, padded.at[k],
+        )
+        grad_out[k] = result
+        if last:
+            out = scale[count * image + k, 1] * result
+            above_grad[...] += jnp.sum(out, 0, keepdims=True)
+            low_out[part] = out.astype(jnp.bfloat16)
+        found.append(sums)
+    for k in range(4):
+        vector[k : k + 1] += sum(sums[0][k] for sums in found)
+    vector[5:6, : padded.shape[1]] += sum(sums[1] for sums in found)
+    w_in_grad[...] += sum(sums[2] for sums in found)
+    w_out_grad[...] += sum(sums[3] for sums in found)
+
+    @pl.when(image == pl.num_programs(0) - 1)
+    def _():
+        targets = (mine_out, other_out)
+        if last:
+
+            def put(which, i, side, part):
+                targets[side][which, i] = part
+
+        else:
+
+            def put(which, i, side, part):
+                place_tokens(targets[side], position(which ^ place[2]), i, part)
+
+            for side in range(2):
+                for which in range(2):
+                    for i in range(4):
+                        part = earlier[side][which, i]
+                        place_tokens(targets[side], position((2 + which) ^ place[2]), i, part)
+        token_blocks(place, w_in_grad, w_out_grad, whole, put)
+
+
+def place_tokens(target, j, i, part):
+    rows, wide = target.shape[2], part.shape[1]
+    for k in range(part.shape[0] // rows):
+        target[j, i, :, k * wide : (k + 1) * wide] = part[k * rows : (k + 1) * rows]
+
+
+def out_weight_grad(place, low, hidden, mine_out, other_out, turned, whole):
+    @pl.when(pl.program_id(0) == 0)
+    def _():
+        turned[...] = low[...].T
+
+    out_blocks(place, turned, hidden[0], mine_out, other_out, whole)
+
+
+class Weight:
+    def __init__(self, refs, which):
+        self.which = which
+        self.shards, self.parts = (refs[which], refs[2 + which]), (refs[4 : 4 + 4], refs[8:12])
+
+    def blocks(self, copy, i):
+        for side, (line, from_x, from_y, corner) in enumerate(self.parts):
+            yield side, (line, from_x, from_y, corner)[copy].at[i - 1, self.which], 0
+
+
+def fetch_in(place, layer, weight, target, sem):
+    z, c, q = place[0], place[1], place[2]
+    copies, _, columns = target.shape
+    rows = weight.shards[0].shape[1]
+    for copy in range(copies):
+        j = copy ^ q
+
+        def put(ref, i, side, first):
+            start = pl.multiple_of((2 * (i ^ z) + (c ^ side)) * rows + first, 16)
+            goal = target.at[j, pl.ds(start, ref.shape[0])]
+            pltpu.make_async_copy(ref, goal, sem.at[j]).start()
+
+        for side, shard in enumerate(weight.shards):
+            put(shard.at[layer, :, pl.ds(pl.multiple_of(j * columns, columns), columns)], 0, side, 0)
+        for i in range(1, copies):
+            for side, ref, first in weight.blocks(copy, i):
+                put(ref, i, side, first)
+
+
+def fetch_out(place, layer, weight, target, sem):
+    z, c, q = place[0], place[1], place[2]
+    lines, part, _ = target.shape
+    for i in range(lines):
+
+        def put(ref, start):
+            goal = target.at[i ^ z, pl.ds(pl.multiple_of(start, 16), ref.shape[0])]
+            pltpu.make_async_copy(ref, goal, sem.at[i ^ z]).start()
+
+        if i == 0:
+            for side, shard in enumerate(weight.shards):
+                put(shard.at[layer], (c ^ side) * (part // 2))
+            continue
+        for copy in range(4):
+            for side, ref, first in weight.blocks(copy, i):
+                put(ref, (c ^ side) * (part // 2) + (copy ^ q) * (part // 8) + first)
+
+
+def arrive(weight, sem, step):
+    pltpu.make_async_copy(weight.at[step], weight.at[step], sem.at[step]).wait()
+
+
+def out_blocks(place, turned, hidden, mine_out, other_out, whole):
+    c, q = place[1], place[2]
+    whole[...] = dot(turned[...], hidden, 1, 0).astype(jnp.bfloat16)
+    copies, _, rows, columns = mine_out.shape
+    size = columns // 2
+    for side, target in ((c, mine_out), (1 - c, other_out)):
+        units = pl.ds(pl.multiple_of(side * size, 128), size)
+        for j in range(copies):
+            start = 2 * j * rows
+            target[position(j ^ q), 0, :, :size] = whole[start : start + rows, units]
+            target[position(j ^ q), 0, :, size:] = whole[start + rows : start + 2 * rows, units]
+
+
+def first_forward(place, scale, v, middle, bias_in, bias_out, *rest):
+    weight_in, weight_out = Weight(rest[:12], 0), Weight(rest[:12], 1)
+    hidden_out, slope_out, x_out, w_in, w_out, hidden, total, sem_in, sem_out = rest[12:]
+    step = pl.program_id(0)
+    rows = middle.shape[1]
+
+    @pl.when(step == 0)
+    def _():
+        fetch_in(place, 0, weight_in, w_in, sem_in)
+        fetch_out(place, 0, weight_out, w_out, sem_out)
+        total[...] = jnp.zeros_like(total)
+
+    @pl.when(step < 4)
+    def _():
+        j = (step & 3) ^ place[2]
+        arrive(w_in, sem_in, j)
+        for part in chunks(v.shape[0], 2):
+            value, slope = gelu_pair(dot(v[part], w_in[j], 1, 0) + bias_in[...])
+            hidden_out[0, part] = value
+            hidden[j, part] = value
+            slope_out[0, part] = slope
+
+    @pl.when(step >= 4)
+    def _():
+        j = (step & 3) ^ place[0]
+        arrive(w_out, sem_out, j)
+        total[...] += dot(hidden[j], w_out[j], 1, 0)
+
+    @pl.when(step == 7)
+    def _():
+        for image in range(middle.shape[0]):
+            branch = total[image * rows : (image + 1) * rows] + bias_out[...]
+            x_out[image] = middle[image] + scale[image, 1] * branch
+
+
+def last_hidden(place, scale, v, bias, grad, *rest):
+    weight = Weight(rest[:12], 0)
+    (
+        hidden_out, slope_out, mine_out, other_out, low_out, bias_grad, w_in, hidden, turned, whole, sem,
+    ) = rest[12:]
+    step = pl.program_id(0)
+
+    @pl.when(step == 0)
+    def _():
+        fetch_in(place, 1, weight, w_in, sem)
+        rows = grad.shape[1]
+        sums = 0.0
+        for image in range(grad.shape[0]):
+            out = scale[image, 3] * grad[image].astype(jnp.float32)
+            sums = sums + jnp.sum(out, 0, keepdims=True)
+            low_out[image * rows : (image + 1) * rows] = out.astype(jnp.bfloat16)
+        bias_grad[...] = sums
+        turned[...] = low_out[...].T
+
+    @pl.when(step < 4)
+    def _():
+        j = (step & 3) ^ place[2]
+        arrive(w_in, sem, j)
+        for part in chunks(v.shape[0], 2):
+            value, slope = gelu_pair(dot(v[part], w_in[j], 1, 0) + bias[...])
+            hidden_out[0, part] = value
+            hidden[j, part] = value
+            slope_out[0, part] = slope
+
+    @pl.when(step >= 4)
+    def _():
+        out_blocks(place, turned, hidden[(step & 3) ^ place[0]], mine_out, other_out, whole)
+
+
+def out_forward(place, scale, hidden, middle, bias, *rest, layer):
+    x_out, weight, total, sem = rest[12:]
+    step = pl.program_id(0)
+
+    @pl.when(step == 0)
+    def _():
+        fetch_out(place, layer, Weight(rest[:12], 1), weight, sem)
+        total[...] = jnp.zeros_like(total)
+
+    j = step ^ place[0]
+    arrive(weight, sem, j)
+    total[...] += dot(hidden[0], weight[j], 1, 0)
+
+    @pl.when(step == pl.num_programs(0) - 1)
+    def _():
+        for image in range(middle.shape[0]):
+            rows = middle.shape[1]
+            branch = total[image * rows : (image + 1) * rows] + bias[...]
+            x_out[image] = (middle[image] + scale[image, 2 * layer + 1] * branch).astype(x_out.dtype)
+
+
+def channel_backward(place, low, v, slope, *rest, layer):
+    mine, theirs, back_out, bias_grad, w_out, w_in, turned, pre, whole, sem_out, sem_in = rest[12:]
+    z, c = place[0], place[1]
+    step = pl.program_id(0)
+
+    @pl.when(step == 0)
+    def _():
+        fetch_out(place, layer, Weight(rest[:12], 1), w_out, sem_out)
+        fetch_in(place, layer, Weight(rest[:12], 0), w_in, sem_in)
+        turned[...] = v[...].T
+        back_out[...] = jnp.zeros_like(back_out)
+
+    j = step ^ z
+    arrive(w_out, sem_out, j)
+    arrive(w_in, sem_in, j)
+    sums = 0.0
+    for part in chunks(low.shape[0], 2):
+        grad = dot(low[part], w_out[j], 1, 1) * slope[0, part].astype(jnp.float32)
+        sums = sums + jnp.sum(grad, 0, keepdims=True)
+        pre[part] = grad.astype(jnp.bfloat16)
+    bias_grad[0] = sums
+    for part in chunks(turned.shape[0], 3):
+        whole[part] = dot(turned[part], pre[...], 1, 0).astype(jnp.bfloat16)
+    lines = mine.shape[1]
+    rows = whole.shape[0] // (2 * lines)
+    for i in range(lines):
+        for side, target in ((c, mine), (1 - c, theirs)):
+            start = pl.multiple_of((2 * (i ^ z) + side) * rows, rows)
+            target[0, i] = whole[pl.ds(start, rows)]
+    back_out[...] += dot(pre[...], w_in[j], 1, 1)
+
+
+def finish_out(place, *refs):
+    parts, out, whole = refs[:4], refs[-2], refs[-1]
+    for j in range(4):
+        rows, columns = parts[j].shape[1:]
+        for half in range(2):
+            start = pl.multiple_of((2 * (j ^ place[2]) + half) * rows, rows)
+            part = parts[j][0, :, half * columns // 2 : (half + 1) * columns // 2]
+            whole[pl.ds(start, rows)] = part.astype(jnp.float32)
+    out[0] = whole[...].T
+
+
+def finish_in(place, *refs, tokens):
+    parts, out = refs[:4], refs[-2] if tokens else refs[-1]
+    rows = out.shape[1]
+    for j in range(4):
+        columns = parts[j].shape[2]
+        start = pl.multiple_of((j ^ place[2]) * columns, columns)
+        out[0, :, pl.ds(start, columns)] = parts[j][0, :rows].astype(jnp.float32)
+        if tokens:
+            wide = refs[-1].shape[2]
+            for k in range(columns // wide):
+                part = parts[j][0, rows:, k * wide : (k + 1) * wide]
+                refs[-1][j ^ place[2], 16 * k : 16 * k + 16] = part.astype(jnp.float32)
+
+
+class Kernels:
+    def __init__(self, place, slots, rows, width, inner, hidden, lines, block):
+        self.place = place
+        self.slots, self.rows, self.width = slots, rows, width
+        self.inner, self.hidden = inner, hidden
+        self.lines, self.block = lines, block
+        self.part = hidden // 4
+        self.wide = 256
+
+    def run(self, body, steps, inputs, outputs, scratch, flops, aliases=None, **fixed):
+        sizes = sum(a.size * a.dtype.itemsize for a, _, _ in inputs)
+        sizes += sum(math.prod(o[0]) * jnp.dtype(o[1]).itemsize for o in outputs)
+
+        def spec(block, index):
+            if isinstance(block, tuple):
+                return pl.BlockSpec(block, index)
+            return pl.BlockSpec(memory_space=block)
+
+        return pl.pallas_call(
+            functools.partial(body, **fixed) if fixed else body,
+            name=body.__name__,
+            grid_spec=pltpu.PrefetchScalarGridSpec(
+                num_scalar_prefetch=1,
+                grid=(steps,),
+                in_specs=[spec(block, index) for _, block, index in inputs],
+                out_specs=[spec(o[2], o[3]) for o in outputs],
+                scratch_shapes=scratch,
+            ),
+            out_shape=[jax.ShapeDtypeStruct(o[0], o[1]) for o in outputs],
+            input_output_aliases=aliases or {},
+            compiler_params=pltpu.CompilerParams(
+                dimension_semantics=("arbitrary",), vmem_limit_bytes=VMEM_BYTES
+            ),
+            cost_estimate=pl.CostEstimate(flops=flops, bytes_accessed=sizes, transcendentals=0),
+        )(self.place, *[a for a, _, _ in inputs])
+
+    def image(self, array):
+        return (array, (1,) + array.shape[1:], lambda i, s: (i, 0, 0))
+
+    def fixed(self, array):
+        zeros = (0,) * array.ndim
+        return (array, array.shape, lambda i, s: zeros)
+
+    def scalars(self, array):
+        return (array, pltpu.SMEM, None)
+
+    def in_hbm(self, arrays):
+        return [(a, pltpu.HBM, None) for a in arrays]
+
+    def fixed_out(self, shape, dtype):
+        zeros = (0,) * len(shape)
+        return (shape, dtype, shape, lambda i, s: zeros)
+
+    def columns(self, array, count):
+        return (array, (array.shape[0], array.shape[1] // count), lambda i, s: (0, i))
+
+    def columns_out(self, rows, columns, count, dtype):
+        return ((rows, columns), dtype, (rows, columns // count), lambda i, s: (0, i))
+
+    def late(self, step, start):
+        return jnp.clip(step - start, 0, 3)
+
+    def images_out(self, rows, dtype):
+        block = (IMAGES, rows, self.width)
+        return ((self.slots, rows, self.width), dtype, block, lambda i, s: (i, 0, 0))
+
+    def images(self, array):
+        return (array, (IMAGES,) + array.shape[1:], lambda i, s: (i, 0, 0))
+
+    def rows_out(self):
+        shape = (self.slots * self.rows, self.width)
+        return (shape, jnp.bfloat16, (IMAGES * self.rows, self.width), lambda i, s: (i, 0))
+
+    def quarters(self, array, which, start=0):
+        return (array, (1,) + array.shape[1:], lambda i, s: (self.late(i, start) ^ s[which], 0, 0))
+
+    def quarters_out(self, which, start=0):
+        rows = self.slots * self.rows
+        block = (1, rows, self.part)
+        return ((4,) + block[1:], jnp.bfloat16, block, lambda i, s: (self.late(i, start) ^ s[which], 0, 0))
+
+    def row(self, array, which, start=0):
+        return (array, (1, self.part), lambda i, s: (0, self.late(i, start) ^ s[which]))
+
+    def out_blocks_out(self, start=0):
+        block = (4, 1, self.block, self.width)
+        shape = (4, self.lines) + block[2:]
+        return (shape, jnp.bfloat16, block, lambda i, s: (0, self.late(i, start), 0, 0))
+
+    def product(self):
+        return 2 * self.slots * self.rows * self.width * self.hidden
+
+    def unpack_small(self, own, other, layers, shards, extra):
+        bf16, f32 = jnp.bfloat16, jnp.float32
+        inner, wide, width = self.inner, self.wide, self.width
+        outputs = [((inner, wide), bf16), ((wide, inner), bf16)] * 2
+        outputs += [((1, width), f32)] * 5 + [((1, self.hidden), f32)]
+        found = self.run(
+            unpack_small,
+            1,
+            [self.fixed(own), self.fixed(other)],
+            [self.fixed_out(*part) for part in outputs * layers],
+            [pltpu.VMEM((shards, layers, extra, wide), bf16)],
+            0,
+        )
+        return [list(found[10 * layer : 10 * layer + 10]) for layer in range(layers)]
+
+    def token_product(self):
+        return 2 * self.slots * self.wide * self.width * self.inner
+
+    def b_out(self, array, layer):
+        return (array, (1,) + array.shape[1:], lambda i, s: (layer, 0, 0))
+
+    def token_outs(self):
+        bf16 = jnp.bfloat16
+        outs = [self.images_out(rows, bf16) for rows in (self.wide, self.inner, self.inner)]
+        return outs + [self.images_out(self.rows, jnp.float32), self.rows_out()]
+
+    def token_forward(self, scale, x, b_out, small, layer):
+        return self.run(
+            token_forward,
+            self.slots // IMAGES,
+            [self.scalars(scale), self.images(x), self.b_out(b_out, layer)] + [self.fixed(a) for a in small],
+            self.token_outs(),
+            [],
+            2 * self.token_product(),
+            layer=layer,
+        )
+
+    def first_forward(self, scale, v, middle, bias_in, bias_out, weights):
+        bf16, f32 = jnp.bfloat16, jnp.float32
+        rows = self.slots * self.rows
+        return self.run(
+            first_forward,
+            8,
+            [self.scalars(scale), self.fixed(v), self.fixed(middle), self.row(bias_in, 2), self.fixed(bias_out)]
+            + self.in_hbm(weights),
+            [self.quarters_out(2)] * 2 + [self.fixed_out((self.slots, self.rows, self.width), f32)],
+            [
+                self.weight(),
+                self.weight(),
+                pltpu.VMEM((4, rows, self.part), bf16),
+                pltpu.VMEM((rows, self.width), f32),
+                pltpu.SemaphoreType.DMA((4,)),
+                pltpu.SemaphoreType.DMA((4,)),
+            ],
+            2 * self.product(),
+        )
+
+    def last_hidden(self, scale, v, bias, grad, weights):
+        bf16, f32 = jnp.bfloat16, jnp.float32
+        rows = self.slots * self.rows
+        return self.run(
+            last_hidden,
+            8,
+            [self.scalars(scale), self.fixed(v), self.row(bias, 2), self.fixed(grad)] + self.in_hbm(weights),
+            [self.quarters_out(2)] * 2
+            + [self.out_blocks_out(4)] * 2
+            + [self.fixed_out((rows, self.width), bf16), self.fixed_out((1, self.width), f32)],
+            [
+                self.weight(),
+                pltpu.VMEM((4, rows, self.part), bf16),
+                pltpu.VMEM((self.width, rows), bf16),
+                pltpu.VMEM((self.width, self.part), bf16),
+                pltpu.SemaphoreType.DMA((4,)),
+            ],
+            2 * self.product(),
+        )
+
+    def token_backward(self, scale, grad, back, kept, small, g_cout, g_cin, keys, earlier=(), blocks=()):
+        bf16, f32 = jnp.bfloat16, jnp.float32
+        rows, width = self.slots * self.rows, self.width
+        middle, x, u, hidden, slope = kept
+        inputs = [self.scalars(scale), self.images(grad)]
+        inputs += [(back, (IMAGES * self.rows, width), lambda i, s: (i, 0))]
+        inputs += [self.images(a) for a in (middle, x, u, hidden, slope)]
+        inputs += [self.fixed(a) for a in tuple(small) + (g_cout, g_cin) + tuple(earlier)]
+        outputs = [self.images_out(self.rows, f32)]
+        aliases = None
+        if earlier:
+            aliases = {1 + len(inputs): 1, 2 + len(inputs): 2}
+            inputs += self.in_hbm(blocks)
+            extra = blocks[0].shape[2] - self.block
+            block = (4, self.lines, extra, width)
+            outputs += [(blocks[0].shape, bf16, block, lambda i, s: (0, 0, self.block // extra, 0))] * 2
+            outputs += [self.fixed_out((32, width), f32)]
+        else:
+            outputs += [self.fixed_out((2, self.lines, keys, self.wide), bf16)] * 2
+            outputs += [self.fixed_out((16, width), f32), self.rows_out(), self.fixed_out((1, width), f32)]
+        return self.run(
+            token_backward,
+            self.slots // IMAGES,
+            inputs,
+            outputs,
+            [
+                pltpu.VMEM((IMAGES, self.wide, width), bf16),
+                pltpu.VMEM((self.inner, self.wide), f32),
+                pltpu.VMEM((self.inner, self.wide), f32),
+                pltpu.VMEM((2, self.inner, self.wide), bf16),
+            ],
+            4 * self.token_product(),
+            aliases,
+        )
+
+    def out_weight_grad(self, low, hidden):
+        rows = self.slots * self.rows
+        return self.run(
+            out_weight_grad,
+            4,
+            [self.fixed(low), self.quarters(hidden, 0)],
+            [self.out_blocks_out()] * 2,
+            [pltpu.VMEM((self.width, rows), jnp.bfloat16), pltpu.VMEM((self.width, self.part), jnp.bfloat16)],
+            self.product(),
+        )
+
+    def weight(self):
+        return pltpu.VMEM((4, self.width, self.part), jnp.bfloat16)
+
+    def out_forward(self, scale, hidden, middle, bias, weights, layer, dtype):
+        return self.run(
+            out_forward,
+            4,
+            [self.scalars(scale), self.quarters(hidden, 0), self.fixed(middle), self.fixed(bias)]
+            + self.in_hbm(weights),
+            [self.fixed_out(middle.shape, dtype)],
+            [
+                self.weight(),
+                pltpu.VMEM((self.slots * self.rows, self.width), jnp.float32),
+                pltpu.SemaphoreType.DMA((4,)),
+            ],
+            self.product(),
+            layer=layer,
+        )[0]
+
+    def channel_backward(self, low, v, slope, weights, layer, extra=0):
+        bf16, f32 = jnp.bfloat16, jnp.float32
+        rows = self.slots * self.rows
+        block = (1, self.lines, self.block, self.width)
+        shape = (4, self.lines, self.block + extra, self.width)
+        blocks = (shape, bf16, block, lambda j, s: (position(j ^ s[0] ^ s[2]), 0, 0, 0))
+        return self.run(
+            channel_backward,
+            4,
+            [self.fixed(low), self.fixed(v), self.quarters(slope, 0)]
+            + self.in_hbm(weights),
+            [
+                blocks,
+                blocks,
+                self.fixed_out((rows, self.width), f32),
+                ((4, 1, self.part), f32, (1, 1, self.part), lambda i, s: (i ^ s[0], 0, 0)),
+            ],
+            [
+                self.weight(),
+                self.weight(),
+                pltpu.VMEM((self.width, rows), bf16),
+                pltpu.VMEM((rows, self.part), bf16),
+                pltpu.VMEM((self.width, self.part), bf16),
+                pltpu.SemaphoreType.DMA((4,)),
+                pltpu.SemaphoreType.DMA((4,)),
+            ],
+            3 * self.product(),
+            layer=layer,
+        )
+
+    def parts(self, parts):
+        def one(array, index):
+            return (array, (1,) + array.shape[1:], lambda i, s: (index, 0, 0))
+
+        return [one(*part) for part in parts]
+
+    def finish_out(self, parts, layer, layers, earlier=()):
+        shape = (layers, self.part // 2, self.width)
+        return self.run(
+            finish_out,
+            1,
+            self.parts(parts) + self.in_hbm(earlier),
+            [(shape, jnp.float32, (1,) + shape[1:], lambda i, s: (layer, 0, 0))],
+            [pltpu.VMEM((self.width, self.part // 2), jnp.float32)],
+            0,
+            {1 + len(parts): 0} if earlier else None,
+        )
+
+    def finish_in(self, parts, layer, layers, keys=0, earlier=()):
+        shape = (layers, self.block, self.hidden)
+        outputs = [(shape, jnp.float32, (1,) + shape[1:], lambda i, s: (layer, 0, 0))]
+        if keys:
+            outputs.append(self.fixed_out((4, keys, self.wide), jnp.float32))
+        return self.run(
+            finish_in,
+            1,
+            self.parts(parts) + self.in_hbm(earlier),
+            outputs,
+            [],
+            0,
+            {1 + len(parts): 0} if earlier else None,
+            tokens=bool(keys),
+        )
+
+
+class Moves:
+    def __init__(self):
+        self.lines = lax.axis_size("fsdp") // 2
+        self.copies = lax.axis_size("dp")
+        me = lax.axis_index("fsdp")
+        self.z, self.c, self.q = me // 2, me % 2, lax.axis_index("dp")
+
+    def along(self, values, bits):
+        return lax.ppermute(values, "fsdp", [(f, f ^ (2 * bits)) for f in range(2 * self.lines)])
+
+    def core(self, values):
+        return lax.ppermute(values, "fsdp", [(f, f ^ 1) for f in range(2 * self.lines)])
+
+    def across(self, values, bits):
+        return lax.ppermute(values, "dp", [(q, q ^ bits) for q in range(self.copies)])
+
+
+class Held:
+    def __init__(self, moves):
+        self.moves, self.fresh = moves, []
+        self.half = moves.lines // 2
+
+    def bring(self, **arrays):
+        for name, array in arrays.items():
+            setattr(self, name, array)
+            self.fresh.append(name)
+
+
+def settle(held, *values):
+    names = [(part, name) for part in held for name in part.fresh]
+    arrays = tuple(getattr(part, name) for part, name in names)
+    arrays = lax.optimization_barrier(tuple(values) + arrays)
+    for (part, name), array in zip(names, arrays[len(values) :]):
+        setattr(part, name, array)
+    for part in held:
+        part.fresh = []
+    return arrays[: len(values)]
+
+
+class Gather(Held):
+    def __init__(self, moves, part):
+        super().__init__(moves)
+        self.part = part
+
+    def direct(self):
+        self.bring(**{"z%d" % i: self.moves.along(self.part, i) for i in range(1, self.moves.lines)})
+
+    def join(self):
+        self.line = jnp.stack([getattr(self, "z%d" % i) for i in range(1, self.moves.lines)])
+
+    def first(self):
+        self.bring(x=self.moves.across(self.line, 1), y=self.moves.across(self.line, 2))
+
+    def second(self):
+        self.bring(low=self.moves.across(self.y[:, :1], 1), high=self.moves.across(self.x[:, 1:], 2))
+
+    def corner_core(self):
+        self.corner = jnp.concatenate([self.low, self.high], 1)
+        self.core("corner")
+
+    def core(self, *names):
+        self.bring(**{name + "_core": self.moves.core(getattr(self, name)) for name in names})
+
+    def whole(self):
+        names = ("line", "x", "y", "corner")
+        return [getattr(self, name) for name in names] + [getattr(self, name + "_core") for name in names]
+
+
+class Sum(Held):
+    def __init__(self, moves, mine, other):
+        super().__init__(moves)
+        self.mine, self.theirs = mine, other
+        self.low, self.high = slice(0, self.half), slice(self.half, None)
+
+    def both(self, copies, part):
+        return self.mine[copies, part] + self.got[copies, part]
+
+    def core(self):
+        self.bring(got=self.moves.core(self.theirs))
+
+    def first(self):
+        self.bring(
+            from_x=self.moves.across(self.both(slice(2, 4), self.low), 1),
+            from_y=self.moves.across(self.both(slice(1, 3), self.high), 2),
+        )
+
+    def second(self):
+        self.bring(
+            low2=self.moves.across(self.both(1, self.low) + self.from_x[0], 2),
+            high1=self.moves.across(self.both(3, self.high) + self.from_y[1], 1),
+        )
+
+    def halves(self):
+        low = self.both(0, self.low) + self.from_x[1] + self.low2
+        high = self.both(0, self.high) + self.from_y[0] + self.high1
+        return low, high
+
+    def once(self):
+        low, high = self.halves()
+        self.block = low[0]
+        blocks = [low[i] for i in range(1, self.half)] + [high[i] for i in range(self.half)]
+        self.bring(**{"z%d" % (i + 1): self.moves.along(block, i + 1) for i, block in enumerate(blocks)})
+
+    def far(self):
+        self.block, high = self.halves()
+        self.bring(z=self.moves.along(high, 2))
+
+    def near(self):
+        pair = self.block + self.z
+        self.block = pair[0]
+        self.bring(z1=self.moves.along(pair[1], 1))
+
+    def total(self):
+        total = self.block.astype(jnp.float32)
+        for i in range(1, self.moves.lines):
+            if hasattr(self, "z%d" % i):
+                total = total + getattr(self, "z%d" % i).astype(jnp.float32)
+        return total.astype(jnp.bfloat16)
+
+
+class Share(Held):
+    def __init__(self, moves, part, axis):
+        super().__init__(moves)
+        self.part, self.axis = part, axis
+
+    def first(self):
+        self.bring(near=self.moves.across(self.part, self.axis))
+
+    def second(self):
+        self.bring(far=self.moves.across(jnp.stack([self.part, self.near]), 3 - self.axis))
+
+    def parts(self):
+        near, far = (self.near[None], 0), (self.far, 0)
+        return [(self.part[None], 0)] + ([near, far] if self.axis == 1 else [far, near]) + [(self.far, 1)]
+
+
+class SumAll(Held):
+    def __init__(self, moves, value):
+        super().__init__(moves)
+        self.value = value
+        self.steps = [(axis, 2**k) for axis in ("fsdp", "dp") for k in range((lax.axis_size(axis) - 1).bit_length())]
+
+    def step(self):
+        axis, bit = self.steps.pop(0)
+        count = lax.axis_size(axis)
+        got = lax.ppermute(self.value, axis, [(i, i ^ bit) for i in range(count)])
+        self.bring(value=self.value + got)
+
+
+def blocked_shards(
+    tokens, image_counts, skip_mask, norm1_gain, norm1_bias, token_in, token_in_bias, token_out,
+    token_out_bias, norm2_gain, norm2_bias, channel_in, channel_in_bias, channel_out,
+    channel_out_bias, cotangent,
+):
+    f32, bf16 = jnp.float32, jnp.bfloat16
+    slots, patches, width = tokens.shape
+    layers, in_rows, hidden = channel_in.shape
+    keys = token_out.shape[1]
+    moves = Moves()
+    shards_count = 2 * moves.lines
+    inner = keys * shards_count
+    rows = -(-patches // 16) * 16
+    place = jnp.stack([moves.z, moves.c, moves.q]).astype(jnp.int32)
+    kernels = Kernels(place, slots, rows, width, inner, hidden, moves.lines, in_rows)
+    wide = kernels.wide
+
+    live = (jnp.arange(slots, dtype=jnp.int32) < image_counts[0]).astype(f32)
+    scale = live[:, None, None] * skip_mask.astype(f32)
+
+    def padded(images):
+        return jnp.pad(images, ((0, 0), (0, rows - patches), (0, 0)))
+
+    def quarter(array, axis):
+        size = array.shape[axis] // 4
+        return lax.dynamic_slice_in_dim(array, moves.q * size, size, axis)
+
+    def widen(array):
+        return jnp.pad(array, ((0, 0), (0, 0), (0, wide - array.shape[2])))
+
+    gap = jnp.zeros((layers, keys, rows - patches), bf16)
+    with_bias = jnp.concatenate([jnp.swapaxes(token_in, 1, 2), gap, token_in_bias[:, :, None]], 2)
+    vectors = jnp.stack([norm1_gain, norm1_bias, norm2_gain, norm2_bias, channel_out_bias], 1)
+    biases = jnp.pad(channel_in_bias, ((0, 0), (0, 2 * wide - channel_in_bias.shape[1])))
+    vectors = jnp.concatenate([widen(vectors), biases.reshape(layers, 2, wide)], 1)
+    extra = 16
+    vectors = jnp.pad(vectors, ((0, 0), (0, extra - vectors.shape[1]), (0, 0)))
+    vectors = jnp.pad(vectors, ((0, 0), (0, keys - extra), (0, 0)))
+    packs = jnp.concatenate([widen(with_bias), widen(token_out), vectors], 2).reshape(layers * keys, width)
+    b_outs = jnp.pad(token_out_bias.astype(f32), ((0, 0), (0, wide - patches)))[:, :, None]
+    scale = scale.reshape(slots, 2 * layers)
+
+    def both(layer):
+        return jnp.stack([quarter(channel_in[layer], 1), quarter(channel_out[layer], 0)])
+
+    first, last = Gather(moves, both(0)), Gather(moves, both(1))
+    small = Gather(moves, packs)
+    shards_held = Held(moves)
+    first.direct()
+    shards_held.bring(ins=moves.core(channel_in), outs=moves.core(channel_out))
+    small.part, last.part = settle((first, shards_held), small.part, last.part)
+    first.join()
+
+    def weights(gather):
+        return [channel_in, channel_out, shards_held.ins, shards_held.outs] + gather.whole()
+
+    first.first()
+    began, first.fresh = first.fresh, []
+    first.core("line")
+    small.direct()
+    (last.part, first.line) = settle((first, small), last.part, first.line)
+    first.fresh = began
+    small.line = jnp.stack([small.part, small.z1, small.z2, small.z3])
+    small.core("line")
+    last.direct()
+    last.fresh = ["z1"]
+    settle((first, small, last))
+    first.second()
+    found = kernels.unpack_small(small.line, small.line_core, layers, shards_count, extra)
+    x0 = padded(tokens)
+    (w_in0, w_in_t0, w_out0, w_out_t0, gain1_0, shift1_0, gain2_0, shift2_0, b_cout0, b_cin0) = found[0]
+    (w_in1, w_in_t1, w_out1, w_out_t1, gain1_1, shift1_1, gain2_1, shift2_1, b_cout1, b_cin1) = found[1]
+
+    u0, h0, d0, mid0, v0 = kernels.token_forward(
+        scale, x0, b_outs, (gain1_0, shift1_0, w_in0, w_out_t0, gain2_0, shift2_0), 0
+    )
+    last.fresh = ["z2"]
+    (v0,) = settle((first, last), v0)
+    first.core("x", "y")
+    first.corner_core()
+    last.fresh = ["z3"]
+    (v0,) = settle((first, last), v0)
+
+    last.join()
+    last.first()
+    hid0, slope0, x1 = kernels.first_forward(scale, v0, mid0, b_cin0, b_cout0, weights(first))
+    (x1,) = settle((last,), x1)
+
+    last.second()
+    last.core("line", "x", "y")
+    u1, h1, d1, mid1, v1 = kernels.token_forward(
+        scale, x1, b_outs, (gain1_1, shift1_1, w_in1, w_out_t1, gain2_1, shift2_1), 1
+    )
+    (v1,) = settle((last,), v1)
+    last.corner_core()
+    grad2 = padded(cotangent)
+    hid1, slope1, mine, theirs, low1, g_cout1 = kernels.last_hidden(scale, v1, b_cin1, grad2, weights(last))
+    mine, theirs, low1 = settle((last,), mine, theirs, low1)
+
+    sum_out1 = Sum(moves, mine, theirs)
+    sum_out1.core()
+    mine, theirs, back, g_cin1 = kernels.channel_backward(low1, v1, slope1, weights(last), 1)
+    mine, theirs, back = settle((sum_out1,), mine, theirs, back)
+
+    sum_in1 = Sum(moves, mine, theirs)
+    sum_in1.core()
+    sum_out1.first()
+    grads1 = kernels.token_backward(
+        scale, grad2, back, (mid1, x1, u1, h1, d1), (w_in_t1, w_out1, gain1_1, gain2_1), g_cout1, g_cin1, keys
+    )
+    grad1, *tokens1, vector1, low0, g_cout0 = settle((sum_out1, sum_in1), *grads1)
+
+    sum_out1.second()
+    sum_in1.first()
+    mine, theirs = kernels.out_weight_grad(low0, hid0)
+    mine, theirs = settle((sum_out1, sum_in1), mine, theirs)
+
+    sum_out0 = Sum(moves, mine, theirs)
+    sum_out0.core()
+    sum_in1.second()
+    sum_out1.far()
+    *blocks, back, g_cin0 = kernels.channel_backward(low0, v0, slope0, weights(first), 0, 16)
+    *blocks, back = settle((sum_out1, sum_in1, sum_out0), *blocks, back)
+
+    sum_out0.first()
+    sum_in1.far()
+    sum_out1.near()
+    grad0, mine, theirs, vector = kernels.token_backward(
+        scale, grad1, back, (mid0, x0, u0, h0, d0), (w_in_t0, w_out0, gain1_0, gain2_0), g_cout0, g_cin0, keys,
+        (*tokens1, vector1), blocks,
+    )
+    hid1, grad0, mine, theirs, vector = settle((sum_out1, sum_in1, sum_out0), hid1, grad0, mine, theirs, vector)
+
+    sum_in0 = Sum(moves, mine, theirs)
+    sum_in0.core()
+    sum_out0.second()
+    sum_in1.near()
+    vector_sum = SumAll(moves, vector)
+    vector_sum.step()
+    output = kernels.out_forward(scale, hid1, mid1, b_cout1, weights(last), 1, bf16)
+    (output,) = settle((sum_in0, sum_out0, sum_in1, vector_sum), output)
+    output = output[:, :patches]
+    input_grad = grad0[:, :patches]
+
+    sum_in0.first()
+    sum_out0.far()
+    vector_sum.step()
+    share_out1 = Share(moves, sum_out1.total(), 1)
+    share_out1.first()
+    settle((sum_in0, sum_out0, share_out1, vector_sum))
+
+    sum_in0.second()
+    sum_out0.near()
+    vector_sum.step()
+    share_in1 = Share(moves, sum_in1.total(), 2)
+    share_in1.first()
+    share_out1.second()
+    settle((sum_in0, sum_out0, share_in1, share_out1, vector_sum))
+
+    sum_in0.once()
+    share_in1.second()
+    share_out0 = Share(moves, sum_out0.total(), 1)
+    share_out0.first()
+    vector_sum.step()
+    settle((sum_in0, share_in1, share_out0, vector_sum))
+
+    total = sum_in0.total()
+    vector_sum.step()
+    share_out0.second()
+    near = [moves.across(total, bits) for bits in (1, 2, 3)]
+    (done_in,) = kernels.finish_in(share_in1.parts(), 1, layers)
+    (done_out,) = kernels.finish_out(share_out1.parts(), 1, layers)
+    done_in, done_out, *near = settle((share_out0, vector_sum), done_in, done_out, *near)
+    (grad_out,) = kernels.finish_out(share_out0.parts(), 0, layers, (done_out,))
+    parts = [(part[None], 0) for part in [total] + near]
+    grad_in, near = kernels.finish_in(parts, 0, layers, keys, (done_in,))
+
+    near = near.reshape(layers, 2, keys, wide)
+    grad_t_in = jnp.swapaxes(near[:, 0, :, :patches], 1, 2)
+    grad_b_in = near[:, 0, :, rows]
+    grad_t_out = near[:, 1, :, :patches]
+    sums = vector_sum.value.reshape(layers, 16, width)
+    me = lax.axis_index("fsdp")
+
+    def owned(row):
+        size = width // shards_count
+        return lax.dynamic_slice_in_dim(sums[:, row], me * size, size, 1)
+
+    grad_gain1, grad_shift1, grad_gain2, grad_shift2, grad_b_cout = [owned(row) for row in range(5)]
+    size = hidden // shards_count
+    grad_b_cin = lax.dynamic_slice(sums, (0, 8 + me // 2, (me % 2) * size), (layers, 1, size))[:, 0]
+    bias_total = sums[:, 5, :patches]
+    return (
+        output, input_grad, grad_gain1, grad_shift1, grad_t_in, grad_b_in, grad_t_out, bias_total,
+        grad_gain2, grad_shift2, grad_in, grad_b_cin, grad_out, grad_b_cout,
+    )
+
+
+def fits(mesh):
+    return mesh.shape["dp"] == 4 and mesh.shape["fsdp"] == 8
+
+
 def solution(mesh):
     in_specs = (
         P(("dp", "fsdp"), None, None),
@@ -263,4 +1341,5 @@
         P(None, "fsdp", None),
         P(None, "fsdp"),
     )
-    return jax.shard_map(shards, mesh=mesh, in_specs=in_specs, out_specs=out_specs, check_vma=False)
+    program = blocked_shards if fits(mesh) else shards
+    return jax.shard_map(program, mesh=mesh, in_specs=in_specs, out_specs=out_specs, check_vma=False)

time: 1050 us -> 402 us (0.38)
  waiting for transfers between devices: 550 us -> 85.3 us
  blocking collectives: 215 us -> 0 us
  Pallas kernels: 0 us -> 163 us
  matrix products: 162 us -> 0 us
  starting transfers between devices: 1.08 us -> 80.4 us
  other arithmetic: 54.1 us -> 32.8 us
  between operations: 18.2 us -> 2.75 us
    reduce_scatter x2 -> x0, waiting for transfers between devices: 372 us -> none  [the longest x1 186 us: shards(): lax.psum_scatter(joined[9], 'fsdp', scatter_dimension=1, tiled=True)]
    pallas_call x0 -> x15, Pallas kernels: none -> 163 us  [run(): pl.pallas_call(functools.partial(body, **fixed) if fixed else body, name=...]
    dot_general x24 -> x0, matrix products: 162 us -> none  [the longest x2 27.3 us: shards(): jnp.einsum('isd,fd->isf', low_chan, w_cout, preferred_element_type=f32)]
    unnamed x2 -> x0, blocking collectives: 92.4 us -> none
    ppermute x0 -> x71, waiting for transfers between devices: none -> 85.3 us  [the longest x18 48.2 us: along(): lax.ppermute(values, 'fsdp', [(f, f ^ 2 * bits) for f in range(2 * self.l...]
    all_gather x6 -> x0, blocking collectives: 84.5 us -> none  [the longest x2 29.5 us: fetch_forward(): lax.all_gather(pieces[2], 'fsdp', axis=1, tiled=True)]
    unnamed x22 -> x0, waiting for transfers between devices: 82.2 us -> none
    ppermute x0 -> x71, starting transfers between devices: none -> 80.4 us  [the longest x33 38.3 us: across(): lax.ppermute(values, 'dp', [(q, q ^ bits) for q in range(self.copies)])]
  transfers between devices with their start and end apart: 15 -> 71, of which waited for: 8 -> 20; matrix products, arithmetic and copies ran while one was open for 16% -> 9% of each run, Pallas kernels for 0% -> 34%
where the time goes in v1:
time: 402 us; the launch traced here: 397 us
  Pallas kernels  163 us (41%)
  waiting for transfers between devices  85.3 us (21%)
  starting transfers between devices  80.4 us (20%)
  local copies, waits for them, and re-layouts  33 us (8%)
  other arithmetic  32.8 us (8%)
    pallas_call x15, Pallas kernels, run(): pl.pallas_call(functools.partial(body, **fixed) if fixed else body, name=...  163 us
    ppermute x18, waiting for transfers between devices, along(): lax.ppermute(values, 'fsdp', [(f, f ^ 2 * bits) for f in range(2 * self.l...  48.2 us
    ppermute x33, starting transfers between devices, across(): lax.ppermute(values, 'dp', [(q, q ^ bits) for q in range(self.copies)])  38.3 us
    ppermute x18, starting transfers between devices, along(): lax.ppermute(values, 'fsdp', [(f, f ^ 2 * bits) for f in range(2 * self.l...  34 us
    ppermute x33, waiting for transfers between devices, across(): lax.ppermute(values, 'dp', [(q, q ^ bits) for q in range(self.copies)])  30.2 us
    unnamed x131, local copies, waits for them, and re-layouts  13.2 us
    add x4, other arithmetic, both(): return self.mine[copies, part] + self.got[copies, part]  8.71 us
  transfers between devices with their start and end apart: 71, of which 20 were waited for; matrix products, arithmetic and copies ran while one was open for 9% of the time, Pallas kernels for 34%

profile of v1, /device:TPU:0, one launch (start us, length us, event | category | flops | bytes accessed | tf_op | source)
XLA Modules:
  0.0 397.1 jit_solution(1429387965976475739)
XLA Ops:
  0.7 2.2 fusion.12
  5.8 5.0 %collective-permute-start.2 = (bf16[2,96,768]{2,1,0:T(8,128)(2,1)}, bf16[2,96,768]{2,1,0:T(8,128)(2,1)}, u32[]{:S(2)}, u32[]{:S(2)}) collective-permute-start(bf16[2,96,768]{2,1,0:T(8,128)(2,1)} %pad_maximum_fusion.4), channel_id=1, source_target_pairs={{0,6},{1,7},{2,4},{3,5},{4,2},{5,3},{6,0},{7,1},{8,14},{9,15},{10,... | collective-permute-start | bytes 884744 | tf_op jit(solution)/shard_map/ppermute | solution.py:966
  13.6 5.5 %collective-permute-done.2 = bf16[2,96,768]{2,1,0:T(8,128)(2,1)} collective-permute-done((bf16[2,96,768]{2,1,0:T(8,128)(2,1)}, bf16[2,96,768]{2,1,0:T(8,128)(2,1)}, u32[]{:S(2)}, u32[]{:S(2)}) %collective-permute-start.2) | collective-permute-done | bytes 294944 | tf_op jit(solution)/shard_map/ppermute | solution.py:966
  19.2 17.1 %collective-permute-done.1 = bf16[2,96,768]{2,1,0:T(8,128)(2,1)} collective-permute-done((bf16[2,96,768]{2,1,0:T(8,128)(2,1)}, bf16[2,96,768]{2,1,0:T(8,128)(2,1)}, u32[]{:S(2)}, u32[]{:S(2)}) %collective-permute-start.1) | collective-permute-done | bytes 294944 | tf_op jit(solution)/shard_map/ppermute | solution.py:966
  36.4 1.3 pad_maximum_fusion.rest_4_
  37.8 2.5 collective-permute-start.8
  40.3 1.5 collective-permute-start.10
  41.8 1.5 collective-permute-start.9
  43.3 3.1 collective-permute-done.8
  46.4 3.9 collective-permute-start.6
  50.3 2.4 collective-permute-done.7
  52.7 1.7 collective-permute-done.6
  57.3 4.8 %collective-permute-done.10.rest_6_ = bf16[3,2,96,768]{3,2,1,0:T(8,128)(2,1)S(1)} collective-permute-done((bf16[3,2,96,768]{3,2,1,0:T(8,128)(2,1)S(1)}, bf16[3,2,96,768]{3,2,1,0:T(8,128)(2,1)S(1)}, u32[]{:S(2)}, u32[]{:S(2)}) %collective-permute-start.10) | collective-permute-done | bytes 884768 | tf_op jit(solution)/shard_map/ppermute | solution.py:972
  63.3 1.7 collective-permute-done.12
  66.6 1.5 collective-permute-start.14
  68.1 1.5 collective-permute-start.13
  74.8 3.2 unpack_small.1
  78.1 9.4 %token_forward.2 = (bf16[4,256,768]{2,1,0:T(8,128)(2,1)}, bf16[4,384,768]{2,1,0:T(8,128)(2,1)}, bf16[4,384,768]{2,1,0:T(8,128)(2,1)}, f32[4,208,768]{2,1,0:T(8,128)}, bf16[832,768]{1,0:T(8,128)(2,1)}) custom-call(s32[3]{0:T(128)} %pad_add_fusion.place, f32[4,4]{1,0:T(4,128)} %copy.67.scale, bf16[4,208,768]{2,1,0:T(8,128)(2,1)} %pad.36.x, ...), custom_call_target="tpu_custom_call" | custom-call | flops 1207959552 | bytes 11810880 | tf_op jit(solution)/shard_map/token_forward/pallas_call | solution.py:677
  88.7 2.2 collective-permute-start.19
  91.0 9.1 %collective-permute-done.19 = bf16[2,96,768]{2,1,0:T(8,128)(2,1)S(1)} collective-permute-done((bf16[2,96,768]{2,1,0:T(8,128)(2,1)S(1)}, bf16[2,96,768]{2,1,0:T(8,128)(2,1)S(1)}, u32[]{:S(2)}, u32[]{:S(2)}) %collective-permute-start.19) | collective-permute-done | bytes 294944 | tf_op jit(solution)/shard_map/ppermute | solution.py:966
  103.1 20.7 %first_forward.1 = (bf16[4,832,768]{2,1,0:T(8,128)(2,1)}, bf16[4,832,768]{2,1,0:T(8,128)(2,1)}, f32[4,208,768]{2,1,0:T(8,128)}) custom-call(s32[3]{0:T(128)} %pad_add_fusion.place, f32[4,4]{1,0:T(4,128)} %copy.67.scale, bf16[832,768]{1,0:T(8,128)(2,1)} %get-tuple-element.201.v, f32[4,208,768]{2,1,0:T(8,128)} %get-tuple-element.202.middle, ...), custom_call_target="tpu_custom_call" | custom-call | flops 7851737088 | bytes 28425280 | tf_op jit(solution)/shard_map/first_forward/pallas_call | solution.py:677
  126.1 1.4 collective-permute-start.23
  127.4 1.6 collective-permute-start.22
  129.1 9.1 %token_forward.3 = (bf16[4,256,768]{2,1,0:T(8,128)(2,1)}, bf16[4,384,768]{2,1,0:T(8,128)(2,1)}, bf16[4,384,768]{2,1,0:T(8,128)(2,1)}, f32[4,208,768]{2,1,0:T(8,128)}, bf16[832,768]{1,0:T(8,128)(2,1)}) custom-call(s32[3]{0:T(128)} %pad_add_fusion.place, f32[4,4]{1,0:T(4,128)} %copy.67.scale, f32[4,208,768]{2,1,0:T(8,128)} %get-tuple-element.216.x, ...), custom_call_target="tpu_custom_call" | custom-call | flops 1207959552 | bytes 13088832 | tf_op jit(solution)/shard_map/token_forward/pallas_call | solution.py:677
  144.5 21.3 %last_hidden.1 = (bf16[4,832,768]{2,1,0:T(8,128)(2,1)}, bf16[4,832,768]{2,1,0:T(8,128)(2,1)}, bf16[4,4,96,768]{3,2,1,0:T(8,128)(2,1)}, bf16[4,4,96,768]{3,2,1,0:...) custom-call(s32[3]{0:T(128)} %pad_add_fusion.place, f32[4,4]{1,0:T(4,128)} %copy.67.scale, ...), custom_call_target="tpu_custom_call" | custom-call | flops 7851737088 | bytes 30587968 | tf_op jit(solution)/shard_map/last_hidden/pallas_call | solution.py:677
  166.0 20.1 %channel_backward.2 = (bf16[4,4,96,768]{3,2,1,0:T(8,128)(2,1)}, bf16[4,4,96,768]{3,2,1,0:T(8,128)(2,1)}, f32[832,768]{1,0:T(8,128)}, f32[4,1,768]{2,1,0:T(1,128)}) custom-call(s32[3]{0:T(128)} %pad_add_fusion.place, bf16[832,768]{1,0:T(8,128)(2,1)} %get-tuple-element.237.low, bf16[832,768]{1,0:T(8,128)(2,1)} %get-tuple-element.226.v, ...), custom_call_target="tpu_custom_call" | custom-call | flops 11777605632 | bytes 26750976 | tf_op jit(solution)/shard_map/channel_backward/pallas_call | solution.py:677
  186.6 2.2 slice_add_fusion.6
  188.8 2.0 collective-permute-start.30
  190.8 2.0 collective-permute-start.29
  192.8 12.6 %token_backward.2 = (f32[4,208,768]{2,1,0:T(8,128)}, bf16[2,4,48,256]{3,2,1,0:T(8,128)(2,1)}, bf16[2,4,48,256]{3,2,1,0:T(8,128)(2,1)}, f32[16,768]{1,0:T(8,128)}...) custom-call(s32[3]{0:T(128)} %pad_add_fusion.place, f32[4,4]{1,0:T(4,128)} %copy.67.scale, bf16[4,208,768]{2,1,0:T(8,128)(2,1)} %pad.44.grad, ...), custom_call_target="tpu_custom_call" | custom-call | flops 2415919104 | bytes 19931200 | tf_op jit(solution)/shard_map/token_backward/pallas_call | solution.py:677
  206.2 2.6 slice_add_fusion.4
  209.3 2.0 collective-permute-start.34
  211.3 2.3 add_bitcast_fusion.6
  213.6 1.6 collective-permute-start.32
  215.1 10.5 %out_weight_grad.1 = (bf16[4,4,96,768]{3,2,1,0:T(8,128)(2,1)}, bf16[4,4,96,768]{3,2,1,0:T(8,128)(2,1)}) custom-call(s32[3]{0:T(128)} %pad_add_fusion.place, bf16[832,768]{1,0:T(8,128)(2,1)} %get-tuple-element.263.low, bf16[4,832,768]{2,1,0:T(8,128)(2,1)} %get-tuple-element.269.hidden), custom_call_target="tpu_custom_call" | custom-call | flops 3925868544 | bytes 11108352 | tf_op jit(solution)/shard_map/out_weight_grad/pallas_call | solution.py:677
  225.6 4.8 %collective-permute-done.33 = bf16[2,96,768]{2,1,0:T(8,128)(2,1)} collective-permute-done((bf16[2,96,768]{2,1,0:T(8,128)(2,1)}, bf16[2,96,768]{2,1,0:T(8,128)(2,1)}, u32[]{:S(2)}, u32[]{:S(2)}) %collective-permute-start.33) | collective-permute-done | bytes 294944 | tf_op jit(solution)/shard_map/ppermute | solution.py:972
  230.5 2.0 bitcast_add_fusion.7
  232.6 7.1 %collective-permute-start.36 = (bf16[2,96,768]{2,1,0:T(8,128)(2,1)}, bf16[2,96,768]{2,1,0:T(8,128)(2,1)}, u32[]{:S(2)}, u32[]{:S(2)}) collective-permute-start(bf16[2,96,768]{2,1,0:T(8,128)(2,1)} %bitcast_add_fusion.7), channel_id=1, source_target_pairs={{0,4},{1,5},{2,6},{3,7},{4,0},{5,1},{6,2},{7,3},{8,12},{9,13},{10,... | collective-permute-start | bytes 884744 | tf_op jit(solution)/shard_map/ppermute | solution.py:966
  240.8 1.5 collective-permute-start.38
  243.3 20.6 %channel_backward.3 = (bf16[4,4,112,768]{3,2,1,0:T(8,128)(2,1)}, bf16[4,4,112,768]{3,2,1,0:T(8,128)(2,1)}, f32[832,768]{1,0:T(8,128)}, f32[4,1,768]{2,1,0:T(1,128)}) custom-call(s32[3]{0:T(128)} %pad_add_fusion.place, bf16[832,768]{1,0:T(8,128)(2,1)} %get-tuple-element.263.low, bf16[832,768]{1,0:T(8,128)(2,1)} %get-tuple-element.201.v, ...), custom_call_target="tpu_custom_call" | custom-call | flops 11777605632 | bytes 27537408 | tf_op jit(solution)/shard_map/channel_backward/pallas_call | solution.py:677
  264.0 2.0 bitcast_add_fusion.5
  265.9 1.4 collective-permute-start.41
  267.3 2.4 slice_add_fusion.2
  274.2 12.2 %token_backward.3 = (f32[4,208,768]{2,1,0:T(8,128)}, bf16[4,4,112,768]{3,2,1,0:T(8,128)(2,1)}, bf16[4,4,112,768]{3,2,1,0:T(8,128)(2,1)}, f32[32,768]{1,0:T(8,128)}) custom-call(s32[3]{0:T(128)} %pad_add_fusion.place, f32[4,4]{1,0:T(4,128)} %copy.67.scale, f32[4,208,768]{2,1,0:T(8,128)} %get-tuple-element.262.grad, ...), custom_call_target="tpu_custom_call", output_to_operand_aliasing={{1}: (18, {}), {2}: (19, {})} | custom-call | flops 2415919104 | bytes 29758528 | tf_op jit(solution)/shard_map/token_backward/pallas_call | solution.py:677
  290.4 2.0 add_bitcast_fusion.2
  294.6 10.8 %out_forward.1 = bf16[4,208,768]{2,1,0:T(8,128)(2,1)} custom-call(s32[3]{0:T(128)} %pad_add_fusion.place, f32[4,4]{1,0:T(4,128)} %copy.67.scale, bf16[4,832,768]{2,1,0:T(8,128)(2,1)} %get-tuple-element.301.hidden, f32[4,208,768]{2,1,0:T(8,128)} %get-tuple-element.245.middle, f32[1,768]{1,0:T(1,128)} %get-tuple-element.302.bias, ...), custom_call_target="tpu_custom_call" | custom-call | flops 3925868544 | bytes 20745280 | tf_op jit(solution)/shard_map/out_forward/pallas_call | solution.py:677
  306.4 1.5 slice_add_fusion
  311.2 3.0 collective-permute-start.51
  316.0 5.8 %collective-permute-done.53 = f32[32,768]{1,0:T(8,128)S(1)} collective-permute-done((f32[32,768]{1,0:T(8,128)S(1)}, f32[32,768]{1,0:T(8,128)S(1)}, u32[]{:S(2)}, u32[]{:S(2)}) %collective-permute-start.53) | collective-permute-done | bytes 98336 | tf_op jit(solution)/shard_map/ppermute | solution.py:1103
  322.2 6.3 %collective-permute-done.52 = bf16[96,768]{1,0:T(8,128)(2,1)S(1)} collective-permute-done((bf16[96,768]{1,0:T(8,128)(2,1)S(1)}, bf16[96,768]{1,0:T(8,128)(2,1)S(1)}, u32[]{:S(2)}, u32[]{:S(2)}) %collective-permute-start.52) | collective-permute-done | bytes 147488 | tf_op jit(solution)/shard_map/ppermute | solution.py:972
  328.5 3.0 collective-permute-start.59
  334.5 1.7 collective-permute-start.54
  337.8 4.8 %collective-permute-done.56 = bf16[96,768]{1,0:T(8,128)(2,1)S(1)} collective-permute-done((bf16[96,768]{1,0:T(8,128)(2,1)S(1)}, bf16[96,768]{1,0:T(8,128)(2,1)S(1)}, u32[]{:S(2)}, u32[]{:S(2)}) %collective-permute-start.56) | collective-permute-done | bytes 147488 | tf_op jit(solution)/shard_map/ppermute | solution.py:966
  342.6 3.4 collective-permute-done.54
  350.5 1.7 collective-permute-start.61
  354.5 7.0 %collective-permute-done.64 = bf16[96,768]{1,0:T(8,128)(2,1)S(1)} collective-permute-done((bf16[96,768]{1,0:T(8,128)(2,1)S(1)}, bf16[96,768]{1,0:T(8,128)(2,1)S(1)}, u32[]{:S(2)}, u32[]{:S(2)}) %collective-permute-start.64) | collective-permute-done | bytes 147488 | tf_op jit(solution)/shard_map/ppermute | solution.py:972
  361.5 2.7 collective-permute-done.61
  371.6 2.4 copy.73
  375.3 1.5 copy.72
  376.8 3.2 finish_out.2.refs_4_
  380.0 2.9 finish_in.2.refs_4_
  383.0 3.0 finish_in.3
  386.9 1.6 slice_bitcast_fusion.10
  393.6 3.2 finish_out.3
  (301 shorter events, 75.6 us)
Async XLA Ops:
  5.8 13.3 %collective-permute-start.2 = (bf16[2,96,768]{2,1,0:T(8,128)(2,1)}, bf16[2,96,768]{2,1,0:T(8,128)(2,1)}, u32[]{:S(2)}, u32[]{:S(2)}) collective-permute-start(bf16[2,96,768]{2,1,0:T(8,128)(2,1)} %pad_maximum_fusion.4), channel_id=1, source_target_pairs={{0,6},{1,7},{2,4},{3,5},{4,2},{5,3},{6,0},{7,1},{8,14},{9,15},{10,... | collective-permute-start | bytes 884744 | tf_op jit(solution)/shard_map/ppermute | solution.py:966
  10.9 25.4 %collective-permute-start.1 = (bf16[2,96,768]{2,1,0:T(8,128)(2,1)}, bf16[2,96,768]{2,1,0:T(8,128)(2,1)}, u32[]{:S(2)}, u32[]{:S(2)}) collective-permute-start(bf16[2,96,768]{2,1,0:T(8,128)(2,1)} %pad_maximum_fusion.4), channel_id=1, source_target_pairs={{0,4},{1,5},{2,6},{3,7},{4,0},{5,1},{6,2},{7,3},{8,12},{9,13},{10,... | collective-permute-start | bytes 884744 | tf_op jit(solution)/shard_map/ppermute | solution.py:966
  10.9 25.4 %collective-permute-start = (bf16[2,96,768]{2,1,0:T(8,128)(2,1)}, bf16[2,96,768]{2,1,0:T(8,128)(2,1)}, u32[]{:S(2)}, u32[]{:S(2)}) collective-permute-start(bf16[2,96,768]{2,1,0:T(8,128)(2,1)} %pad_maximum_fusion.4), channel_id=1, source_target_pairs={{0,2},{1,3},{2,0},{3,1},{4,6},{5,7},{6,4},{7,5},{8,10},{9,11},{10,... | collective-permute-start | bytes 884744 | tf_op jit(solution)/shard_map/ppermute | solution.py:966
  11.4 24.9 %collective-permute-start.3 = (bf16[2,96,3072]{2,1,0:T(8,128)(2,1)S(1)}, bf16[2,96,3072]{2,1,0:T(8,128)(2,1)}, u32[]{:S(2)}, u32[]{:S(2)}) collective-permute-start(bf16[2,96,3072]{2,1,0:T(8,128)(2,1)S(1)} %copy-done.1), channel_id=1, source_target_pairs={{0,1},{1,0},{2,3},{3,2},{4,5},{5,4},{6,7},{7,6},{8,9},{9,8},{10,11... | collective-permute-start | bytes 3538952 | tf_op jit(solution)/shard_map/ppermute | solution.py:969
  11.4 24.9 %collective-permute-start.4 = (bf16[2,384,768]{2,1,0:T(8,128)(2,1)S(1)}, bf16[2,384,768]{2,1,0:T(8,128)(2,1)}, u32[]{:S(2)}, u32[]{:S(2)}) collective-permute-start(bf16[2,384,768]{2,1,0:T(8,128)(2,1)S(1)} %copy-done.2), channel_id=1, source_target_pairs={{0,1},{1,0},{2,3},{3,2},{4,5},{5,4},{6,7},{7,6},{8,9},{9,8},{10,11... | collective-permute-start | bytes 3538952 | tf_op jit(solution)/shard_map/ppermute | solution.py:969
  37.7 16.8 %collective-permute-start.5 = (bf16[3,2,96,768]{3,2,1,0:T(8,128)(2,1)S(1)}, bf16[3,2,96,768]{3,2,1,0:T(8,128)(2,1)S(1)}, u32[]{:S(2)}, u32[]{:S(2)}) collective-permute-start(bf16[3,2,96,768]{3,2,1,0:T(8,128)(2,1)S(1)} %pad_maximum_fusion.rest_4_), channel_id=1, source_target_pairs={{0,1},{1,0},{2,3},{3,2},{4,5},{5,4},{6,7},{7,6},{8,9},{9,8},{10,11... | collective-permute-start | bytes 2654216 | tf_op jit(solution)/shard_map/ppermute | solution.py:969
  40.3 21.7 %collective-permute-start.10 = (bf16[3,2,96,768]{3,2,1,0:T(8,128)(2,1)S(1)}, bf16[3,2,96,768]{3,2,1,0:T(8,128)(2,1)S(1)}, u32[]{:S(2)}, u32[]{:S(2)}) collective-permute-start(bf16[3,2,96,768]{3,2,1,0:T(8,128)(2,1)S(1)} %pad_maximum_fusion.rest_4_), channel_id=1, source_target_pairs={{0,16},{8,24},{16,0},{24,8},{1,17},{9,25},{17,1},{25,9},{2,18},{10... | collective-permute-start | bytes 2654216 | tf_op jit(solution)/shard_map/ppermute | solution.py:972
  41.8 21.4 %collective-permute-start.9 = (bf16[3,2,96,768]{3,2,1,0:T(8,128)(2,1)S(1)}, bf16[3,2,96,768]{3,2,1,0:T(8,128)(2,1)S(1)}, u32[]{:S(2)}, u32[]{:S(2)}) collective-permute-start(bf16[3,2,96,768]{3,2,1,0:T(8,128)(2,1)S(1)} %pad_maximum_fusion.rest_4_), channel_id=1, source_target_pairs={{0,8},{8,0},{16,24},{24,16},{1,9},{9,1},{17,25},{25,17},{2,10},{10... | collective-permute-start | bytes 2654216 | tf_op jit(solution)/shard_map/ppermute | solution.py:972
  43.3 9.4 %collective-permute-start.7 = (bf16[96,768]{1,0:T(8,128)(2,1)S(1)}, bf16[96,768]{1,0:T(8,128)(2,1)S(1)}, u32[]{:S(2)}, u32[]{:S(2)}) collective-permute-start(bf16[96,768]{1,0:T(8,128)(2,1)S(1)} %bitcast.147), channel_id=1, source_target_pairs={{0,4},{1,5},{2,6},{3,7},{4,0},{5,1},{6,2},{7,3},{8,12},{9,13},{10,... | collective-permute-start | bytes 442376 | tf_op jit(solution)/shard_map/ppermute | solution.py:966
  55.5 10.2 %collective-permute-start.11 = (bf16[4,96,768]{2,1,0:T(8,128)(2,1)S(1)}, bf16[4,96,768]{2,1,0:T(8,128)(2,1)S(1)}, u32[]{:S(2)}, u32[]{:S(2)}) collective-permute-start(bf16[4,96,768]{2,1,0:T(8,128)(2,1)S(1)} %pad_maximum_fusion.2.own), channel_id=1, source_target_pairs={{0,1},{1,0},{2,3},{3,2},{4,5},{5,4},{6,7},{7,6},{8,9},{9,8},{10,11... | collective-permute-start | bytes 1769480 | tf_op jit(solution)/shard_map/ppermute | solution.py:969
  55.5 9.4 %collective-permute-start.12 = (bf16[2,96,768]{2,1,0:T(8,128)(2,1)S(1)}, bf16[2,96,768]{2,1,0:T(8,128)(2,1)S(1)}, u32[]{:S(2)}, u32[]{:S(2)}) collective-permute-start(bf16[2,96,768]{2,1,0:T(8,128)(2,1)S(1)} %pad_maximum_fusion.3), channel_id=1, source_target_pairs={{0,2},{1,3},{2,0},{3,1},{4,6},{5,7},{6,4},{7,5},{8,10},{9,11},{10,... | collective-permute-start | bytes 884744 | tf_op jit(solution)/shard_map/ppermute | solution.py:966
  66.6 20.9 %collective-permute-start.14 = (bf16[3,1,96,768]{3,2,1,0:T(8,128)(2,1)}, bf16[3,1,96,768]{3,2,1,0:T(8,128)(2,1)S(1)}, u32[]{:S(2)}, u32[]{:S(2)}) collective-permute-start(bf16[3,1,96,768]{3,2,1,0:T(8,128)(2,1)} %slice.284), channel_id=1, source_target_pairs={{0,16},{8,24},{16,0},{24,8},{1,17},{9,25},{17,1},{25,9},{2,18},{10... | collective-permute-start | bytes 1327112 | tf_op jit(solution)/shard_map/ppermute | solution.py:972
  68.1 19.4 %collective-permute-start.13 = (bf16[3,1,96,768]{3,2,1,0:T(8,128)(2,1)S(1)}, bf16[3,1,96,768]{3,2,1,0:T(8,128)(2,1)}, u32[]{:S(2)}, u32[]{:S(2)}) collective-permute-start(bf16[3,1,96,768]{3,2,1,0:T(8,128)(2,1)S(1)} %slice.283), channel_id=1, source_target_pairs={{0,8},{8,0},{16,24},{24,16},{1,9},{9,1},{17,25},{25,17},{2,10},{10... | collective-permute-start | bytes 1327112 | tf_op jit(solution)/shard_map/ppermute | solution.py:972
  70.3 17.2 %collective-permute-start.15 = (bf16[2,96,768]{2,1,0:T(8,128)(2,1)}, bf16[2,96,768]{2,1,0:T(8,128)(2,1)}, u32[]{:S(2)}, u32[]{:S(2)}) collective-permute-start(bf16[2,96,768]{2,1,0:T(8,128)(2,1)} %copy-done.37), channel_id=1, source_target_pairs={{0,4},{1,5},{2,6},{3,7},{4,0},{5,1},{6,2},{7,3},{8,12},{9,13},{10,... | collective-permute-start | bytes 884744 | tf_op jit(solution)/shard_map/ppermute | solution.py:966
  74.3 25.7 %collective-permute-start.17 = (bf16[3,2,96,768]{3,2,1,0:T(8,128)(2,1)S(1)}, bf16[3,2,96,768]{3,2,1,0:T(8,128)(2,1)}, u32[]{:S(2)}, u32[]{:S(2)}) collective-permute-start(bf16[3,2,96,768]{3,2,1,0:T(8,128)(2,1)S(1)} %copy-done.40), channel_id=1, source_target_pairs={{0,1},{1,0},{2,3},{3,2},{4,5},{5,4},{6,7},{7,6},{8,9},{9,8},{10,11... | collective-permute-start | bytes 2654216 | tf_op jit(solution)/shard_map/ppermute | solution.py:969
  74.3 25.7 %collective-permute-start.16 = (bf16[3,2,96,768]{3,2,1,0:T(8,128)(2,1)}, bf16[3,2,96,768]{3,2,1,0:T(8,128)(2,1)}, u32[]{:S(2)}, u32[]{:S(2)}) collective-permute-start(bf16[3,2,96,768]{3,2,1,0:T(8,128)(2,1)} %copy-done.41), channel_id=1, source_target_pairs={{0,1},{1,0},{2,3},{3,2},{4,5},{5,4},{6,7},{7,6},{8,9},{9,8},{10,11... | collective-permute-start | bytes 2654216 | tf_op jit(solution)/shard_map/ppermute | solution.py:969
  88.6 11.4 %collective-permute-start.18 = (bf16[3,2,96,768]{3,2,1,0:T(8,128)(2,1)S(1)}, bf16[3,2,96,768]{3,2,1,0:T(8,128)(2,1)S(1)}, u32[]{:S(2)}, u32[]{:S(2)}) collective-permute-start(bf16[3,2,96,768]{3,2,1,0:T(8,128)(2,1)S(1)} %constant_dynamic-update-slice_fusion.5.rest_7_), channel_id=1, source_target_pairs={{0,1},{1,0},{2,3},{3,2},{4,5},{5,4},{6,7},{7,6},{8,9},{9,8},{10,11... | collective-permute-start | bytes 2654216 | tf_op jit(solution)/shard_map/ppermute | solution.py:969
  88.7 11.3 %collective-permute-start.19 = (bf16[2,96,768]{2,1,0:T(8,128)(2,1)S(1)}, bf16[2,96,768]{2,1,0:T(8,128)(2,1)S(1)}, u32[]{:S(2)}, u32[]{:S(2)}) collective-permute-start(bf16[2,96,768]{2,1,0:T(8,128)(2,1)S(1)} %copy-done.38), channel_id=1, source_target_pairs={{0,6},{1,7},{2,4},{3,5},{4,2},{5,3},{6,0},{7,1},{8,14},{9,15},{10,... | collective-permute-start | bytes 884744 | tf_op jit(solution)/shard_map/ppermute | solution.py:966
  102.1 21.7 %collective-permute-start.21 = (bf16[3,2,96,768]{3,2,1,0:T(8,128)(2,1)S(1)}, bf16[3,2,96,768]{3,2,1,0:T(8,128)(2,1)S(1)}, u32[]{:S(2)}, u32[]{:S(2)}) collective-permute-start(bf16[3,2,96,768]{3,2,1,0:T(8,128)(2,1)S(1)} %pad_maximum_fusion.1.rest_4_), channel_id=1, source_target_pairs={{0,16},{8,24},{16,0},{24,8},{1,17},{9,25},{17,1},{25,9},{2,18},{10... | collective-permute-start | bytes 2654216 | tf_op jit(solution)/shard_map/ppermute | solution.py:972
  102.6 21.2 %collective-permute-start.20 = (bf16[3,2,96,768]{3,2,1,0:T(8,128)(2,1)S(1)}, bf16[3,2,96,768]{3,2,1,0:T(8,128)(2,1)S(1)}, u32[]{:S(2)}, u32[]{:S(2)}) collective-permute-start(bf16[3,2,96,768]{3,2,1,0:T(8,128)(2,1)S(1)} %pad_maximum_fusion.1.rest_4_), channel_id=1, source_target_pairs={{0,8},{8,0},{16,24},{24,16},{1,9},{9,1},{17,25},{25,17},{2,10},{10... | collective-permute-start | bytes 2654216 | tf_op jit(solution)/shard_map/ppermute | solution.py:972
  103.1 35.1 %collective-permute-start.24 = (bf16[3,2,96,768]{3,2,1,0:T(8,128)(2,1)S(1)}, bf16[3,2,96,768]{3,2,1,0:T(8,128)(2,1)S(1)}, u32[]{:S(2)}, u32[]{:S(2)}) collective-permute-start(bf16[3,2,96,768]{3,2,1,0:T(8,128)(2,1)S(1)} %pad_maximum_fusion.1.rest_4_), channel_id=1, source_target_pairs={{0,1},{1,0},{2,3},{3,2},{4,5},{5,4},{6,7},{7,6},{8,9},{9,8},{10,11... | collective-permute-start | bytes 2654216 | tf_op jit(solution)/shard_map/ppermute | solution.py:969
  123.8 16.1 %collective-permute-start.26 = (bf16[3,2,96,768]{3,2,1,0:T(8,128)(2,1)S(1)}, bf16[3,2,96,768]{3,2,1,0:T(8,128)(2,1)}, u32[]{:S(2)}, u32[]{:S(2)}) collective-permute-start(bf16[3,2,96,768]{3,2,1,0:T(8,128)(2,1)S(1)} %collective-permute-done.21.rest_6_), channel_id=1, source_target_pairs={{0,1},{1,0},{2,3},{3,2},{4,5},{5,4},{6,7},{7,6},{8,9},{9,8},{10,11... | collective-permute-start | bytes 2654216 | tf_op jit(solution)/shard_map/ppermute | solution.py:969
  124.4 15.6 %collective-permute-start.25 = (bf16[3,2,96,768]{3,2,1,0:T(8,128)(2,1)S(1)}, bf16[3,2,96,768]{3,2,1,0:T(8,128)(2,1)}, u32[]{:S(2)}, u32[]{:S(2)}) collective-permute-start(bf16[3,2,96,768]{3,2,1,0:T(8,128)(2,1)S(1)} %collective-permute-done.20.rest_5_), channel_id=1, source_target_pairs={{0,1},{1,0},{2,3},{3,2},{4,5},{5,4},{6,7},{7,6},{8,9},{9,8},{10,11... | collective-permute-start | bytes 2654216 | tf_op jit(solution)/shard_map/ppermute | solution.py:969
  126.1 12.7 %collective-permute-start.23 = (bf16[3,1,96,768]{3,2,1,0:T(8,128)(2,1)}, bf16[3,1,96,768]{3,2,1,0:T(8,128)(2,1)S(1)}, u32[]{:S(2)}, u32[]{:S(2)}) collective-permute-start(bf16[3,1,96,768]{3,2,1,0:T(8,128)(2,1)} %slice.286), channel_id=1, source_target_pairs={{0,16},{8,24},{16,0},{24,8},{1,17},{9,25},{17,1},{25,9},{2,18},{10... | collective-permute-start | bytes 1327112 | tf_op jit(solution)/shard_map/ppermute | solution.py:972
  127.4 12.6 %collective-permute-start.22 = (bf16[3,1,96,768]{3,2,1,0:T(8,128)(2,1)}, bf16[3,1,96,768]{3,2,1,0:T(8,128)(2,1)}, u32[]{:S(2)}, u32[]{:S(2)}) collective-permute-start(bf16[3,1,96,768]{3,2,1,0:T(8,128)(2,1)} %slice.285), channel_id=1, source_target_pairs={{0,8},{8,0},{16,24},{24,16},{1,9},{9,1},{17,25},{25,17},{2,10},{10... | collective-permute-start | bytes 1327112 | tf_op jit(solution)/shard_map/ppermute | solution.py:972
  165.8 20.3 %collective-permute-start.28 = (bf16[4,4,96,768]{3,2,1,0:T(8,128)(2,1)}, bf16[4,4,96,768]{3,2,1,0:T(8,128)(2,1)}, u32[]{:S(2)}, u32[]{:S(2)}) collective-permute-start(bf16[4,4,96,768]{3,2,1,0:T(8,128)(2,1)} %get-tuple-element.243), channel_id=1, source_target_pairs={{0,1},{1,0},{2,3},{3,2},{4,5},{5,4},{6,7},{7,6},{8,9},{9,8},{10,11... | collective-permute-start | bytes 7077896 | tf_op jit(solution)/shard_map/ppermute | solution.py:969
  186.1 20.0 %collective-permute-start.31 = (bf16[4,4,96,768]{3,2,1,0:T(8,128)(2,1)}, bf16[4,4,96,768]{3,2,1,0:T(8,128)(2,1)}, u32[]{:S(2)}, u32[]{:S(2)}) collective-permute-start(bf16[4,4,96,768]{3,2,1,0:T(8,128)(2,1)} %get-tuple-element.261), channel_id=1, source_target_pairs={{0,1},{1,0},{2,3},{3,2},{4,5},{5,4},{6,7},{7,6},{8,9},{9,8},{10,11... | collective-permute-start | bytes 7077896 | tf_op jit(solution)/shard_map/ppermute | solution.py:969
  188.8 16.6 %collective-permute-start.30 = (bf16[2,2,96,768]{3,2,1,0:T(8,128)(2,1)}, bf16[2,2,96,768]{3,2,1,0:T(8,128)(2,1)S(1)}, u32[]{:S(2)}, u32[]{:S(2)}) collective-permute-start(bf16[2,2,96,768]{3,2,1,0:T(8,128)(2,1)} %get-tuple-element.388), channel_id=1, source_target_pairs={{0,16},{8,24},{16,0},{24,8},{1,17},{9,25},{17,1},{25,9},{2,18},{10... | collective-permute-start | bytes 1769480 | tf_op jit(solution)/shard_map/ppermute | solution.py:972
  190.8 15.3 %collective-permute-start.29 = (bf16[2,2,96,768]{3,2,1,0:T(8,128)(2,1)S(1)}, bf16[2,2,96,768]{3,2,1,0:T(8,128)(2,1)S(1)}, u32[]{:S(2)}, u32[]{:S(2)}) collective-permute-start(bf16[2,2,96,768]{3,2,1,0:T(8,128)(2,1)S(1)} %get-tuple-element.389), channel_id=1, source_target_pairs={{0,8},{8,0},{16,24},{24,16},{1,9},{9,1},{17,25},{25,17},{2,10},{10... | collective-permute-start | bytes 1769480 | tf_op jit(solution)/shard_map/ppermute | solution.py:972
  208.8 21.6 %collective-permute-start.35 = (bf16[2,2,96,768]{3,2,1,0:T(8,128)(2,1)}, bf16[2,2,96,768]{3,2,1,0:T(8,128)(2,1)S(1)}, u32[]{:S(2)}, u32[]{:S(2)}) collective-permute-start(bf16[2,2,96,768]{3,2,1,0:T(8,128)(2,1)} %get-tuple-element.384), channel_id=1, source_target_pairs={{0,16},{8,24},{16,0},{24,8},{1,17},{9,25},{17,1},{25,9},{2,18},{10... | collective-permute-start | bytes 1769480 | tf_op jit(solution)/shard_map/ppermute | solution.py:972
  209.3 21.1 %collective-permute-start.34 = (bf16[2,2,96,768]{3,2,1,0:T(8,128)(2,1)}, bf16[2,2,96,768]{3,2,1,0:T(8,128)(2,1)S(1)}, u32[]{:S(2)}, u32[]{:S(2)}) collective-permute-start(bf16[2,2,96,768]{3,2,1,0:T(8,128)(2,1)} %get-tuple-element.385), channel_id=1, source_target_pairs={{0,8},{8,0},{16,24},{24,16},{1,9},{9,1},{17,25},{25,17},{2,10},{10... | collective-permute-start | bytes 1769480 | tf_op jit(solution)/shard_map/ppermute | solution.py:972
  213.5 16.9 %collective-permute-start.33 = (bf16[2,96,768]{2,1,0:T(8,128)(2,1)}, bf16[2,96,768]{2,1,0:T(8,128)(2,1)}, u32[]{:S(2)}, u32[]{:S(2)}) collective-permute-start(bf16[2,96,768]{2,1,0:T(8,128)(2,1)} %get-tuple-element.386), channel_id=1, source_target_pairs={{0,8},{8,0},{16,24},{24,16},{1,9},{9,1},{17,25},{25,17},{2,10},{10... | collective-permute-start | bytes 884744 | tf_op jit(solution)/shard_map/ppermute | solution.py:972
  213.6 16.9 %collective-permute-start.32 = (bf16[2,96,768]{2,1,0:T(8,128)(2,1)}, bf16[2,96,768]{2,1,0:T(8,128)(2,1)}, u32[]{:S(2)}, u32[]{:S(2)}) collective-permute-start(bf16[2,96,768]{2,1,0:T(8,128)(2,1)} %get-tuple-element.387), channel_id=1, source_target_pairs={{0,16},{8,24},{16,0},{24,8},{1,17},{9,25},{17,1},{25,9},{2,18},{10... | collective-permute-start | bytes 884744 | tf_op jit(solution)/shard_map/ppermute | solution.py:972
  230.4 33.5 %collective-permute-start.39 = (bf16[4,4,96,768]{3,2,1,0:T(8,128)(2,1)}, bf16[4,4,96,768]{3,2,1,0:T(8,128)(2,1)}, u32[]{:S(2)}, u32[]{:S(2)}) collective-permute-start(bf16[4,4,96,768]{3,2,1,0:T(8,128)(2,1)} %get-tuple-element.278), channel_id=1, source_target_pairs={{0,1},{1,0},{2,3},{3,2},{4,5},{5,4},{6,7},{7,6},{8,9},{9,8},{10,11... | collective-permute-start | bytes 7077896 | tf_op jit(solution)/shard_map/ppermute | solution.py:969
  232.6 31.4 %collective-permute-start.36 = (bf16[2,96,768]{2,1,0:T(8,128)(2,1)}, bf16[2,96,768]{2,1,0:T(8,128)(2,1)}, u32[]{:S(2)}, u32[]{:S(2)}) collective-permute-start(bf16[2,96,768]{2,1,0:T(8,128)(2,1)} %bitcast_add_fusion.7), channel_id=1, source_target_pairs={{0,4},{1,5},{2,6},{3,7},{4,0},{5,1},{6,2},{7,3},{8,12},{9,13},{10,... | collective-permute-start | bytes 884744 | tf_op jit(solution)/shard_map/ppermute | solution.py:966
  240.8 23.1 %collective-permute-start.38 = (bf16[2,96,768]{2,1,0:T(8,128)(2,1)S(1)}, bf16[2,96,768]{2,1,0:T(8,128)(2,1)}, u32[]{:S(2)}, u32[]{:S(2)}) collective-permute-start(bf16[2,96,768]{2,1,0:T(8,128)(2,1)S(1)} %get-tuple-element.382), channel_id=1, source_target_pairs={{0,8},{8,0},{16,24},{24,16},{1,9},{9,1},{17,25},{25,17},{2,10},{10... | collective-permute-start | bytes 884744 | tf_op jit(solution)/shard_map/ppermute | solution.py:972
  242.3 21.7 %collective-permute-start.37 = (bf16[2,96,768]{2,1,0:T(8,128)(2,1)S(1)}, bf16[2,96,768]{2,1,0:T(8,128)(2,1)}, u32[]{:S(2)}, u32[]{:S(2)}) collective-permute-start(bf16[2,96,768]{2,1,0:T(8,128)(2,1)S(1)} %get-tuple-element.383), channel_id=1, source_target_pairs={{0,16},{8,24},{16,0},{24,8},{1,17},{9,25},{17,1},{25,9},{2,18},{10... | collective-permute-start | bytes 884744 | tf_op jit(solution)/shard_map/ppermute | solution.py:972
  265.9 20.4 %collective-permute-start.41 = (bf16[2,96,768]{2,1,0:T(8,128)(2,1)}, bf16[2,96,768]{2,1,0:T(8,128)(2,1)S(1)}, u32[]{:S(2)}, u32[]{:S(2)}) collective-permute-start(bf16[2,96,768]{2,1,0:T(8,128)(2,1)} %bitcast_add_fusion.5), channel_id=1, source_target_pairs={{0,4},{1,5},{2,6},{3,7},{4,0},{5,1},{6,2},{7,3},{8,12},{9,13},{10,... | collective-permute-start | bytes 884744 | tf_op jit(solution)/shard_map/ppermute | solution.py:966
  269.7 16.7 %collective-permute-start.43 = (bf16[2,2,96,768]{3,2,1,0:T(8,128)(2,1)}, bf16[2,2,96,768]{3,2,1,0:T(8,128)(2,1)}, u32[]{:S(2)}, u32[]{:S(2)}) collective-permute-start(bf16[2,2,96,768]{3,2,1,0:T(8,128)(2,1)} %get-tuple-element.380), channel_id=1, source_target_pairs={{0,16},{8,24},{16,0},{24,8},{1,17},{9,25},{17,1},{25,9},{2,18},{10... | collective-permute-start | bytes 1769480 | tf_op jit(solution)/shard_map/ppermute | solution.py:972
  270.7 15.7 %collective-permute-start.42 = (bf16[2,2,96,768]{3,2,1,0:T(8,128)(2,1)}, bf16[2,2,96,768]{3,2,1,0:T(8,128)(2,1)S(1)}, u32[]{:S(2)}, u32[]{:S(2)}) collective-permute-start(bf16[2,2,96,768]{3,2,1,0:T(8,128)(2,1)} %get-tuple-element.381), channel_id=1, source_target_pairs={{0,8},{8,0},{16,24},{24,16},{1,9},{9,1},{17,25},{25,17},{2,10},{10... | collective-permute-start | bytes 1769480 | tf_op jit(solution)/shard_map/ppermute | solution.py:972
  273.3 13.1 %collective-permute-start.40 = (bf16[96,768]{1,0:T(8,128)(2,1)S(1)}, bf16[96,768]{1,0:T(8,128)(2,1)S(1)}, u32[]{:S(2)}, u32[]{:S(2)}) collective-permute-start(bf16[96,768]{1,0:T(8,128)(2,1)S(1)} %slice_bitcast_fusion.9), channel_id=1, source_target_pairs={{0,2},{1,3},{2,0},{3,1},{4,6},{5,7},{6,4},{7,5},{8,10},{9,11},{10,... | collective-permute-start | bytes 442376 | tf_op jit(solution)/shard_map/ppermute | solution.py:966
  286.4 20.0 %collective-permute-start.44 = (bf16[4,4,112,768]{3,2,1,0:T(8,128)(2,1)}, bf16[4,4,112,768]{3,2,1,0:T(8,128)(2,1)}, u32[]{:S(2)}, u32[]{:S(2)}) collective-permute-start(bf16[4,4,112,768]{3,2,1,0:T(8,128)(2,1)} %get-tuple-element.303), channel_id=1, source_target_pairs={{0,1},{1,0},{2,3},{3,2},{4,5},{5,4},{6,7},{7,6},{8,9},{9,8},{10,11... | collective-permute-start | bytes 8257544 | tf_op jit(solution)/shard_map/ppermute | solution.py:969
  287.2 18.2 %collective-permute-start.48 = (f32[32,768]{1,0:T(8,128)}, f32[32,768]{1,0:T(8,128)}, u32[]{:S(2)}, u32[]{:S(2)}) collective-permute-start(f32[32,768]{1,0:T(8,128)} %get-tuple-element.308), channel_id=1, source_target_pairs={{0,1},{1,0},{2,3},{3,2},{4,5},{5,4},{6,7},{7,6},{8,9},{9,8},{10,11... | collective-permute-start | bytes 294920 | tf_op jit(solution)/shard_map/ppermute | solution.py:1103
  289.2 17.1 %collective-permute-start.47 = (bf16[96,768]{1,0:T(8,128)(2,1)}, bf16[96,768]{1,0:T(8,128)(2,1)S(1)}, u32[]{:S(2)}, u32[]{:S(2)}) collective-permute-start(bf16[96,768]{1,0:T(8,128)(2,1)} %slice_bitcast_fusion.8), channel_id=1, source_target_pairs={{0,2},{1,3},{2,0},{3,1},{4,6},{5,7},{6,4},{7,5},{8,10},{9,11},{10,... | collective-permute-start | bytes 442376 | tf_op jit(solution)/shard_map/ppermute | solution.py:966
  292.5 13.9 %collective-permute-start.46 = (bf16[2,96,768]{2,1,0:T(8,128)(2,1)}, bf16[2,96,768]{2,1,0:T(8,128)(2,1)}, u32[]{:S(2)}, u32[]{:S(2)}) collective-permute-start(bf16[2,96,768]{2,1,0:T(8,128)(2,1)} %get-tuple-element.378), channel_id=1, source_target_pairs={{0,8},{8,0},{16,24},{24,16},{1,9},{9,1},{17,25},{25,17},{2,10},{10... | collective-permute-start | bytes 884744 | tf_op jit(solution)/shard_map/ppermute | solution.py:972
  293.2 13.1 %collective-permute-start.45 = (bf16[2,96,768]{2,1,0:T(8,128)(2,1)S(1)}, bf16[2,96,768]{2,1,0:T(8,128)(2,1)}, u32[]{:S(2)}, u32[]{:S(2)}) collective-permute-start(bf16[2,96,768]{2,1,0:T(8,128)(2,1)S(1)} %get-tuple-element.379), channel_id=1, source_target_pairs={{0,16},{8,24},{16,0},{24,8},{1,17},{9,25},{17,1},{25,9},{2,18},{10... | collective-permute-start | bytes 884744 | tf_op jit(solution)/shard_map/ppermute | solution.py:972
  307.9 20.7 %collective-permute-start.50 = (bf16[2,2,112,768]{3,2,1,0:T(8,128)(2,1)S(1)}, bf16[2,2,112,768]{3,2,1,0:T(8,128)(2,1)S(1)}, u32[]{:S(2)}, u32[]{:S(2)}) collective-permute-start(bf16[2,2,112,768]{3,2,1,0:T(8,128)(2,1)S(1)} %get-tuple-element.376), channel_id=1, source_target_pairs={{0,16},{8,24},{16,0},{24,8},{1,17},{9,25},{17,1},{25,9},{2,18},{10... | collective-permute-start | bytes 2064392 | tf_op jit(solution)/shard_map/ppermute | solution.py:972
  308.6 19.9 %collective-permute-start.49 = (bf16[2,2,112,768]{3,2,1,0:T(8,128)(2,1)S(1)}, bf16[2,2,112,768]{3,2,1,0:T(8,128)(2,1)S(1)}, u32[]{:S(2)}, u32[]{:S(2)}) collective-permute-start(bf16[2,2,112,768]{3,2,1,0:T(8,128)(2,1)S(1)} %get-tuple-element.377), channel_id=1, source_target_pairs={{0,8},{8,0},{16,24},{24,16},{1,9},{9,1},{17,25},{25,17},{2,10},{10... | collective-permute-start | bytes 2064392 | tf_op jit(solution)/shard_map/ppermute | solution.py:972
  311.2 17.3 %collective-permute-start.51 = (bf16[2,96,768]{2,1,0:T(8,128)(2,1)S(1)}, bf16[2,96,768]{2,1,0:T(8,128)(2,1)S(1)}, u32[]{:S(2)}, u32[]{:S(2)}) collective-permute-start(bf16[2,96,768]{2,1,0:T(8,128)(2,1)S(1)} %bitcast_add_fusion.3), channel_id=1, source_target_pairs={{0,4},{1,5},{2,6},{3,7},{4,0},{5,1},{6,2},{7,3},{8,12},{9,13},{10,... | collective-permute-start | bytes 884744 | tf_op jit(solution)/shard_map/ppermute | solution.py:966
  314.2 14.3 %collective-permute-start.52 = (bf16[96,768]{1,0:T(8,128)(2,1)S(1)}, bf16[96,768]{1,0:T(8,128)(2,1)S(1)}, u32[]{:S(2)}, u32[]{:S(2)}) collective-permute-start(bf16[96,768]{1,0:T(8,128)(2,1)S(1)} %fusion.4), channel_id=1, source_target_pairs={{0,8},{8,0},{16,24},{24,16},{1,9},{9,1},{17,25},{25,17},{2,10},{10... | collective-permute-start | bytes 442376 | tf_op jit(solution)/shard_map/ppermute | solution.py:972
  321.9 15.9 %collective-permute-start.57 = (bf16[96,768]{1,0:T(8,128)(2,1)S(1)}, bf16[96,768]{1,0:T(8,128)(2,1)S(1)}, u32[]{:S(2)}, u32[]{:S(2)}) collective-permute-start(bf16[96,768]{1,0:T(8,128)(2,1)S(1)} %fusion.5), channel_id=1, source_target_pairs={{0,16},{8,24},{16,0},{24,8},{1,17},{9,25},{17,1},{25,9},{2,18},{10... | collective-permute-start | bytes 442376 | tf_op jit(solution)/shard_map/ppermute | solution.py:972
  328.5 8.9 %collective-permute-start.59 = (f32[32,768]{1,0:T(8,128)S(1)}, f32[32,768]{1,0:T(8,128)S(1)}, u32[]{:S(2)}, u32[]{:S(2)}) collective-permute-start(f32[32,768]{1,0:T(8,128)S(1)} %add.352), channel_id=1, source_target_pairs={{0,4},{1,5},{2,6},{3,7},{4,0},{5,1},{6,2},{7,3},{8,12},{9,13},{10,... | collective-permute-start | bytes 294920 | tf_op jit(solution)/shard_map/ppermute | solution.py:1103
  331.5 11.1 %collective-permute-start.58 = (bf16[2,96,768]{2,1,0:T(8,128)(2,1)S(1)}, bf16[2,96,768]{2,1,0:T(8,128)(2,1)S(1)}, u32[]{:S(2)}, u32[]{:S(2)}) collective-permute-start(bf16[2,96,768]{2,1,0:T(8,128)(2,1)S(1)} %pad_maximum_fusion.5), channel_id=1, source_target_pairs={{0,16},{8,24},{16,0},{24,8},{1,17},{9,25},{17,1},{25,9},{2,18},{10... | collective-permute-start | bytes 884744 | tf_op jit(solution)/shard_map/ppermute | solution.py:972
  333.2 9.5 %collective-permute-start.55 = (bf16[2,112,768]{2,1,0:T(8,128)(2,1)S(1)}, bf16[2,112,768]{2,1,0:T(8,128)(2,1)S(1)}, u32[]{:S(2)}, u32[]{:S(2)}) collective-permute-start(bf16[2,112,768]{2,1,0:T(8,128)(2,1)S(1)} %get-tuple-element.374), channel_id=1, source_target_pairs={{0,8},{8,0},{16,24},{24,16},{1,9},{9,1},{17,25},{25,17},{2,10},{10... | collective-permute-start | bytes 1032200 | tf_op jit(solution)/shard_map/ppermute | solution.py:972
  334.5 11.6 %collective-permute-start.54 = (bf16[2,112,768]{2,1,0:T(8,128)(2,1)S(1)}, bf16[2,112,768]{2,1,0:T(8,128)(2,1)S(1)}, u32[]{:S(2)}, u32[]{:S(2)}) collective-permute-start(bf16[2,112,768]{2,1,0:T(8,128)(2,1)S(1)} %get-tuple-element.375), channel_id=1, source_target_pairs={{0,16},{8,24},{16,0},{24,8},{1,17},{9,25},{17,1},{25,9},{2,18},{10... | collective-permute-start | bytes 1032200 | tf_op jit(solution)/shard_map/ppermute | solution.py:972
  348.7 12.8 %collective-permute-start.60 = (bf16[112,768]{1,0:T(8,128)(2,1)S(1)}, bf16[112,768]{1,0:T(8,128)(2,1)S(1)}, u32[]{:S(2)}, u32[]{:S(2)}) collective-permute-start(bf16[112,768]{1,0:T(8,128)(2,1)S(1)} %slice_bitcast_fusion.3), channel_id=1, source_target_pairs={{0,2},{1,3},{2,0},{3,1},{4,6},{5,7},{6,4},{7,5},{8,10},{9,11},{10,... | collective-permute-start | bytes 516104 | tf_op jit(solution)/shard_map/ppermute | solution.py:966
  349.3 12.2 %collective-permute-start.62 = (bf16[112,768]{1,0:T(8,128)(2,1)S(1)}, bf16[112,768]{1,0:T(8,128)(2,1)S(1)}, u32[]{:S(2)}, u32[]{:S(2)}) collective-permute-start(bf16[112,768]{1,0:T(8,128)(2,1)S(1)} %get-tuple-element.394), channel_id=1, source_target_pairs={{0,6},{1,7},{2,4},{3,5},{4,2},{5,3},{6,0},{7,1},{8,14},{9,15},{10,... | collective-permute-start | bytes 516104 | tf_op jit(solution)/shard_map/ppermute | solution.py:966
  350.5 13.7 %collective-permute-start.61 = (bf16[112,768]{1,0:T(8,128)(2,1)S(1)}, bf16[112,768]{1,0:T(8,128)(2,1)S(1)}, u32[]{:S(2)}, u32[]{:S(2)}) collective-permute-start(bf16[112,768]{1,0:T(8,128)(2,1)S(1)} %get-tuple-element.395), channel_id=1, source_target_pairs={{0,4},{1,5},{2,6},{3,7},{4,0},{5,1},{6,2},{7,3},{8,12},{9,13},{10,... | collective-permute-start | bytes 516104 | tf_op jit(solution)/shard_map/ppermute | solution.py:966
  352.3 12.0 %collective-permute-start.63 = (bf16[2,96,768]{2,1,0:T(8,128)(2,1)S(1)}, bf16[2,96,768]{2,1,0:T(8,128)(2,1)S(1)}, u32[]{:S(2)}, u32[]{:S(2)}) collective-permute-start(bf16[2,96,768]{2,1,0:T(8,128)(2,1)S(1)} %pad_maximum_fusion.6), channel_id=1, source_target_pairs={{0,8},{8,0},{16,24},{24,16},{1,9},{9,1},{17,25},{25,17},{2,10},{10... | collective-permute-start | bytes 884744 | tf_op jit(solution)/shard_map/ppermute | solution.py:972
  365.7 17.2 %collective-permute-start.69 = (bf16[2,96,768]{2,1,0:T(8,128)(2,1)}, bf16[2,96,768]{2,1,0:T(8,128)(2,1)S(1)}, u32[]{:S(2)}, u32[]{:S(2)}) collective-permute-start(bf16[2,96,768]{2,1,0:T(8,128)(2,1)} %pad_maximum_fusion.7), channel_id=1, source_target_pairs={{0,16},{8,24},{16,0},{24,8},{1,17},{9,25},{17,1},{25,9},{2,18},{10... | collective-permute-start | bytes 884744 | tf_op jit(solution)/shard_map/ppermute | solution.py:972
  366.8 16.1 %collective-permute-start.68 = (bf16[112,768]{1,0:T(8,128)(2,1)S(1)}, bf16[112,768]{1,0:T(8,128)(2,1)}, u32[]{:S(2)}, u32[]{:S(2)}) collective-permute-start(bf16[112,768]{1,0:T(8,128)(2,1)S(1)} %fusion.2), channel_id=1, source_target_pairs={{0,24},{8,16},{16,8},{24,0},{1,25},{9,17},{17,9},{25,1},{2,26},{10... | collective-permute-start | bytes 516104 | tf_op jit(solution)/shard_map/ppermute | solution.py:972
  368.1 14.8 %collective-permute-start.67 = (bf16[112,768]{1,0:T(8,128)(2,1)S(1)}, bf16[112,768]{1,0:T(8,128)(2,1)}, u32[]{:S(2)}, u32[]{:S(2)}) collective-permute-start(bf16[112,768]{1,0:T(8,128)(2,1)S(1)} %fusion.2), channel_id=1, source_target_pairs={{0,16},{8,24},{16,0},{24,8},{1,17},{9,25},{17,1},{25,9},{2,18},{10... | collective-permute-start | bytes 516104 | tf_op jit(solution)/shard_map/ppermute | solution.py:972
  369.1 13.8 %collective-permute-start.66 = (bf16[112,768]{1,0:T(8,128)(2,1)S(1)}, bf16[112,768]{1,0:T(8,128)(2,1)}, u32[]{:S(2)}, u32[]{:S(2)}) collective-permute-start(bf16[112,768]{1,0:T(8,128)(2,1)S(1)} %fusion.2), channel_id=1, source_target_pairs={{0,8},{8,0},{16,24},{24,16},{1,9},{9,1},{17,25},{25,17},{2,10},{10... | collective-permute-start | bytes 516104 | tf_op jit(solution)/shard_map/ppermute | solution.py:972
  370.4 12.5 %collective-permute-start.70 = (f32[32,768]{1,0:T(8,128)S(1)}, f32[32,768]{1,0:T(8,128)S(1)}, u32[]{:S(2)}, u32[]{:S(2)}) collective-permute-start(f32[32,768]{1,0:T(8,128)S(1)} %add.373), channel_id=1, source_target_pairs={{0,16},{8,24},{16,0},{24,8},{1,17},{9,25},{17,1},{25,9},{2,18},{10... | collective-permute-start | bytes 294920 | tf_op jit(solution)/shard_map/ppermute | solution.py:1103
  (66 other events, 820.7 us)

commit v2 on v1

--- a/solution.py
+++ b/solution.py
@@ -274,6 +274,14 @@
     return 2 * odd + (odd ^ (copy >> 1))
 
 
+def staggered(parts, product, finish):
+    held = product(parts[0])
+    for k, part in enumerate(parts):
+        later = product(parts[k + 1]) if k + 1 < len(parts) else None
+        finish(part, held)
+        held = later
+
+
 def clear(first, *refs):
     @pl.when(first)
     def _():
@@ -374,7 +382,7 @@
         grad_out, mine_out, other_out, vector, low_out, above_grad = rest[2:8]
         layer = 1
     else:
-        earlier, grad_out, mine_out, other_out, vector = rest[2:5], *rest[7:11]
+        earlier, grad_out, mine_out, other_out, vector = rest[2:5], *rest[5:9]
         layer = 0
     padded, w_in_grad, w_out_grad, whole = rest[-4:]
     count, rows = x.shape[:2]
@@ -413,28 +421,14 @@
     @pl.when(image == pl.num_programs(0) - 1)
     def _():
         targets = (mine_out, other_out)
-        if last:
-
-            def put(which, i, side, part):
-                targets[side][which, i] = part
-
-        else:
-
-            def put(which, i, side, part):
-                place_tokens(targets[side], position(which ^ place[2]), i, part)
-
+
+        def put(which, i, side, part):
+            targets[side][i, which] = part
+
+        if not last:
             for side in range(2):
-                for which in range(2):
-                    for i in range(4):
-                        part = earlier[side][which, i]
-                        place_tokens(targets[side], position((2 + which) ^ place[2]), i, part)
+                targets[side][:, 2:] = earlier[side][...]
         token_blocks(place, w_in_grad, w_out_grad, whole, put)
-
-
-def place_tokens(target, j, i, part):
-    rows, wide = target.shape[2], part.shape[1]
-    for k in range(part.shape[0] // rows):
-        target[j, i, :, k * wide : (k + 1) * wide] = part[k * rows : (k + 1) * rows]
 
 
 def out_weight_grad(place, low, hidden, mine_out, other_out, turned, whole):
@@ -525,11 +519,16 @@
     def _():
         j = (step & 3) ^ place[2]
         arrive(w_in, sem_in, j)
-        for part in chunks(v.shape[0], 2):
-            value, slope = gelu_pair(dot(v[part], w_in[j], 1, 0) + bias_in[...])
+        def product(part):
+            return dot(v[part], w_in[j], 1, 0) + bias_in[...]
+
+        def finish(part, found):
+            value, slope = gelu_pair(found)
             hidden_out[0, part] = value
             hidden[j, part] = value
             slope_out[0, part] = slope
+
+        staggered(chunks(v.shape[0], 4), product, finish)
 
     @pl.when(step >= 4)
     def _():
@@ -567,11 +566,16 @@
     def _():
         j = (step & 3) ^ place[2]
         arrive(w_in, sem, j)
-        for part in chunks(v.shape[0], 2):
-            value, slope = gelu_pair(dot(v[part], w_in[j], 1, 0) + bias[...])
+        def product(part):
+            return dot(v[part], w_in[j], 1, 0) + bias[...]
+
+        def finish(part, found):
+            value, slope = gelu_pair(found)
             hidden_out[0, part] = value
             hidden[j, part] = value
             slope_out[0, part] = slope
+
+        staggered(chunks(v.shape[0], 4), product, finish)
 
     @pl.when(step >= 4)
     def _():
@@ -614,12 +618,18 @@
     j = step ^ z
     arrive(w_out, sem_out, j)
     arrive(w_in, sem_in, j)
-    sums = 0.0
-    for part in chunks(low.shape[0], 2):
-        grad = dot(low[part], w_out[j], 1, 1) * slope[0, part].astype(jnp.float32)
-        sums = sums + jnp.sum(grad, 0, keepdims=True)
+    sums = []
+
+    def product(part):
+        return dot(low[part], w_out[j], 1, 1)
+
+    def finish(part, found):
+        grad = found * slope[0, part].astype(jnp.float32)
+        sums.append(jnp.sum(grad, 0, keepdims=True))
         pre[part] = grad.astype(jnp.bfloat16)
-    bias_grad[0] = sums
+
+    staggered(chunks(low.shape[0], 4), product, finish)
+    bias_grad[0] = sum(sums)
     for part in chunks(turned.shape[0], 3):
         whole[part] = dot(turned[part], pre[...], 1, 0).astype(jnp.bfloat16)
     lines = mine.shape[1]
@@ -642,18 +652,12 @@
     out[0] = whole[...].T
 
 
-def finish_in(place, *refs, tokens):
-    parts, out = refs[:4], refs[-2] if tokens else refs[-1]
-    rows = out.shape[1]
+def finish_in(place, *refs):
+    parts, out = refs[:4], refs[-1]
     for j in range(4):
         columns = parts[j].shape[2]
         start = pl.multiple_of((j ^ place[2]) * columns, columns)
-        out[0, :, pl.ds(start, columns)] = parts[j][0, :rows].astype(jnp.float32)
-        if tokens:
-            wide = refs[-1].shape[2]
-            for k in range(columns // wide):
-                part = parts[j][0, rows:, k * wide : (k + 1) * wide]
-                refs[-1][j ^ place[2], 16 * k : 16 * k + 16] = part.astype(jnp.float32)
+        out[0, :, pl.ds(start, columns)] = parts[j][0].astype(jnp.float32)
 
 
 class Kernels:
@@ -825,26 +829,19 @@
             2 * self.product(),
         )
 
-    def token_backward(self, scale, grad, back, kept, small, g_cout, g_cin, keys, earlier=(), blocks=()):
+    def token_backward(self, scale, grad, back, kept, small, g_cout, g_cin, keys, earlier=()):
         bf16, f32 = jnp.bfloat16, jnp.float32
-        rows, width = self.slots * self.rows, self.width
+        width = self.width
         middle, x, u, hidden, slope = kept
         inputs = [self.scalars(scale), self.images(grad)]
         inputs += [(back, (IMAGES * self.rows, width), lambda i, s: (i, 0))]
         inputs += [self.images(a) for a in (middle, x, u, hidden, slope)]
         inputs += [self.fixed(a) for a in tuple(small) + (g_cout, g_cin) + tuple(earlier)]
         outputs = [self.images_out(self.rows, f32)]
-        aliases = None
-        if earlier:
-            aliases = {1 + len(inputs): 1, 2 + len(inputs): 2}
-            inputs += self.in_hbm(blocks)
-            extra = blocks[0].shape[2] - self.block
-            block = (4, self.lines, extra, width)
-            outputs += [(blocks[0].shape, bf16, block, lambda i, s: (0, 0, self.block // extra, 0))] * 2
-            outputs += [self.fixed_out((32, width), f32)]
-        else:
-            outputs += [self.fixed_out((2, self.lines, keys, self.wide), bf16)] * 2
-            outputs += [self.fixed_out((16, width), f32), self.rows_out(), self.fixed_out((1, width), f32)]
+        outputs += [self.fixed_out((self.lines, 4 if earlier else 2, keys, self.wide), bf16)] * 2
+        outputs += [self.fixed_out((32 if earlier else 16, width), f32)]
+        if not earlier:
+            outputs += [self.rows_out(), self.fixed_out((1, width), f32)]
         return self.run(
             token_backward,
             self.slots // IMAGES,
@@ -857,7 +854,6 @@
                 pltpu.VMEM((2, self.inner, self.wide), bf16),
             ],
             4 * self.token_product(),
-            aliases,
         )
 
     def out_weight_grad(self, low, hidden):
@@ -890,11 +886,11 @@
             layer=layer,
         )[0]
 
-    def channel_backward(self, low, v, slope, weights, layer, extra=0):
+    def channel_backward(self, low, v, slope, weights, layer):
         bf16, f32 = jnp.bfloat16, jnp.float32
         rows = self.slots * self.rows
         block = (1, self.lines, self.block, self.width)
-        shape = (4, self.lines, self.block + extra, self.width)
+        shape = (4, self.lines, self.block, self.width)
         blocks = (shape, bf16, block, lambda j, s: (position(j ^ s[0] ^ s[2]), 0, 0, 0))
         return self.run(
             channel_backward,
@@ -938,20 +934,16 @@
             {1 + len(parts): 0} if earlier else None,
         )
 
-    def finish_in(self, parts, layer, layers, keys=0, earlier=()):
+    def finish_in(self, parts, layer, layers, earlier=()):
         shape = (layers, self.block, self.hidden)
-        outputs = [(shape, jnp.float32, (1,) + shape[1:], lambda i, s: (layer, 0, 0))]
-        if keys:
-            outputs.append(self.fixed_out((4, keys, self.wide), jnp.float32))
         return self.run(
             finish_in,
             1,
             self.parts(parts) + self.in_hbm(earlier),
-            outputs,
+            [(shape, jnp.float32, (1,) + shape[1:], lambda i, s: (layer, 0, 0))],
             [],
             0,
             {1 + len(parts): 0} if earlier else None,
-            tokens=bool(keys),
         )
 
 
@@ -1089,6 +1081,27 @@
     def parts(self):
         near, far = (self.near[None], 0), (self.far, 0)
         return [(self.part[None], 0)] + ([near, far] if self.axis == 1 else [far, near]) + [(self.far, 1)]
+
+
+class SumSmall(Held):
+    def __init__(self, moves, mine, other):
+        super().__init__(moves)
+        self.value, self.theirs = mine, other
+
+    def core(self):
+        self.bring(got=self.moves.core(self.theirs))
+
+    def across(self, bits):
+        self.value = self.value + self.got
+        self.bring(got=self.moves.across(self.value, bits))
+
+    def along(self):
+        self.value = self.value + self.got
+        self.bring(**{"z%d" % i: self.moves.along(self.value[i], i) for i in range(1, self.moves.lines)})
+
+    def total(self):
+        parts = [self.value[0]] + [getattr(self, "z%d" % i) for i in range(1, self.moves.lines)]
+        return sum(part.astype(jnp.float32) for part in parts)
 
 
 class SumAll(Held):
@@ -1169,9 +1182,7 @@
     small.line = jnp.stack([small.part, small.z1, small.z2, small.z3])
     small.core("line")
     last.direct()
-    last.fresh = ["z1"]
-    settle((first, small, last))
-    first.second()
+    last.fresh = ["z2"]
     found = kernels.unpack_small(small.line, small.line_core, layers, shards_count, extra)
     x0 = padded(tokens)
     (w_in0, w_in_t0, w_out0, w_out_t0, gain1_0, shift1_0, gain2_0, shift2_0, b_cout0, b_cin0) = found[0]
@@ -1180,11 +1191,14 @@
     u0, h0, d0, mid0, v0 = kernels.token_forward(
         scale, x0, b_outs, (gain1_0, shift1_0, w_in0, w_out_t0, gain2_0, shift2_0), 0
     )
-    last.fresh = ["z2"]
-    (v0,) = settle((first, last), v0)
+    (v0,) = settle((first, small, last), v0)
+
+    first.second()
+    last.fresh = ["z3"]
+    (v0, first.x, first.y) = settle((first, last), v0, first.x, first.y)
     first.core("x", "y")
     first.corner_core()
-    last.fresh = ["z3"]
+    last.fresh = ["z1"]
     (v0,) = settle((first, last), v0)
 
     last.join()
@@ -1225,61 +1239,65 @@
     sum_out0.core()
     sum_in1.second()
     sum_out1.far()
-    *blocks, back, g_cin0 = kernels.channel_backward(low0, v0, slope0, weights(first), 0, 16)
-    *blocks, back = settle((sum_out1, sum_in1, sum_out0), *blocks, back)
-
+    mine, theirs, back, g_cin0 = kernels.channel_backward(low0, v0, slope0, weights(first), 0)
+    mine, theirs, back = settle((sum_out1, sum_in1, sum_out0), mine, theirs, back)
+
+    sum_in0 = Sum(moves, mine, theirs)
+    sum_in0.core()
     sum_out0.first()
     sum_in1.far()
     sum_out1.near()
-    grad0, mine, theirs, vector = kernels.token_backward(
+    grad0, *tokens, vector = kernels.token_backward(
         scale, grad1, back, (mid0, x0, u0, h0, d0), (w_in_t0, w_out0, gain1_0, gain2_0), g_cout0, g_cin0, keys,
-        (*tokens1, vector1), blocks,
-    )
-    hid1, grad0, mine, theirs, vector = settle((sum_out1, sum_in1, sum_out0), hid1, grad0, mine, theirs, vector)
-
-    sum_in0 = Sum(moves, mine, theirs)
-    sum_in0.core()
+        (*tokens1, vector1),
+    )
+    hid1, grad0, *tokens, vector = settle((sum_out1, sum_in1, sum_in0, sum_out0), hid1, grad0, *tokens, vector)
+
+    sum_tokens = SumSmall(moves, *tokens)
+    sum_tokens.core()
+    sum_in0.first()
     sum_out0.second()
-    sum_in1.near()
     vector_sum = SumAll(moves, vector)
     vector_sum.step()
     output = kernels.out_forward(scale, hid1, mid1, b_cout1, weights(last), 1, bf16)
-    (output,) = settle((sum_in0, sum_out0, sum_in1, vector_sum), output)
+    (output,) = settle((sum_in0, sum_out0, sum_tokens, vector_sum), output)
+
+    sum_in0.second()
+    sum_out0.once()
+    sum_in1.near()
+    sum_tokens.across(1)
+    vector_sum.step()
+    share_out1 = Share(moves, sum_out1.total(), 2)
+    share_out1.first()
     output = output[:, :patches]
-    input_grad = grad0[:, :patches]
-
-    sum_in0.first()
-    sum_out0.far()
+    (output,) = settle((sum_in0, sum_out0, sum_in1, sum_tokens, share_out1, vector_sum), output)
+
+    sum_in0.once()
+    sum_tokens.across(2)
     vector_sum.step()
-    share_out1 = Share(moves, sum_out1.total(), 1)
-    share_out1.first()
-    settle((sum_in0, sum_out0, share_out1, vector_sum))
-
-    sum_in0.second()
-    sum_out0.near()
-    vector_sum.step()
-    share_in1 = Share(moves, sum_in1.total(), 2)
+    share_out0, share_in1 = Share(moves, sum_out0.total(), 2), Share(moves, sum_in1.total(), 1)
+    share_out0.first()
     share_in1.first()
     share_out1.second()
-    settle((sum_in0, sum_out0, share_in1, share_out1, vector_sum))
-
-    sum_in0.once()
+    input_grad = grad0[:, :patches]
+    (input_grad,) = settle(
+        (sum_in0, sum_tokens, share_out0, share_in1, share_out1, vector_sum), input_grad
+    )
+
+    total = sum_in0.total()
+    near = [moves.across(total, bits) for bits in (1, 2, 3)]
+    share_out0.second()
     share_in1.second()
-    share_out0 = Share(moves, sum_out0.total(), 1)
-    share_out0.first()
+    sum_tokens.along()
     vector_sum.step()
-    settle((sum_in0, share_in1, share_out0, vector_sum))
-
-    total = sum_in0.total()
+    (done_out,) = kernels.finish_out(share_out1.parts(), 1, layers)
+    done_out, *near = settle((sum_tokens, share_out0, share_in1, vector_sum), done_out, *near)
     vector_sum.step()
-    share_out0.second()
-    near = [moves.across(total, bits) for bits in (1, 2, 3)]
     (done_in,) = kernels.finish_in(share_in1.parts(), 1, layers)
-    (done_out,) = kernels.finish_out(share_out1.parts(), 1, layers)
-    done_in, done_out, *near = settle((share_out0, vector_sum), done_in, done_out, *near)
     (grad_out,) = kernels.finish_out(share_out0.parts(), 0, layers, (done_out,))
     parts = [(part[None], 0) for part in [total] + near]
-    grad_in, near = kernels.finish_in(parts, 0, layers, keys, (done_in,))
+    (grad_in,) = kernels.finish_in(parts, 0, layers, (done_in,))
+    near = sum_tokens.total()
 
     near = near.reshape(layers, 2, keys, wide)
     grad_t_in = jnp.swapaxes(near[:, 0, :, :patches], 1, 2)

time: 402 us -> 405 us (level)
  waiting for transfers between devices: 85.3 us -> 71.3 us
  other arithmetic: 32.8 us -> 39.3 us
  local copies, waits for them, and re-layouts: 33 us -> 38.1 us
  starting transfers between devices: 80.4 us -> 85.2 us
    ppermute x33 -> x35, waiting for transfers between devices: 30.2 us -> 12.4 us  [across(): lax.ppermute(values, 'dp', [(q, q ^ bits) for q in range(self.copies)])]
    unnamed x131 -> x119, local copies, waits for them, and re-layouts: 13.2 us -> 17.6 us
    ppermute x18 -> x22, starting transfers between devices: 34 us -> 38.2 us  [along(): lax.ppermute(values, 'fsdp', [(f, f ^ 2 * bits) for f in range(2 * self.l...]
    ppermute x18 -> x22, waiting for transfers between devices: 48.2 us -> 52.2 us  [along(): lax.ppermute(values, 'fsdp', [(f, f ^ 2 * bits) for f in range(2 * self.l...]
    ppermute x33 -> x35, starting transfers between devices: 38.3 us -> 39.1 us  [across(): lax.ppermute(values, 'dp', [(q, q ^ bits) for q in range(self.copies)])]
  transfers between devices with their start and end apart: 71 -> 78, of which waited for: 20 -> 17; matrix products, arithmetic and copies ran while one was open for 9% -> 13% of each run, Pallas kernels for 34% -> 36%
where the time goes in v2:
time: 405 us; the launch traced here: 401 us
  Pallas kernels  164 us (40%)
  starting transfers between devices  85.2 us (21%)
  waiting for transfers between devices  71.3 us (18%)
  other arithmetic  39.3 us (10%)
  local copies, waits for them, and re-layouts  38.1 us (9%)
    pallas_call x15, Pallas kernels, run(): pl.pallas_call(functools.partial(body, **fixed) if fixed else body, name=...  164 us
    ppermute x22, waiting for transfers between devices, along(): lax.ppermute(values, 'fsdp', [(f, f ^ 2 * bits) for f in range(2 * self.l...  52.2 us
    ppermute x35, starting transfers between devices, across(): lax.ppermute(values, 'dp', [(q, q ^ bits) for q in range(self.copies)])  39.1 us
    ppermute x22, starting transfers between devices, along(): lax.ppermute(values, 'fsdp', [(f, f ^ 2 * bits) for f in range(2 * self.l...  38.2 us
    unnamed x119, local copies, waits for them, and re-layouts  17.6 us
    ppermute x35, waiting for transfers between devices, across(): lax.ppermute(values, 'dp', [(q, q ^ bits) for q in range(self.copies)])  12.4 us
    add x4, other arithmetic, both(): return self.mine[copies, part] + self.got[copies, part]  9.99 us
  transfers between devices with their start and end apart: 78, of which 17 were waited for; matrix products, arithmetic and copies ran while one was open for 13% of the time, Pallas kernels for 36%

profile of v2, /device:TPU:0, one launch (start us, length us, event | category | flops | bytes accessed | tf_op | source)
XLA Modules:
  0.0 400.6 jit_solution(16453206835991195758)
XLA Ops:
  0.7 2.2 fusion.15
  4.6 5.0 %collective-permute-start.2 = (bf16[2,96,768]{2,1,0:T(8,128)(2,1)}, bf16[2,96,768]{2,1,0:T(8,128)(2,1)}, u32[]{:S(2)}, u32[]{:S(2)}) collective-permute-start(bf16[2,96,768]{2,1,0:T(8,128)(2,1)} %pad_maximum_fusion.4), channel_id=1, source_target_pairs={{0,6},{1,7},{2,4},{3,5},{4,2},{5,3},{6,0},{7,1},{8,14},{9,15},{10,... | collective-permute-start | bytes 884744 | tf_op jit(solution)/shard_map/ppermute | solution.py:958
  18.7 16.4 %collective-permute-done.1 = bf16[2,96,768]{2,1,0:T(8,128)(2,1)} collective-permute-done((bf16[2,96,768]{2,1,0:T(8,128)(2,1)}, bf16[2,96,768]{2,1,0:T(8,128)(2,1)}, u32[]{:S(2)}, u32[]{:S(2)}) %collective-permute-start.1) | collective-permute-done | bytes 294944 | tf_op jit(solution)/shard_map/ppermute | solution.py:958
  35.1 1.7 pad_maximum_fusion.rest_4_
  36.8 2.5 collective-permute-start.8
  39.4 1.9 collective-permute-start.6
  41.3 1.5 collective-permute-start.11
  42.8 2.7 collective-permute-done.8
  45.5 1.5 collective-permute-start.10
  47.0 4.7 %collective-permute-done.7 = bf16[96,768]{1,0:T(8,128)(2,1)S(1)} collective-permute-done((bf16[96,768]{1,0:T(8,128)(2,1)S(1)}, bf16[96,768]{1,0:T(8,128)(2,1)S(1)}, u32[]{:S(2)}, u32[]{:S(2)}) %collective-permute-start.7) | collective-permute-done | bytes 147488 | tf_op jit(solution)/shard_map/ppermute | solution.py:958
  59.3 3.2 unpack_small.1
  62.5 9.4 %token_forward.2 = (bf16[4,256,768]{2,1,0:T(8,128)(2,1)}, bf16[4,384,768]{2,1,0:T(8,128)(2,1)}, bf16[4,384,768]{2,1,0:T(8,128)(2,1)}, f32[4,208,768]{2,1,0:T(8,128)}, bf16[832,768]{1,0:T(8,128)(2,1)}) custom-call(s32[3]{0:T(128)} %pad_add_fusion.place, f32[4,4]{1,0:T(4,128)} %copy.65.scale, bf16[4,208,768]{2,1,0:T(8,128)(2,1)} %pad.36.x, ...), custom_call_target="tpu_custom_call" | custom-call | flops 1207959552 | bytes 11810880 | tf_op jit(solution)/shard_map/token_forward/pallas_call | solution.py:681
  74.2 1.6 collective-permute-start.13
  75.7 1.5 collective-permute-start.14
  77.3 2.5 collective-permute-start.15
  79.7 8.0 %collective-permute-done.15 = bf16[2,96,768]{2,1,0:T(8,128)(2,1)S(1)} collective-permute-done((bf16[2,96,768]{2,1,0:T(8,128)(2,1)S(1)}, bf16[2,96,768]{2,1,0:T(8,128)(2,1)S(1)}, u32[]{:S(2)}, u32[]{:S(2)}) %collective-permute-start.15) | collective-permute-done | bytes 294944 | tf_op jit(solution)/shard_map/ppermute | solution.py:958
  88.5 6.8 %collective-permute-start.19 = (bf16[2,96,768]{2,1,0:T(8,128)(2,1)S(1)}, bf16[2,96,768]{2,1,0:T(8,128)(2,1)S(1)}, u32[]{:S(2)}, u32[]{:S(2)}) collective-permute-start(bf16[2,96,768]{2,1,0:T(8,128)(2,1)S(1)} %copy-done.38), channel_id=1, source_target_pairs={{0,2},{1,3},{2,0},{3,1},{4,6},{5,7},{6,4},{7,5},{8,10},{9,11},{10,... | collective-permute-start | bytes 884744 | tf_op jit(solution)/shard_map/ppermute | solution.py:958
  95.3 7.6 %collective-permute-done.19 = bf16[2,96,768]{2,1,0:T(8,128)(2,1)S(1)} collective-permute-done((bf16[2,96,768]{2,1,0:T(8,128)(2,1)S(1)}, bf16[2,96,768]{2,1,0:T(8,128)(2,1)S(1)}, u32[]{:S(2)}, u32[]{:S(2)}) %collective-permute-start.19) | collective-permute-done | bytes 294944 | tf_op jit(solution)/shard_map/ppermute | solution.py:958
  106.6 20.0 %first_forward.1 = (bf16[4,832,768]{2,1,0:T(8,128)(2,1)}, bf16[4,832,768]{2,1,0:T(8,128)(2,1)}, f32[4,208,768]{2,1,0:T(8,128)}) custom-call(s32[3]{0:T(128)} %pad_add_fusion.place, f32[4,4]{1,0:T(4,128)} %copy.65.scale, bf16[832,768]{1,0:T(8,128)(2,1)} %get-tuple-element.210.v, f32[4,208,768]{2,1,0:T(8,128)} %get-tuple-element.211.middle, ...), custom_call_target="tpu_custom_call" | custom-call | flops 7851737088 | bytes 28425280 | tf_op jit(solution)/shard_map/first_forward/pallas_call | solution.py:681
  129.3 1.5 collective-permute-start.23
  131.8 9.3 %token_forward.3 = (bf16[4,256,768]{2,1,0:T(8,128)(2,1)}, bf16[4,384,768]{2,1,0:T(8,128)(2,1)}, bf16[4,384,768]{2,1,0:T(8,128)(2,1)}, f32[4,208,768]{2,1,0:T(8,128)}, bf16[832,768]{1,0:T(8,128)(2,1)}) custom-call(s32[3]{0:T(128)} %pad_add_fusion.place, f32[4,4]{1,0:T(4,128)} %copy.65.scale, f32[4,208,768]{2,1,0:T(8,128)} %get-tuple-element.225.x, ...), custom_call_target="tpu_custom_call" | custom-call | flops 1207959552 | bytes 13088832 | tf_op jit(solution)/shard_map/token_forward/pallas_call | solution.py:681
  148.5 20.6 %last_hidden.1 = (bf16[4,832,768]{2,1,0:T(8,128)(2,1)}, bf16[4,832,768]{2,1,0:T(8,128)(2,1)}, bf16[4,4,96,768]{3,2,1,0:T(8,128)(2,1)}, bf16[4,4,96,768]{3,2,1,0:...) custom-call(s32[3]{0:T(128)} %pad_add_fusion.place, f32[4,4]{1,0:T(4,128)} %copy.65.scale, ...), custom_call_target="tpu_custom_call" | custom-call | flops 7851737088 | bytes 30587968 | tf_op jit(solution)/shard_map/last_hidden/pallas_call | solution.py:681
  169.3 21.7 %channel_backward.2 = (bf16[4,4,96,768]{3,2,1,0:T(8,128)(2,1)}, bf16[4,4,96,768]{3,2,1,0:T(8,128)(2,1)}, f32[832,768]{1,0:T(8,128)}, f32[4,1,768]{2,1,0:T(1,128)}) custom-call(s32[3]{0:T(128)} %pad_add_fusion.place, bf16[832,768]{1,0:T(8,128)(2,1)} %get-tuple-element.246.low, bf16[832,768]{1,0:T(8,128)(2,1)} %get-tuple-element.235.v, ...), custom_call_target="tpu_custom_call" | custom-call | flops 11777605632 | bytes 26750976 | tf_op jit(solution)/shard_map/channel_backward/pallas_call | solution.py:681
  191.5 2.2 slice_add_fusion.6
  193.7 1.8 collective-permute-start.30
  195.5 2.0 collective-permute-start.29
  197.5 12.5 %token_backward.2 = (f32[4,208,768]{2,1,0:T(8,128)}, bf16[4,2,48,256]{3,2,1,0:T(8,128)(2,1)}, bf16[4,2,48,256]{3,2,1,0:T(8,128)(2,1)}, f32[16,768]{1,0:T(8,128)}...) custom-call(s32[3]{0:T(128)} %pad_add_fusion.place, f32[4,4]{1,0:T(4,128)} %copy.65.scale, bf16[4,208,768]{2,1,0:T(8,128)(2,1)} %pad.44.grad, ...), custom_call_target="tpu_custom_call" | custom-call | flops 2415919104 | bytes 19931200 | tf_op jit(solution)/shard_map/token_backward/pallas_call | solution.py:681
  210.9 2.6 slice_add_fusion.4
  213.9 2.0 collective-permute-start.34
  215.9 2.2 add_bitcast_fusion.6
  218.2 1.6 collective-permute-start.32
  219.8 10.5 %out_weight_grad.1 = (bf16[4,4,96,768]{3,2,1,0:T(8,128)(2,1)}, bf16[4,4,96,768]{3,2,1,0:T(8,128)(2,1)}) custom-call(s32[3]{0:T(128)} %pad_add_fusion.place, bf16[832,768]{1,0:T(8,128)(2,1)} %get-tuple-element.272.low, bf16[4,832,768]{2,1,0:T(8,128)(2,1)} %get-tuple-element.278.hidden), custom_call_target="tpu_custom_call" | custom-call | flops 3925868544 | bytes 11108352 | tf_op jit(solution)/shard_map/out_weight_grad/pallas_call | solution.py:681
  230.2 4.8 %collective-permute-done.33 = bf16[2,96,768]{2,1,0:T(8,128)(2,1)} collective-permute-done((bf16[2,96,768]{2,1,0:T(8,128)(2,1)}, bf16[2,96,768]{2,1,0:T(8,128)(2,1)}, u32[]{:S(2)}, u32[]{:S(2)}) %collective-permute-start.33) | collective-permute-done | bytes 294944 | tf_op jit(solution)/shard_map/ppermute | solution.py:964
  235.2 2.1 bitcast_add_fusion.7
  237.2 2.9 collective-permute-start.36
  241.3 1.5 collective-permute-start.38
  243.8 21.6 %channel_backward.3 = (bf16[4,4,96,768]{3,2,1,0:T(8,128)(2,1)}, bf16[4,4,96,768]{3,2,1,0:T(8,128)(2,1)}, f32[832,768]{1,0:T(8,128)}, f32[4,1,768]{2,1,0:T(1,128)}) custom-call(s32[3]{0:T(128)} %pad_add_fusion.place, bf16[832,768]{1,0:T(8,128)(2,1)} %get-tuple-element.272.low, bf16[832,768]{1,0:T(8,128)(2,1)} %get-tuple-element.210.v, ...), custom_call_target="tpu_custom_call" | custom-call | flops 11777605632 | bytes 26750976 | tf_op jit(solution)/shard_map/channel_backward/pallas_call | solution.py:681
  265.6 1.9 bitcast_add_fusion.5
  267.5 1.7 collective-permute-start.41
  269.1 2.8 slice_add_fusion.2
  276.4 12.2 %token_backward.3 = (f32[4,208,768]{2,1,0:T(8,128)}, bf16[4,4,48,256]{3,2,1,0:T(8,128)(2,1)}, bf16[4,4,48,256]{3,2,1,0:T(8,128)(2,1)}, f32[32,768]{1,0:T(8,128)}) custom-call(s32[3]{0:T(128)} %pad_add_fusion.place, f32[4,4]{1,0:T(4,128)} %copy.65.scale, f32[4,208,768]{2,1,0:T(8,128)} %get-tuple-element.271.grad, f32[832,768]{1,0:T(8,128)} %get-tuple-element.288.back_v, ...), custom_call_target="tpu_custom_call" | custom-call | flops 2415919104 | bytes 19534912 | tf_op jit(solution)/shard_map/token_backward/pallas_call | solution.py:681
  289.2 2.7 add_bitcast_fusion.2
  293.3 2.4 slice_add_fusion
  295.7 2.0 collective-permute-start.46
  298.4 10.6 %out_forward.1 = bf16[4,208,768]{2,1,0:T(8,128)(2,1)} custom-call(s32[3]{0:T(128)} %pad_add_fusion.place, f32[4,4]{1,0:T(4,128)} %copy.65.scale, bf16[4,832,768]{2,1,0:T(8,128)(2,1)} %get-tuple-element.309.hidden, f32[4,208,768]{2,1,0:T(8,128)} %get-tuple-element.254.middle, f32[1,768]{1,0:T(1,128)} %get-tuple-element.310.bias, ...), custom_call_target="tpu_custom_call" | custom-call | flops 3925868544 | bytes 20745280 | tf_op jit(solution)/shard_map/out_forward/pallas_call | solution.py:681
  312.7 1.5 collective-permute-start.56
  314.2 4.2 %collective-permute-done.47 = bf16[2,96,768]{2,1,0:T(8,128)(2,1)S(1)} collective-permute-done((bf16[2,96,768]{2,1,0:T(8,128)(2,1)}, bf16[2,96,768]{2,1,0:T(8,128)(2,1)S(1)}, u32[]{:S(2)}, u32[]{:S(2)}) %collective-permute-start.47) | collective-permute-done | bytes 294944 | tf_op jit(solution)/shard_map/ppermute | solution.py:964
  326.8 1.7 collective-permute-start.51
  328.5 2.3 collective-permute-start.55
  332.0 3.6 collective-permute-done.55
  335.6 4.5 %collective-permute-done.54 = bf16[96,768]{1,0:T(8,128)(2,1)S(1)} collective-permute-done((bf16[96,768]{1,0:T(8,128)(2,1)S(1)}, bf16[96,768]{1,0:T(8,128)(2,1)S(1)}, u32[]{:S(2)}, u32[]{:S(2)}) %collective-permute-start.54) | collective-permute-done | bytes 147488 | tf_op jit(solution)/shard_map/ppermute | solution.py:958
  341.8 3.0 collective-permute-start.60
  344.8 1.4 collective-permute-start.62
  348.4 5.5 %collective-permute-done.67 = f32[32,768]{1,0:T(8,128)S(1)} collective-permute-done((f32[32,768]{1,0:T(8,128)S(1)}, f32[32,768]{1,0:T(8,128)S(1)}, u32[]{:S(2)}, u32[]{:S(2)}) %collective-permute-start.67) | collective-permute-done | bytes 98336 | tf_op jit(solution)/shard_map/ppermute | solution.py:1116
  356.2 4.7 %collective-permute-done.61 = bf16[96,768]{1,0:T(8,128)(2,1)S(1)} collective-permute-done((bf16[96,768]{1,0:T(8,128)(2,1)S(1)}, bf16[96,768]{1,0:T(8,128)(2,1)S(1)}, u32[]{:S(2)}, u32[]{:S(2)}) %collective-permute-start.61) | collective-permute-done | bytes 147488 | tf_op jit(solution)/shard_map/ppermute | solution.py:958
  363.7 2.1 collective-permute-start.72
  370.4 2.3 collective-permute-start.70
  373.9 2.8 copy.70
  376.7 2.4 copy.71
  379.0 3.4 finish_out.2.refs_4_
  382.5 1.9 collective-permute-start.77
  386.8 2.9 finish_in.2.refs_4_
  389.7 3.2 finish_out.3
  393.0 2.9 finish_in.3
  (307 shorter events, 81.3 us)
Async XLA Ops:
  4.6 14.1 %collective-permute-start.2 = (bf16[2,96,768]{2,1,0:T(8,128)(2,1)}, bf16[2,96,768]{2,1,0:T(8,128)(2,1)}, u32[]{:S(2)}, u32[]{:S(2)}) collective-permute-start(bf16[2,96,768]{2,1,0:T(8,128)(2,1)} %pad_maximum_fusion.4), channel_id=1, source_target_pairs={{0,6},{1,7},{2,4},{3,5},{4,2},{5,3},{6,0},{7,1},{8,14},{9,15},{10,... | collective-permute-start | bytes 884744 | tf_op jit(solution)/shard_map/ppermute | solution.py:958
  9.6 25.4 %collective-permute-start.1 = (bf16[2,96,768]{2,1,0:T(8,128)(2,1)}, bf16[2,96,768]{2,1,0:T(8,128)(2,1)}, u32[]{:S(2)}, u32[]{:S(2)}) collective-permute-start(bf16[2,96,768]{2,1,0:T(8,128)(2,1)} %pad_maximum_fusion.4), channel_id=1, source_target_pairs={{0,4},{1,5},{2,6},{3,7},{4,0},{5,1},{6,2},{7,3},{8,12},{9,13},{10,... | collective-permute-start | bytes 884744 | tf_op jit(solution)/shard_map/ppermute | solution.py:958
  9.6 25.4 %collective-permute-start = (bf16[2,96,768]{2,1,0:T(8,128)(2,1)}, bf16[2,96,768]{2,1,0:T(8,128)(2,1)}, u32[]{:S(2)}, u32[]{:S(2)}) collective-permute-start(bf16[2,96,768]{2,1,0:T(8,128)(2,1)} %pad_maximum_fusion.4), channel_id=1, source_target_pairs={{0,2},{1,3},{2,0},{3,1},{4,6},{5,7},{6,4},{7,5},{8,10},{9,11},{10,... | collective-permute-start | bytes 884744 | tf_op jit(solution)/shard_map/ppermute | solution.py:958
  10.2 24.9 %collective-permute-start.3 = (bf16[2,96,3072]{2,1,0:T(8,128)(2,1)S(1)}, bf16[2,96,3072]{2,1,0:T(8,128)(2,1)S(1)}, u32[]{:S(2)}, u32[]{:S(2)}) collective-permute-start(bf16[2,96,3072]{2,1,0:T(8,128)(2,1)S(1)} %copy-done.1), channel_id=1, source_target_pairs={{0,1},{1,0},{2,3},{3,2},{4,5},{5,4},{6,7},{7,6},{8,9},{9,8},{10,11... | collective-permute-start | bytes 3538952 | tf_op jit(solution)/shard_map/ppermute | solution.py:961
  10.2 24.9 %collective-permute-start.4 = (bf16[2,384,768]{2,1,0:T(8,128)(2,1)S(1)}, bf16[2,384,768]{2,1,0:T(8,128)(2,1)}, u32[]{:S(2)}, u32[]{:S(2)}) collective-permute-start(bf16[2,384,768]{2,1,0:T(8,128)(2,1)S(1)} %copy-done.2), channel_id=1, source_target_pairs={{0,1},{1,0},{2,3},{3,2},{4,5},{5,4},{6,7},{7,6},{8,9},{9,8},{10,11... | collective-permute-start | bytes 3538952 | tf_op jit(solution)/shard_map/ppermute | solution.py:961
  36.8 14.9 %collective-permute-start.5 = (bf16[3,2,96,768]{3,2,1,0:T(8,128)(2,1)S(1)}, bf16[3,2,96,768]{3,2,1,0:T(8,128)(2,1)S(1)}, u32[]{:S(2)}, u32[]{:S(2)}) collective-permute-start(bf16[3,2,96,768]{3,2,1,0:T(8,128)(2,1)S(1)} %pad_maximum_fusion.rest_4_), channel_id=1, source_target_pairs={{0,1},{1,0},{2,3},{3,2},{4,5},{5,4},{6,7},{7,6},{8,9},{9,8},{10,11... | collective-permute-start | bytes 2654216 | tf_op jit(solution)/shard_map/ppermute | solution.py:961
  39.4 12.3 %collective-permute-start.7 = (bf16[96,768]{1,0:T(8,128)(2,1)S(1)}, bf16[96,768]{1,0:T(8,128)(2,1)S(1)}, u32[]{:S(2)}, u32[]{:S(2)}) collective-permute-start(bf16[96,768]{1,0:T(8,128)(2,1)S(1)} %bitcast.161), channel_id=1, source_target_pairs={{0,4},{1,5},{2,6},{3,7},{4,0},{5,1},{6,2},{7,3},{8,12},{9,13},{10,... | collective-permute-start | bytes 442376 | tf_op jit(solution)/shard_map/ppermute | solution.py:958
  39.4 12.3 %collective-permute-start.6 = (bf16[96,768]{1,0:T(8,128)(2,1)S(1)}, bf16[96,768]{1,0:T(8,128)(2,1)S(1)}, u32[]{:S(2)}, u32[]{:S(2)}) collective-permute-start(bf16[96,768]{1,0:T(8,128)(2,1)S(1)} %bitcast.162), channel_id=1, source_target_pairs={{0,2},{1,3},{2,0},{3,1},{4,6},{5,7},{6,4},{7,5},{8,10},{9,11},{10,... | collective-permute-start | bytes 442376 | tf_op jit(solution)/shard_map/ppermute | solution.py:958
  41.3 30.6 %collective-permute-start.11 = (bf16[3,2,96,768]{3,2,1,0:T(8,128)(2,1)S(1)}, bf16[3,2,96,768]{3,2,1,0:T(8,128)(2,1)}, u32[]{:S(2)}, u32[]{:S(2)}) collective-permute-start(bf16[3,2,96,768]{3,2,1,0:T(8,128)(2,1)S(1)} %pad_maximum_fusion.rest_4_), channel_id=1, source_target_pairs={{0,16},{8,24},{16,0},{24,8},{1,17},{9,25},{17,1},{25,9},{2,18},{10... | collective-permute-start | bytes 2654216 | tf_op jit(solution)/shard_map/ppermute | solution.py:964
  45.5 26.5 %collective-permute-start.10 = (bf16[3,2,96,768]{3,2,1,0:T(8,128)(2,1)S(1)}, bf16[3,2,96,768]{3,2,1,0:T(8,128)(2,1)}, u32[]{:S(2)}, u32[]{:S(2)}) collective-permute-start(bf16[3,2,96,768]{3,2,1,0:T(8,128)(2,1)S(1)} %pad_maximum_fusion.rest_4_), channel_id=1, source_target_pairs={{0,8},{8,0},{16,24},{24,16},{1,9},{9,1},{17,25},{25,17},{2,10},{10... | collective-permute-start | bytes 2654216 | tf_op jit(solution)/shard_map/ppermute | solution.py:964
  54.2 17.8 %collective-permute-start.12 = (bf16[2,96,768]{2,1,0:T(8,128)(2,1)}, bf16[2,96,768]{2,1,0:T(8,128)(2,1)S(1)}, u32[]{:S(2)}, u32[]{:S(2)}) collective-permute-start(bf16[2,96,768]{2,1,0:T(8,128)(2,1)} %pad_maximum_fusion.3), channel_id=1, source_target_pairs={{0,4},{1,5},{2,6},{3,7},{4,0},{5,1},{6,2},{7,3},{8,12},{9,13},{10,... | collective-permute-start | bytes 884744 | tf_op jit(solution)/shard_map/ppermute | solution.py:958
  74.2 13.6 %collective-permute-start.13 = (bf16[3,1,96,768]{3,2,1,0:T(8,128)(2,1)S(1)}, bf16[3,1,96,768]{3,2,1,0:T(8,128)(2,1)S(1)}, u32[]{:S(2)}, u32[]{:S(2)}) collective-permute-start(bf16[3,1,96,768]{3,2,1,0:T(8,128)(2,1)S(1)} %slice.301), channel_id=1, source_target_pairs={{0,8},{8,0},{16,24},{24,16},{1,9},{9,1},{17,25},{25,17},{2,10},{10... | collective-permute-start | bytes 1327112 | tf_op jit(solution)/shard_map/ppermute | solution.py:964
  75.7 12.0 %collective-permute-start.14 = (bf16[3,1,96,768]{3,2,1,0:T(8,128)(2,1)S(1)}, bf16[3,1,96,768]{3,2,1,0:T(8,128)(2,1)S(1)}, u32[]{:S(2)}, u32[]{:S(2)}) collective-permute-start(bf16[3,1,96,768]{3,2,1,0:T(8,128)(2,1)S(1)} %slice.302), channel_id=1, source_target_pairs={{0,16},{8,24},{16,0},{24,8},{1,17},{9,25},{17,1},{25,9},{2,18},{10... | collective-permute-start | bytes 1327112 | tf_op jit(solution)/shard_map/ppermute | solution.py:964
  77.3 10.5 %collective-permute-start.15 = (bf16[2,96,768]{2,1,0:T(8,128)(2,1)S(1)}, bf16[2,96,768]{2,1,0:T(8,128)(2,1)S(1)}, u32[]{:S(2)}, u32[]{:S(2)}) collective-permute-start(bf16[2,96,768]{2,1,0:T(8,128)(2,1)S(1)} %copy-done.38), channel_id=1, source_target_pairs={{0,6},{1,7},{2,4},{3,5},{4,2},{5,3},{6,0},{7,1},{8,14},{9,15},{10,... | collective-permute-start | bytes 884744 | tf_op jit(solution)/shard_map/ppermute | solution.py:958
  87.9 15.0 %collective-permute-start.18 = (bf16[3,2,96,768]{3,2,1,0:T(8,128)(2,1)S(1)}, bf16[3,2,96,768]{3,2,1,0:T(8,128)(2,1)S(1)}, u32[]{:S(2)}, u32[]{:S(2)}) collective-permute-start(bf16[3,2,96,768]{3,2,1,0:T(8,128)(2,1)S(1)} %constant_dynamic-update-slice_fusion.5.rest_7_), channel_id=1, source_target_pairs={{0,1},{1,0},{2,3},{3,2},{4,5},{5,4},{6,7},{7,6},{8,9},{9,8},{10,11... | collective-permute-start | bytes 2654216 | tf_op jit(solution)/shard_map/ppermute | solution.py:961
  88.0 15.0 %collective-permute-start.16 = (bf16[3,2,96,768]{3,2,1,0:T(8,128)(2,1)}, bf16[3,2,96,768]{3,2,1,0:T(8,128)(2,1)S(1)}, u32[]{:S(2)}, u32[]{:S(2)}) collective-permute-start(bf16[3,2,96,768]{3,2,1,0:T(8,128)(2,1)} %collective-permute-done.10.rest_5_), channel_id=1, source_target_pairs={{0,1},{1,0},{2,3},{3,2},{4,5},{5,4},{6,7},{7,6},{8,9},{9,8},{10,11... | collective-permute-start | bytes 2654216 | tf_op jit(solution)/shard_map/ppermute | solution.py:961
  88.5 14.5 %collective-permute-start.17 = (bf16[3,2,96,768]{3,2,1,0:T(8,128)(2,1)}, bf16[3,2,96,768]{3,2,1,0:T(8,128)(2,1)S(1)}, u32[]{:S(2)}, u32[]{:S(2)}) collective-permute-start(bf16[3,2,96,768]{3,2,1,0:T(8,128)(2,1)} %collective-permute-done.11.rest_6_), channel_id=1, source_target_pairs={{0,1},{1,0},{2,3},{3,2},{4,5},{5,4},{6,7},{7,6},{8,9},{9,8},{10,11... | collective-permute-start | bytes 2654216 | tf_op jit(solution)/shard_map/ppermute | solution.py:961
  88.5 14.4 %collective-permute-start.19 = (bf16[2,96,768]{2,1,0:T(8,128)(2,1)S(1)}, bf16[2,96,768]{2,1,0:T(8,128)(2,1)S(1)}, u32[]{:S(2)}, u32[]{:S(2)}) collective-permute-start(bf16[2,96,768]{2,1,0:T(8,128)(2,1)S(1)} %copy-done.38), channel_id=1, source_target_pairs={{0,2},{1,3},{2,0},{3,1},{4,6},{5,7},{6,4},{7,5},{8,10},{9,11},{10,... | collective-permute-start | bytes 884744 | tf_op jit(solution)/shard_map/ppermute | solution.py:958
  105.5 21.5 %collective-permute-start.21 = (bf16[3,2,96,768]{3,2,1,0:T(8,128)(2,1)S(1)}, bf16[3,2,96,768]{3,2,1,0:T(8,128)(2,1)S(1)}, u32[]{:S(2)}, u32[]{:S(2)}) collective-permute-start(bf16[3,2,96,768]{3,2,1,0:T(8,128)(2,1)S(1)} %pad_maximum_fusion.1.rest_4_), channel_id=1, source_target_pairs={{0,16},{8,24},{16,0},{24,8},{1,17},{9,25},{17,1},{25,9},{2,18},{10... | collective-permute-start | bytes 2654216 | tf_op jit(solution)/shard_map/ppermute | solution.py:964
  106.1 21.1 %collective-permute-start.20 = (bf16[3,2,96,768]{3,2,1,0:T(8,128)(2,1)S(1)}, bf16[3,2,96,768]{3,2,1,0:T(8,128)(2,1)S(1)}, u32[]{:S(2)}, u32[]{:S(2)}) collective-permute-start(bf16[3,2,96,768]{3,2,1,0:T(8,128)(2,1)S(1)} %pad_maximum_fusion.1.rest_4_), channel_id=1, source_target_pairs={{0,8},{8,0},{16,24},{24,16},{1,9},{9,1},{17,25},{25,17},{2,10},{10... | collective-permute-start | bytes 2654216 | tf_op jit(solution)/shard_map/ppermute | solution.py:964
  106.6 34.5 %collective-permute-start.24 = (bf16[3,2,96,768]{3,2,1,0:T(8,128)(2,1)S(1)}, bf16[3,2,96,768]{3,2,1,0:T(8,128)(2,1)}, u32[]{:S(2)}, u32[]{:S(2)}) collective-permute-start(bf16[3,2,96,768]{3,2,1,0:T(8,128)(2,1)S(1)} %pad_maximum_fusion.1.rest_4_), channel_id=1, source_target_pairs={{0,1},{1,0},{2,3},{3,2},{4,5},{5,4},{6,7},{7,6},{8,9},{9,8},{10,11... | collective-permute-start | bytes 2654216 | tf_op jit(solution)/shard_map/ppermute | solution.py:961
  127.2 15.8 %collective-permute-start.26 = (bf16[3,2,96,768]{3,2,1,0:T(8,128)(2,1)S(1)}, bf16[3,2,96,768]{3,2,1,0:T(8,128)(2,1)}, u32[]{:S(2)}, u32[]{:S(2)}) collective-permute-start(bf16[3,2,96,768]{3,2,1,0:T(8,128)(2,1)S(1)} %collective-permute-done.21.rest_6_), channel_id=1, source_target_pairs={{0,1},{1,0},{2,3},{3,2},{4,5},{5,4},{6,7},{7,6},{8,9},{9,8},{10,11... | collective-permute-start | bytes 2654216 | tf_op jit(solution)/shard_map/ppermute | solution.py:961
  127.2 15.8 %collective-permute-start.25 = (bf16[3,2,96,768]{3,2,1,0:T(8,128)(2,1)S(1)}, bf16[3,2,96,768]{3,2,1,0:T(8,128)(2,1)}, u32[]{:S(2)}, u32[]{:S(2)}) collective-permute-start(bf16[3,2,96,768]{3,2,1,0:T(8,128)(2,1)S(1)} %collective-permute-done.20.rest_5_), channel_id=1, source_target_pairs={{0,1},{1,0},{2,3},{3,2},{4,5},{5,4},{6,7},{7,6},{8,9},{9,8},{10,11... | collective-permute-start | bytes 2654216 | tf_op jit(solution)/shard_map/ppermute | solution.py:961
  129.3 12.4 %collective-permute-start.23 = (bf16[3,1,96,768]{3,2,1,0:T(8,128)(2,1)}, bf16[3,1,96,768]{3,2,1,0:T(8,128)(2,1)}, u32[]{:S(2)}, u32[]{:S(2)}) collective-permute-start(bf16[3,1,96,768]{3,2,1,0:T(8,128)(2,1)} %slice.304), channel_id=1, source_target_pairs={{0,16},{8,24},{16,0},{24,8},{1,17},{9,25},{17,1},{25,9},{2,18},{10... | collective-permute-start | bytes 1327112 | tf_op jit(solution)/shard_map/ppermute | solution.py:964
  130.9 12.1 %collective-permute-start.22 = (bf16[3,1,96,768]{3,2,1,0:T(8,128)(2,1)}, bf16[3,1,96,768]{3,2,1,0:T(8,128)(2,1)}, u32[]{:S(2)}, u32[]{:S(2)}) collective-permute-start(bf16[3,1,96,768]{3,2,1,0:T(8,128)(2,1)} %slice.303), channel_id=1, source_target_pairs={{0,8},{8,0},{16,24},{24,16},{1,9},{9,1},{17,25},{25,17},{2,10},{10... | collective-permute-start | bytes 1327112 | tf_op jit(solution)/shard_map/ppermute | solution.py:964
  169.1 21.9 %collective-permute-start.28 = (bf16[4,4,96,768]{3,2,1,0:T(8,128)(2,1)}, bf16[4,4,96,768]{3,2,1,0:T(8,128)(2,1)}, u32[]{:S(2)}, u32[]{:S(2)}) collective-permute-start(bf16[4,4,96,768]{3,2,1,0:T(8,128)(2,1)} %get-tuple-element.252), channel_id=1, source_target_pairs={{0,1},{1,0},{2,3},{3,2},{4,5},{5,4},{6,7},{7,6},{8,9},{9,8},{10,11... | collective-permute-start | bytes 7077896 | tf_op jit(solution)/shard_map/ppermute | solution.py:961
  191.0 19.8 %collective-permute-start.31 = (bf16[4,4,96,768]{3,2,1,0:T(8,128)(2,1)}, bf16[4,4,96,768]{3,2,1,0:T(8,128)(2,1)}, u32[]{:S(2)}, u32[]{:S(2)}) collective-permute-start(bf16[4,4,96,768]{3,2,1,0:T(8,128)(2,1)} %get-tuple-element.270), channel_id=1, source_target_pairs={{0,1},{1,0},{2,3},{3,2},{4,5},{5,4},{6,7},{7,6},{8,9},{9,8},{10,11... | collective-permute-start | bytes 7077896 | tf_op jit(solution)/shard_map/ppermute | solution.py:961
  193.7 16.4 %collective-permute-start.30 = (bf16[2,2,96,768]{3,2,1,0:T(8,128)(2,1)}, bf16[2,2,96,768]{3,2,1,0:T(8,128)(2,1)S(1)}, u32[]{:S(2)}, u32[]{:S(2)}) collective-permute-start(bf16[2,2,96,768]{3,2,1,0:T(8,128)(2,1)} %get-tuple-element.404), channel_id=1, source_target_pairs={{0,16},{8,24},{16,0},{24,8},{1,17},{9,25},{17,1},{25,9},{2,18},{10... | collective-permute-start | bytes 1769480 | tf_op jit(solution)/shard_map/ppermute | solution.py:964
  195.5 15.4 %collective-permute-start.29 = (bf16[2,2,96,768]{3,2,1,0:T(8,128)(2,1)S(1)}, bf16[2,2,96,768]{3,2,1,0:T(8,128)(2,1)S(1)}, u32[]{:S(2)}, u32[]{:S(2)}) collective-permute-start(bf16[2,2,96,768]{3,2,1,0:T(8,128)(2,1)S(1)} %get-tuple-element.405), channel_id=1, source_target_pairs={{0,8},{8,0},{16,24},{24,16},{1,9},{9,1},{17,25},{25,17},{2,10},{10... | collective-permute-start | bytes 1769480 | tf_op jit(solution)/shard_map/ppermute | solution.py:964
  213.5 21.6 %collective-permute-start.35 = (bf16[2,2,96,768]{3,2,1,0:T(8,128)(2,1)}, bf16[2,2,96,768]{3,2,1,0:T(8,128)(2,1)S(1)}, u32[]{:S(2)}, u32[]{:S(2)}) collective-permute-start(bf16[2,2,96,768]{3,2,1,0:T(8,128)(2,1)} %get-tuple-element.400), channel_id=1, source_target_pairs={{0,16},{8,24},{16,0},{24,8},{1,17},{9,25},{17,1},{25,9},{2,18},{10... | collective-permute-start | bytes 1769480 | tf_op jit(solution)/shard_map/ppermute | solution.py:964
  213.9 21.1 %collective-permute-start.34 = (bf16[2,2,96,768]{3,2,1,0:T(8,128)(2,1)}, bf16[2,2,96,768]{3,2,1,0:T(8,128)(2,1)S(1)}, u32[]{:S(2)}, u32[]{:S(2)}) collective-permute-start(bf16[2,2,96,768]{3,2,1,0:T(8,128)(2,1)} %get-tuple-element.401), channel_id=1, source_target_pairs={{0,8},{8,0},{16,24},{24,16},{1,9},{9,1},{17,25},{25,17},{2,10},{10... | collective-permute-start | bytes 1769480 | tf_op jit(solution)/shard_map/ppermute | solution.py:964
  218.2 16.9 %collective-permute-start.33 = (bf16[2,96,768]{2,1,0:T(8,128)(2,1)}, bf16[2,96,768]{2,1,0:T(8,128)(2,1)}, u32[]{:S(2)}, u32[]{:S(2)}) collective-permute-start(bf16[2,96,768]{2,1,0:T(8,128)(2,1)} %get-tuple-element.402), channel_id=1, source_target_pairs={{0,8},{8,0},{16,24},{24,16},{1,9},{9,1},{17,25},{25,17},{2,10},{10... | collective-permute-start | bytes 884744 | tf_op jit(solution)/shard_map/ppermute | solution.py:964
  218.2 16.9 %collective-permute-start.32 = (bf16[2,96,768]{2,1,0:T(8,128)(2,1)}, bf16[2,96,768]{2,1,0:T(8,128)(2,1)}, u32[]{:S(2)}, u32[]{:S(2)}) collective-permute-start(bf16[2,96,768]{2,1,0:T(8,128)(2,1)} %get-tuple-element.403), channel_id=1, source_target_pairs={{0,16},{8,24},{16,0},{24,8},{1,17},{9,25},{17,1},{25,9},{2,18},{10... | collective-permute-start | bytes 884744 | tf_op jit(solution)/shard_map/ppermute | solution.py:964
  235.1 30.4 %collective-permute-start.39 = (bf16[4,4,96,768]{3,2,1,0:T(8,128)(2,1)}, bf16[4,4,96,768]{3,2,1,0:T(8,128)(2,1)}, u32[]{:S(2)}, u32[]{:S(2)}) collective-permute-start(bf16[4,4,96,768]{3,2,1,0:T(8,128)(2,1)} %get-tuple-element.287), channel_id=1, source_target_pairs={{0,1},{1,0},{2,3},{3,2},{4,5},{5,4},{6,7},{7,6},{8,9},{9,8},{10,11... | collective-permute-start | bytes 7077896 | tf_op jit(solution)/shard_map/ppermute | solution.py:961
  237.2 28.2 %collective-permute-start.36 = (bf16[2,96,768]{2,1,0:T(8,128)(2,1)}, bf16[2,96,768]{2,1,0:T(8,128)(2,1)}, u32[]{:S(2)}, u32[]{:S(2)}) collective-permute-start(bf16[2,96,768]{2,1,0:T(8,128)(2,1)} %bitcast_add_fusion.7), channel_id=1, source_target_pairs={{0,4},{1,5},{2,6},{3,7},{4,0},{5,1},{6,2},{7,3},{8,12},{9,13},{10,... | collective-permute-start | bytes 884744 | tf_op jit(solution)/shard_map/ppermute | solution.py:958
  241.3 24.2 %collective-permute-start.38 = (bf16[2,96,768]{2,1,0:T(8,128)(2,1)S(1)}, bf16[2,96,768]{2,1,0:T(8,128)(2,1)}, u32[]{:S(2)}, u32[]{:S(2)}) collective-permute-start(bf16[2,96,768]{2,1,0:T(8,128)(2,1)S(1)} %get-tuple-element.398), channel_id=1, source_target_pairs={{0,8},{8,0},{16,24},{24,16},{1,9},{9,1},{17,25},{25,17},{2,10},{10... | collective-permute-start | bytes 884744 | tf_op jit(solution)/shard_map/ppermute | solution.py:964
  242.8 22.7 %collective-permute-start.37 = (bf16[2,96,768]{2,1,0:T(8,128)(2,1)S(1)}, bf16[2,96,768]{2,1,0:T(8,128)(2,1)}, u32[]{:S(2)}, u32[]{:S(2)}) collective-permute-start(bf16[2,96,768]{2,1,0:T(8,128)(2,1)S(1)} %get-tuple-element.399), channel_id=1, source_target_pairs={{0,16},{8,24},{16,0},{24,8},{1,17},{9,25},{17,1},{25,9},{2,18},{10... | collective-permute-start | bytes 884744 | tf_op jit(solution)/shard_map/ppermute | solution.py:964
  265.5 23.1 %collective-permute-start.42 = (bf16[4,4,96,768]{3,2,1,0:T(8,128)(2,1)}, bf16[4,4,96,768]{3,2,1,0:T(8,128)(2,1)}, u32[]{:S(2)}, u32[]{:S(2)}) collective-permute-start(bf16[4,4,96,768]{3,2,1,0:T(8,128)(2,1)} %get-tuple-element.306), channel_id=1, source_target_pairs={{0,1},{1,0},{2,3},{3,2},{4,5},{5,4},{6,7},{7,6},{8,9},{9,8},{10,11... | collective-permute-start | bytes 7077896 | tf_op jit(solution)/shard_map/ppermute | solution.py:961
  267.5 21.1 %collective-permute-start.41 = (bf16[2,96,768]{2,1,0:T(8,128)(2,1)}, bf16[2,96,768]{2,1,0:T(8,128)(2,1)S(1)}, u32[]{:S(2)}, u32[]{:S(2)}) collective-permute-start(bf16[2,96,768]{2,1,0:T(8,128)(2,1)} %bitcast_add_fusion.5), channel_id=1, source_target_pairs={{0,4},{1,5},{2,6},{3,7},{4,0},{5,1},{6,2},{7,3},{8,12},{9,13},{10,... | collective-permute-start | bytes 884744 | tf_op jit(solution)/shard_map/ppermute | solution.py:958
  271.9 16.7 %collective-permute-start.44 = (bf16[2,2,96,768]{3,2,1,0:T(8,128)(2,1)}, bf16[2,2,96,768]{3,2,1,0:T(8,128)(2,1)S(1)}, u32[]{:S(2)}, u32[]{:S(2)}) collective-permute-start(bf16[2,2,96,768]{3,2,1,0:T(8,128)(2,1)} %get-tuple-element.396), channel_id=1, source_target_pairs={{0,16},{8,24},{16,0},{24,8},{1,17},{9,25},{17,1},{25,9},{2,18},{10... | collective-permute-start | bytes 1769480 | tf_op jit(solution)/shard_map/ppermute | solution.py:964
  272.6 16.0 %collective-permute-start.43 = (bf16[2,2,96,768]{3,2,1,0:T(8,128)(2,1)}, bf16[2,2,96,768]{3,2,1,0:T(8,128)(2,1)S(1)}, u32[]{:S(2)}, u32[]{:S(2)}) collective-permute-start(bf16[2,2,96,768]{3,2,1,0:T(8,128)(2,1)} %get-tuple-element.397), channel_id=1, source_target_pairs={{0,8},{8,0},{16,24},{24,16},{1,9},{9,1},{17,25},{25,17},{2,10},{10... | collective-permute-start | bytes 1769480 | tf_op jit(solution)/shard_map/ppermute | solution.py:964
  275.8 12.7 %collective-permute-start.40 = (bf16[96,768]{1,0:T(8,128)(2,1)}, bf16[96,768]{1,0:T(8,128)(2,1)}, u32[]{:S(2)}, u32[]{:S(2)}) collective-permute-start(bf16[96,768]{1,0:T(8,128)(2,1)} %slice_bitcast_fusion.11), channel_id=1, source_target_pairs={{0,2},{1,3},{2,0},{3,1},{4,6},{5,7},{6,4},{7,5},{8,10},{9,11},{10,... | collective-permute-start | bytes 442376 | tf_op jit(solution)/shard_map/ppermute | solution.py:958
  288.6 21.9 %collective-permute-start.50 = (f32[32,768]{1,0:T(8,128)}, f32[32,768]{1,0:T(8,128)}, u32[]{:S(2)}, u32[]{:S(2)}) collective-permute-start(f32[32,768]{1,0:T(8,128)} %get-tuple-element.316), channel_id=1, source_target_pairs={{0,1},{1,0},{2,3},{3,2},{4,5},{5,4},{6,7},{7,6},{8,9},{9,8},{10,11... | collective-permute-start | bytes 294920 | tf_op jit(solution)/shard_map/ppermute | solution.py:1116
  288.7 30.0 %collective-permute-start.49 = (bf16[4,4,48,256]{3,2,1,0:T(8,128)(2,1)}, bf16[4,4,48,256]{3,2,1,0:T(8,128)(2,1)}, u32[]{:S(2)}, u32[]{:S(2)}) collective-permute-start(bf16[4,4,48,256]{3,2,1,0:T(8,128)(2,1)} %get-tuple-element.315), channel_id=1, source_target_pairs={{0,1},{1,0},{2,3},{3,2},{4,5},{5,4},{6,7},{7,6},{8,9},{9,8},{10,11... | collective-permute-start | bytes 1179656 | tf_op jit(solution)/shard_map/ppermute | solution.py:961
  291.9 20.8 %collective-permute-start.48 = (bf16[2,96,768]{2,1,0:T(8,128)(2,1)}, bf16[2,96,768]{2,1,0:T(8,128)(2,1)S(1)}, u32[]{:S(2)}, u32[]{:S(2)}) collective-permute-start(bf16[2,96,768]{2,1,0:T(8,128)(2,1)} %get-tuple-element.392), channel_id=1, source_target_pairs={{0,8},{8,0},{16,24},{24,16},{1,9},{9,1},{17,25},{25,17},{2,10},{10... | collective-permute-start | bytes 884744 | tf_op jit(solution)/shard_map/ppermute | solution.py:964
  295.7 23.0 %collective-permute-start.46 = (bf16[2,2,96,768]{3,2,1,0:T(8,128)(2,1)}, bf16[2,2,96,768]{3,2,1,0:T(8,128)(2,1)S(1)}, u32[]{:S(2)}, u32[]{:S(2)}) collective-permute-start(bf16[2,2,96,768]{3,2,1,0:T(8,128)(2,1)} %get-tuple-element.394), channel_id=1, source_target_pairs={{0,16},{8,24},{16,0},{24,8},{1,17},{9,25},{17,1},{25,9},{2,18},{10... | collective-permute-start | bytes 1769480 | tf_op jit(solution)/shard_map/ppermute | solution.py:964
  297.7 21.0 %collective-permute-start.45 = (bf16[2,2,96,768]{3,2,1,0:T(8,128)(2,1)}, bf16[2,2,96,768]{3,2,1,0:T(8,128)(2,1)S(1)}, u32[]{:S(2)}, u32[]{:S(2)}) collective-permute-start(bf16[2,2,96,768]{3,2,1,0:T(8,128)(2,1)} %get-tuple-element.395), channel_id=1, source_target_pairs={{0,8},{8,0},{16,24},{24,16},{1,9},{9,1},{17,25},{25,17},{2,10},{10... | collective-permute-start | bytes 1769480 | tf_op jit(solution)/shard_map/ppermute | solution.py:964
  312.7 13.3 %collective-permute-start.56 = (bf16[96,768]{1,0:T(8,128)(2,1)S(1)}, bf16[96,768]{1,0:T(8,128)(2,1)S(1)}, u32[]{:S(2)}, u32[]{:S(2)}) collective-permute-start(bf16[96,768]{1,0:T(8,128)(2,1)S(1)} %slice_bitcast_fusion.7), channel_id=1, source_target_pairs={{0,2},{1,3},{2,0},{3,1},{4,6},{5,7},{6,4},{7,5},{8,10},{9,11},{10,... | collective-permute-start | bytes 442376 | tf_op jit(solution)/shard_map/ppermute | solution.py:958
  318.7 9.7 %collective-permute-start.59 = (f32[32,768]{1,0:T(8,128)S(1)}, f32[32,768]{1,0:T(8,128)S(1)}, u32[]{:S(2)}, u32[]{:S(2)}) collective-permute-start(f32[32,768]{1,0:T(8,128)S(1)} %add.360), channel_id=1, source_target_pairs={{0,2},{1,3},{2,0},{3,1},{4,6},{5,7},{6,4},{7,5},{8,10},{9,11},{10,... | collective-permute-start | bytes 294920 | tf_op jit(solution)/shard_map/ppermute | solution.py:1116
  321.5 9.3 %collective-permute-start.53 = (bf16[96,768]{1,0:T(8,128)(2,1)S(1)}, bf16[96,768]{1,0:T(8,128)(2,1)S(1)}, u32[]{:S(2)}, u32[]{:S(2)}) collective-permute-start(bf16[96,768]{1,0:T(8,128)(2,1)S(1)} %slice_bitcast_fusion.10), channel_id=1, source_target_pairs={{0,2},{1,3},{2,0},{3,1},{4,6},{5,7},{6,4},{7,5},{8,10},{9,11},{10,... | collective-permute-start | bytes 442376 | tf_op jit(solution)/shard_map/ppermute | solution.py:958
  323.4 16.7 %collective-permute-start.57 = (bf16[4,4,48,256]{3,2,1,0:T(8,128)(2,1)S(1)}, bf16[4,4,48,256]{3,2,1,0:T(8,128)(2,1)S(1)}, u32[]{:S(2)}, u32[]{:S(2)}) collective-permute-start(bf16[4,4,48,256]{3,2,1,0:T(8,128)(2,1)S(1)} %add.380), channel_id=1, source_target_pairs={{0,8},{8,0},{16,24},{24,16},{1,9},{9,1},{17,25},{25,17},{2,10},{10... | collective-permute-start | bytes 1179656 | tf_op jit(solution)/shard_map/ppermute | solution.py:964
  326.0 14.1 %collective-permute-start.52 = (bf16[2,96,768]{2,1,0:T(8,128)(2,1)S(1)}, bf16[2,96,768]{2,1,0:T(8,128)(2,1)S(1)}, u32[]{:S(2)}, u32[]{:S(2)}) collective-permute-start(bf16[2,96,768]{2,1,0:T(8,128)(2,1)S(1)} %get-tuple-element.390), channel_id=1, source_target_pairs={{0,8},{8,0},{16,24},{24,16},{1,9},{9,1},{17,25},{25,17},{2,10},{10... | collective-permute-start | bytes 884744 | tf_op jit(solution)/shard_map/ppermute | solution.py:964
  326.8 13.3 %collective-permute-start.51 = (bf16[2,96,768]{2,1,0:T(8,128)(2,1)S(1)}, bf16[2,96,768]{2,1,0:T(8,128)(2,1)S(1)}, u32[]{:S(2)}, u32[]{:S(2)}) collective-permute-start(bf16[2,96,768]{2,1,0:T(8,128)(2,1)S(1)} %get-tuple-element.391), channel_id=1, source_target_pairs={{0,16},{8,24},{16,0},{24,8},{1,17},{9,25},{17,1},{25,9},{2,18},{10... | collective-permute-start | bytes 884744 | tf_op jit(solution)/shard_map/ppermute | solution.py:964
  330.7 9.4 %collective-permute-start.54 = (bf16[96,768]{1,0:T(8,128)(2,1)S(1)}, bf16[96,768]{1,0:T(8,128)(2,1)S(1)}, u32[]{:S(2)}, u32[]{:S(2)}) collective-permute-start(bf16[96,768]{1,0:T(8,128)(2,1)S(1)} %get-tuple-element.416), channel_id=1, source_target_pairs={{0,4},{1,5},{2,6},{3,7},{4,0},{5,1},{6,2},{7,3},{8,12},{9,13},{10,... | collective-permute-start | bytes 442376 | tf_op jit(solution)/shard_map/ppermute | solution.py:958
  341.7 12.2 %collective-permute-start.67 = (f32[32,768]{1,0:T(8,128)S(1)}, f32[32,768]{1,0:T(8,128)S(1)}, u32[]{:S(2)}, u32[]{:S(2)}) collective-permute-start(f32[32,768]{1,0:T(8,128)S(1)} %add.382), channel_id=1, source_target_pairs={{0,4},{1,5},{2,6},{3,7},{4,0},{5,1},{6,2},{7,3},{8,12},{9,13},{10,... | collective-permute-start | bytes 294920 | tf_op jit(solution)/shard_map/ppermute | solution.py:1116
  341.8 12.1 %collective-permute-start.60 = (bf16[96,768]{1,0:T(8,128)(2,1)S(1)}, bf16[96,768]{1,0:T(8,128)(2,1)S(1)}, u32[]{:S(2)}, u32[]{:S(2)}) collective-permute-start(bf16[96,768]{1,0:T(8,128)(2,1)S(1)} %slice_bitcast_fusion.5), channel_id=1, source_target_pairs={{0,2},{1,3},{2,0},{3,1},{4,6},{5,7},{6,4},{7,5},{8,10},{9,11},{10,... | collective-permute-start | bytes 442376 | tf_op jit(solution)/shard_map/ppermute | solution.py:958
  344.8 10.1 %collective-permute-start.62 = (bf16[96,768]{1,0:T(8,128)(2,1)S(1)}, bf16[96,768]{1,0:T(8,128)(2,1)S(1)}, u32[]{:S(2)}, u32[]{:S(2)}) collective-permute-start(bf16[96,768]{1,0:T(8,128)(2,1)S(1)} %get-tuple-element.413), channel_id=1, source_target_pairs={{0,6},{1,7},{2,4},{3,5},{4,2},{5,3},{6,0},{7,1},{8,14},{9,15},{10,... | collective-permute-start | bytes 442376 | tf_op jit(solution)/shard_map/ppermute | solution.py:958
  346.2 14.7 %collective-permute-start.66 = (bf16[2,96,768]{2,1,0:T(8,128)(2,1)S(1)}, bf16[2,96,768]{2,1,0:T(8,128)(2,1)S(1)}, u32[]{:S(2)}, u32[]{:S(2)}) collective-permute-start(bf16[2,96,768]{2,1,0:T(8,128)(2,1)S(1)} %pad_maximum_fusion.5), channel_id=1, source_target_pairs={{0,8},{8,0},{16,24},{24,16},{1,9},{9,1},{17,25},{25,17},{2,10},{10... | collective-permute-start | bytes 884744 | tf_op jit(solution)/shard_map/ppermute | solution.py:964
  347.6 13.3 %collective-permute-start.63 = (bf16[4,4,48,256]{3,2,1,0:T(8,128)(2,1)S(1)}, bf16[4,4,48,256]{3,2,1,0:T(8,128)(2,1)S(1)}, u32[]{:S(2)}, u32[]{:S(2)}) collective-permute-start(bf16[4,4,48,256]{3,2,1,0:T(8,128)(2,1)S(1)} %add.391), channel_id=1, source_target_pairs={{0,16},{8,24},{16,0},{24,8},{1,17},{9,25},{17,1},{25,9},{2,18},{10... | collective-permute-start | bytes 1179656 | tf_op jit(solution)/shard_map/ppermute | solution.py:964
  367.7 14.8 %collective-permute-start.75 = (bf16[2,96,768]{2,1,0:T(8,128)(2,1)}, bf16[2,96,768]{2,1,0:T(8,128)(2,1)}, u32[]{:S(2)}, u32[]{:S(2)}) collective-permute-start(bf16[2,96,768]{2,1,0:T(8,128)(2,1)} %pad_maximum_fusion.7), channel_id=1, source_target_pairs={{0,16},{8,24},{16,0},{24,8},{1,17},{9,25},{17,1},{25,9},{2,18},{10... | collective-permute-start | bytes 884744 | tf_op jit(solution)/shard_map/ppermute | solution.py:964
  369.5 13.0 %collective-permute-start.74 = (bf16[2,96,768]{2,1,0:T(8,128)(2,1)}, bf16[2,96,768]{2,1,0:T(8,128)(2,1)S(1)}, u32[]{:S(2)}, u32[]{:S(2)}) collective-permute-start(bf16[2,96,768]{2,1,0:T(8,128)(2,1)} %pad_maximum_fusion.6), channel_id=1, source_target_pairs={{0,8},{8,0},{16,24},{24,16},{1,9},{9,1},{17,25},{25,17},{2,10},{10... | collective-permute-start | bytes 884744 | tf_op jit(solution)/shard_map/ppermute | solution.py:964
  370.4 12.0 %collective-permute-start.70 = (bf16[96,768]{1,0:T(8,128)(2,1)}, bf16[96,768]{1,0:T(8,128)(2,1)}, u32[]{:S(2)}, u32[]{:S(2)}) collective-permute-start(bf16[96,768]{1,0:T(8,128)(2,1)} %fusion.2), channel_id=1, source_target_pairs={{0,24},{8,16},{16,8},{24,0},{1,25},{9,17},{17,9},{25,1},{2,26},{10... | collective-permute-start | bytes 442376 | tf_op jit(solution)/shard_map/ppermute | solution.py:964
  372.7 9.7 %collective-permute-start.69 = (bf16[96,768]{1,0:T(8,128)(2,1)}, bf16[96,768]{1,0:T(8,128)(2,1)}, u32[]{:S(2)}, u32[]{:S(2)}) collective-permute-start(bf16[96,768]{1,0:T(8,128)(2,1)} %fusion.2), channel_id=1, source_target_pairs={{0,16},{8,24},{16,0},{24,8},{1,17},{9,25},{17,1},{25,9},{2,18},{10... | collective-permute-start | bytes 442376 | tf_op jit(solution)/shard_map/ppermute | solution.py:964
  382.5 13.4 %collective-permute-start.77 = (f32[32,768]{1,0:T(8,128)S(1)}, f32[32,768]{1,0:T(8,128)S(1)}, u32[]{:S(2)}, u32[]{:S(2)}) collective-permute-start(f32[32,768]{1,0:T(8,128)S(1)} %add.401), channel_id=1, source_target_pairs={{0,16},{8,24},{16,0},{24,8},{1,17},{9,25},{17,1},{25,9},{2,18},{10... | collective-permute-start | bytes 294920 | tf_op jit(solution)/shard_map/ppermute | solution.py:1116
  (66 other events, 735.8 us)

commit v3 on v2

--- a/solution.py
+++ b/solution.py
@@ -543,16 +543,11 @@
             x_out[image] = middle[image] + scale[image, 1] * branch
 
 
-def last_hidden(place, scale, v, bias, grad, *rest):
-    weight = Weight(rest[:12], 0)
-    (
-        hidden_out, slope_out, mine_out, other_out, low_out, bias_grad, w_in, hidden, turned, whole, sem,
-    ) = rest[12:]
+def last_hidden(place, scale, v, bias, grad, w_in, hidden_out, slope_out, blocks_out, low_out, bias_grad, hidden, turned):
     step = pl.program_id(0)
 
     @pl.when(step == 0)
     def _():
-        fetch_in(place, 1, weight, w_in, sem)
         rows = grad.shape[1]
         sums = 0.0
         for image in range(grad.shape[0]):
@@ -564,43 +559,63 @@
 
     @pl.when(step < 4)
     def _():
-        j = (step & 3) ^ place[2]
-        arrive(w_in, sem, j)
         def product(part):
-            return dot(v[part], w_in[j], 1, 0) + bias[...]
+            return dot(v[part], w_in[...], 1, 0) + bias[...]
 
         def finish(part, found):
             value, slope = gelu_pair(found)
             hidden_out[0, part] = value
-            hidden[j, part] = value
+            hidden[step & 3, part] = value
             slope_out[0, part] = slope
 
         staggered(chunks(v.shape[0], 4), product, finish)
 
     @pl.when(step >= 4)
     def _():
-        out_blocks(place, turned, hidden[(step & 3) ^ place[0]], mine_out, other_out, whole)
-
-
-def out_forward(place, scale, hidden, middle, bias, *rest, layer):
-    x_out, weight, total, sem = rest[12:]
+        found = dot(turned[...], hidden[step & 3], 1, 0).astype(jnp.bfloat16)
+        size = blocks_out.shape[2]
+        for k in range(blocks_out.shape[0]):
+            blocks_out[k] = found[:, k * size : (k + 1) * size]
+
+
+def last_out(place, scale, hidden, middle, bias, w_out, x_out, total):
     step = pl.program_id(0)
 
     @pl.when(step == 0)
     def _():
-        fetch_out(place, layer, Weight(rest[:12], 1), weight, sem)
         total[...] = jnp.zeros_like(total)
 
-    j = step ^ place[0]
-    arrive(weight, sem, j)
-    total[...] += dot(hidden[0], weight[j], 1, 0)
+    total[...] += dot(hidden[0], w_out[...], 1, 0)
 
     @pl.when(step == pl.num_programs(0) - 1)
     def _():
         for image in range(middle.shape[0]):
             rows = middle.shape[1]
             branch = total[image * rows : (image + 1) * rows] + bias[...]
-            x_out[image] = (middle[image] + scale[image, 2 * layer + 1] * branch).astype(x_out.dtype)
+            x_out[image] = (middle[image] + scale[image, 3] * branch).astype(x_out.dtype)
+
+
+def last_backward(place, low, v, slope, w_out, w_in, in_out, back_out, bias_grad, turned, pre):
+    @pl.when(pl.program_id(0) == 0)
+    def _():
+        turned[...] = v[...].T
+        back_out[...] = jnp.zeros_like(back_out)
+
+    sums = []
+
+    def product(part):
+        return dot(low[part], w_out[...], 1, 1)
+
+    def finish(part, found):
+        grad = found * slope[0, part].astype(jnp.float32)
+        sums.append(jnp.sum(grad, 0, keepdims=True))
+        pre[part] = grad.astype(jnp.bfloat16)
+
+    staggered(chunks(low.shape[0], 2), product, finish)
+    bias_grad[0] = sum(sums)
+    for part in chunks(turned.shape[0], 3):
+        in_out[part] = dot(turned[part], pre[...], 1, 0).astype(jnp.bfloat16)
+    back_out[...] += dot(pre[...], w_in[...], 1, 1)
 
 
 def channel_backward(place, low, v, slope, *rest, layer):
@@ -628,7 +643,7 @@
         sums.append(jnp.sum(grad, 0, keepdims=True))
         pre[part] = grad.astype(jnp.bfloat16)
 
-    staggered(chunks(low.shape[0], 4), product, finish)
+    staggered(chunks(low.shape[0], 2), product, finish)
     bias_grad[0] = sum(sums)
     for part in chunks(turned.shape[0], 3):
         whole[part] = dot(turned[part], pre[...], 1, 0).astype(jnp.bfloat16)
@@ -641,23 +656,24 @@
     back_out[...] += dot(pre[...], w_in[j], 1, 1)
 
 
-def finish_out(place, *refs):
-    parts, out, whole = refs[:4], refs[-2], refs[-1]
+def finish_last(place, grad_in, grad_out, in_out, out_out):
+    in_out[0] = grad_in[...].astype(jnp.float32)
+    out_out[0] = grad_out[0].astype(jnp.float32).T
+
+
+def finish_first(place, *refs):
+    parts_in, parts_out = refs[:4], refs[4:8]
+    in_out, out_out, whole = refs[-3:]
     for j in range(4):
-        rows, columns = parts[j].shape[1:]
+        columns = parts_in[j].shape[2]
+        start = pl.multiple_of((j ^ place[2]) * columns, columns)
+        in_out[0, :, pl.ds(start, columns)] = parts_in[j][0].astype(jnp.float32)
+        rows, columns = parts_out[j].shape[1:]
         for half in range(2):
             start = pl.multiple_of((2 * (j ^ place[2]) + half) * rows, rows)
-            part = parts[j][0, :, half * columns // 2 : (half + 1) * columns // 2]
+            part = parts_out[j][0, :, half * columns // 2 : (half + 1) * columns // 2]
             whole[pl.ds(start, rows)] = part.astype(jnp.float32)
-    out[0] = whole[...].T
-
-
-def finish_in(place, *refs):
-    parts, out = refs[:4], refs[-1]
-    for j in range(4):
-        columns = parts[j].shape[2]
-        start = pl.multiple_of((j ^ place[2]) * columns, columns)
-        out[0, :, pl.ds(start, columns)] = parts[j][0].astype(jnp.float32)
+    out_out[0] = whole[...].T
 
 
 class Kernels:
@@ -809,24 +825,58 @@
             2 * self.product(),
         )
 
-    def last_hidden(self, scale, v, bias, grad, weights):
+    def steps(self, array):
+        return (array, (1,) + array.shape[1:], lambda i, s: (jnp.minimum(i, 3), 0, 0))
+
+    def steps_out(self):
+        block = (1, self.slots * self.rows, self.part)
+        return ((4,) + block[1:], jnp.bfloat16, block, lambda i, s: (jnp.minimum(i, 3), 0, 0))
+
+    def columns_in(self, array):
+        return (array, (array.shape[0], self.part), lambda i, s: (0, jnp.minimum(i, 3)))
+
+    def rows_in(self, array):
+        return (array, (self.part, array.shape[1]), lambda i, s: (i, 0))
+
+    def last_hidden(self, scale, v, bias, grad, w_in):
+        bf16, f32 = jnp.bfloat16, jnp.float32
+        rows = self.slots * self.rows
+        block = (2, self.width, self.part // 2)
+        return self.run(
+            last_hidden,
+            8,
+            [self.scalars(scale), self.fixed(v), self.columns_in(bias), self.fixed(grad), self.columns_in(w_in)],
+            [self.steps_out()] * 2
+            + [((8,) + block[1:], bf16, block, lambda i, s: (jnp.maximum(i - 4, 0), 0, 0))]
+            + [self.fixed_out((rows, self.width), bf16), self.fixed_out((1, self.width), f32)],
+            [pltpu.VMEM((4, rows, self.part), bf16), pltpu.VMEM((self.width, rows), bf16)],
+            2 * self.product(),
+        )
+
+    def last_out(self, scale, hidden, middle, bias, w_out):
+        return self.run(
+            last_out,
+            4,
+            [self.scalars(scale), self.steps(hidden), self.fixed(middle), self.fixed(bias), self.rows_in(w_out)],
+            [self.fixed_out(middle.shape, jnp.bfloat16)],
+            [pltpu.VMEM((self.slots * self.rows, self.width), jnp.float32)],
+            self.product(),
+        )[0]
+
+    def last_backward(self, low, v, slope, w_out, w_in):
         bf16, f32 = jnp.bfloat16, jnp.float32
         rows = self.slots * self.rows
         return self.run(
-            last_hidden,
-            8,
-            [self.scalars(scale), self.fixed(v), self.row(bias, 2), self.fixed(grad)] + self.in_hbm(weights),
-            [self.quarters_out(2)] * 2
-            + [self.out_blocks_out(4)] * 2
-            + [self.fixed_out((rows, self.width), bf16), self.fixed_out((1, self.width), f32)],
+            last_backward,
+            4,
+            [self.fixed(low), self.fixed(v), self.steps(slope), self.rows_in(w_out), self.columns_in(w_in)],
             [
-                self.weight(),
-                pltpu.VMEM((4, rows, self.part), bf16),
-                pltpu.VMEM((self.width, rows), bf16),
-                pltpu.VMEM((self.width, self.part), bf16),
-                pltpu.SemaphoreType.DMA((4,)),
+                ((self.width, self.hidden), bf16, (self.width, self.part), lambda i, s: (0, i)),
+                self.fixed_out((rows, self.width), f32),
+                ((4, 1, self.part), f32, (1, 1, self.part), lambda i, s: (i, 0, 0)),
             ],
-            2 * self.product(),
+            [pltpu.VMEM((self.width, rows), bf16), pltpu.VMEM((rows, self.part), bf16)],
+            3 * self.product(),
         )
 
     def token_backward(self, scale, grad, back, kept, small, g_cout, g_cin, keys, earlier=()):
@@ -916,34 +966,28 @@
             layer=layer,
         )
 
-    def parts(self, parts):
-        def one(array, index):
+    def shard_outs(self, layer, layers):
+        shapes = (layers, self.block, self.hidden), (layers, self.part // 2, self.width)
+        return [(shape, jnp.float32, (1,) + shape[1:], lambda i, s: (layer, 0, 0)) for shape in shapes]
+
+    def finish_last(self, grad_in, grad_out, layer, layers):
+        inputs = [self.fixed(grad_in), self.fixed(grad_out)]
+        return self.run(finish_last, 1, inputs, self.shard_outs(layer, layers), [], 0)
+
+    def finish_first(self, parts_in, parts_out, layer, layers, earlier):
+        def one(part):
+            array, index = part
             return (array, (1,) + array.shape[1:], lambda i, s: (index, 0, 0))
 
-        return [one(*part) for part in parts]
-
-    def finish_out(self, parts, layer, layers, earlier=()):
-        shape = (layers, self.part // 2, self.width)
+        inputs = [one(part) for part in parts_in + parts_out]
         return self.run(
-            finish_out,
+            finish_first,
             1,
-            self.parts(parts) + self.in_hbm(earlier),
-            [(shape, jnp.float32, (1,) + shape[1:], lambda i, s: (layer, 0, 0))],
+            inputs + self.in_hbm(earlier),
+            self.shard_outs(layer, layers),
             [pltpu.VMEM((self.width, self.part // 2), jnp.float32)],
             0,
-            {1 + len(parts): 0} if earlier else None,
-        )
-
-    def finish_in(self, parts, layer, layers, earlier=()):
-        shape = (layers, self.block, self.hidden)
-        return self.run(
-            finish_in,
-            1,
-            self.parts(parts) + self.in_hbm(earlier),
-            [(shape, jnp.float32, (1,) + shape[1:], lambda i, s: (layer, 0, 0))],
-            [],
-            0,
-            {1 + len(parts): 0} if earlier else None,
+            {1 + len(inputs): 0, 2 + len(inputs): 1},
         )
 
 
@@ -1102,6 +1146,19 @@
     def total(self):
         parts = [self.value[0]] + [getattr(self, "z%d" % i) for i in range(1, self.moves.lines)]
         return sum(part.astype(jnp.float32) for part in parts)
+
+
+class Copies(Held):
+    def __init__(self, moves, *values):
+        super().__init__(moves)
+        self.values = list(values)
+
+    def step(self, *axes):
+        got = [self.moves.across(value, bits) for value, bits in zip(self.values, axes)]
+        self.bring(got0=got[0], got1=got[1])
+
+    def add(self):
+        self.values = [self.values[0] + self.got0, self.values[1] + self.got1]
 
 
 class SumAll(Held):
@@ -1159,99 +1216,69 @@
     b_outs = jnp.pad(token_out_bias.astype(f32), ((0, 0), (0, wide - patches)))[:, :, None]
     scale = scale.reshape(slots, 2 * layers)
 
-    def both(layer):
-        return jnp.stack([quarter(channel_in[layer], 1), quarter(channel_out[layer], 0)])
-
-    first, last = Gather(moves, both(0)), Gather(moves, both(1))
+    first = Gather(moves, jnp.stack([quarter(channel_in[0], 1), quarter(channel_out[0], 0)]))
     small = Gather(moves, packs)
     shards_held = Held(moves)
+    small.direct()
     first.direct()
-    shards_held.bring(ins=moves.core(channel_in), outs=moves.core(channel_out))
-    small.part, last.part = settle((first, shards_held), small.part, last.part)
+    shards_held.bring(ins=moves.core(channel_in[0]), outs=moves.core(channel_out[0]))
+    shard_in, shard_out = settle((first, small, shards_held), channel_in[1], channel_out[1])
     first.join()
-
-    def weights(gather):
-        return [channel_in, channel_out, shards_held.ins, shards_held.outs] + gather.whole()
-
+    small.line = jnp.stack([small.part, small.z1, small.z2, small.z3])
+
+    w_cin1 = lax.all_gather(shard_in, "fsdp", axis=0, tiled=True)
+    w_cout1 = lax.all_gather(shard_out, "fsdp", axis=0, tiled=True)
+
+    small.core("line")
     first.first()
     began, first.fresh = first.fresh, []
     first.core("line")
-    small.direct()
-    (last.part, first.line) = settle((first, small), last.part, first.line)
+    (first.line,) = settle((first, small), first.line)
     first.fresh = began
-    small.line = jnp.stack([small.part, small.z1, small.z2, small.z3])
-    small.core("line")
-    last.direct()
-    last.fresh = ["z2"]
     found = kernels.unpack_small(small.line, small.line_core, layers, shards_count, extra)
     x0 = padded(tokens)
     (w_in0, w_in_t0, w_out0, w_out_t0, gain1_0, shift1_0, gain2_0, shift2_0, b_cout0, b_cin0) = found[0]
     (w_in1, w_in_t1, w_out1, w_out_t1, gain1_1, shift1_1, gain2_1, shift2_1, b_cout1, b_cin1) = found[1]
-
     u0, h0, d0, mid0, v0 = kernels.token_forward(
         scale, x0, b_outs, (gain1_0, shift1_0, w_in0, w_out_t0, gain2_0, shift2_0), 0
     )
-    (v0,) = settle((first, small, last), v0)
+    (v0,) = settle((first,), v0)
 
     first.second()
-    last.fresh = ["z3"]
-    (v0, first.x, first.y) = settle((first, last), v0, first.x, first.y)
     first.core("x", "y")
+    (v0,) = settle((first,), v0)
     first.corner_core()
-    last.fresh = ["z1"]
-    (v0,) = settle((first, last), v0)
-
-    last.join()
-    last.first()
-    hid0, slope0, x1 = kernels.first_forward(scale, v0, mid0, b_cin0, b_cout0, weights(first))
-    (x1,) = settle((last,), x1)
-
-    last.second()
-    last.core("line", "x", "y")
+    (v0,) = settle((first,), v0)
+    weights = [channel_in, channel_out, shards_held.ins[None], shards_held.outs[None]] + first.whole()
+    hid0, slope0, x1 = kernels.first_forward(scale, v0, mid0, b_cin0, b_cout0, weights)
     u1, h1, d1, mid1, v1 = kernels.token_forward(
         scale, x1, b_outs, (gain1_1, shift1_1, w_in1, w_out_t1, gain2_1, shift2_1), 1
     )
-    (v1,) = settle((last,), v1)
-    last.corner_core()
     grad2 = padded(cotangent)
-    hid1, slope1, mine, theirs, low1, g_cout1 = kernels.last_hidden(scale, v1, b_cin1, grad2, weights(last))
-    mine, theirs, low1 = settle((last,), mine, theirs, low1)
-
-    sum_out1 = Sum(moves, mine, theirs)
-    sum_out1.core()
-    mine, theirs, back, g_cin1 = kernels.channel_backward(low1, v1, slope1, weights(last), 1)
-    mine, theirs, back = settle((sum_out1,), mine, theirs, back)
-
-    sum_in1 = Sum(moves, mine, theirs)
-    sum_in1.core()
-    sum_out1.first()
-    grads1 = kernels.token_backward(
+    hid1, slope1, blocks1, low1, g_cout1 = kernels.last_hidden(scale, v1, b_cin1, grad2, w_cin1)
+
+    grad_cout1 = lax.psum_scatter(blocks1, "fsdp", scatter_dimension=0, tiled=True)
+    grad_cin1, back, g_cin1 = kernels.last_backward(low1, v1, slope1, w_cout1, w_cin1)
+    grad_cin1 = lax.psum_scatter(grad_cin1, "fsdp", scatter_dimension=0, tiled=True)
+    grad1, *tokens1, vector1, low0, g_cout0 = kernels.token_backward(
         scale, grad2, back, (mid1, x1, u1, h1, d1), (w_in_t1, w_out1, gain1_1, gain2_1), g_cout1, g_cin1, keys
     )
-    grad1, *tokens1, vector1, low0, g_cout0 = settle((sum_out1, sum_in1), *grads1)
-
-    sum_out1.second()
-    sum_in1.first()
     mine, theirs = kernels.out_weight_grad(low0, hid0)
-    mine, theirs = settle((sum_out1, sum_in1), mine, theirs)
+    mine, theirs, grad1 = settle((), mine, theirs, grad1)
 
     sum_out0 = Sum(moves, mine, theirs)
     sum_out0.core()
-    sum_in1.second()
-    sum_out1.far()
-    mine, theirs, back, g_cin0 = kernels.channel_backward(low0, v0, slope0, weights(first), 0)
-    mine, theirs, back = settle((sum_out1, sum_in1, sum_out0), mine, theirs, back)
+    mine, theirs, back, g_cin0 = kernels.channel_backward(low0, v0, slope0, weights, 0)
+    mine, theirs, back, grad_cout1 = settle((sum_out0,), mine, theirs, back, grad_cout1)
 
     sum_in0 = Sum(moves, mine, theirs)
     sum_in0.core()
     sum_out0.first()
-    sum_in1.far()
-    sum_out1.near()
     grad0, *tokens, vector = kernels.token_backward(
         scale, grad1, back, (mid0, x0, u0, h0, d0), (w_in_t0, w_out0, gain1_0, gain2_0), g_cout0, g_cin0, keys,
         (*tokens1, vector1),
     )
-    hid1, grad0, *tokens, vector = settle((sum_out1, sum_in1, sum_in0, sum_out0), hid1, grad0, *tokens, vector)
+    hid1, grad0, *tokens, vector = settle((sum_in0, sum_out0), hid1, grad0, *tokens, vector)
 
     sum_tokens = SumSmall(moves, *tokens)
     sum_tokens.core()
@@ -1259,44 +1286,42 @@
     sum_out0.second()
     vector_sum = SumAll(moves, vector)
     vector_sum.step()
-    output = kernels.out_forward(scale, hid1, mid1, b_cout1, weights(last), 1, bf16)
+    output = kernels.last_out(scale, hid1, mid1, b_cout1, w_cout1)
     (output,) = settle((sum_in0, sum_out0, sum_tokens, vector_sum), output)
 
     sum_in0.second()
     sum_out0.once()
-    sum_in1.near()
     sum_tokens.across(1)
     vector_sum.step()
-    share_out1 = Share(moves, sum_out1.total(), 2)
-    share_out1.first()
-    output = output[:, :patches]
-    (output,) = settle((sum_in0, sum_out0, sum_in1, sum_tokens, share_out1, vector_sum), output)
+    output = jnp.swapaxes(output[:, :patches], 0, 1)
+    output, grad_cin1, grad_cout1 = settle(
+        (sum_in0, sum_out0, sum_tokens, vector_sum), output, grad_cin1, grad_cout1
+    )
 
     sum_in0.once()
     sum_tokens.across(2)
     vector_sum.step()
-    share_out0, share_in1 = Share(moves, sum_out0.total(), 2), Share(moves, sum_in1.total(), 1)
+    share_out0 = Share(moves, sum_out0.total(), 2)
     share_out0.first()
-    share_in1.first()
-    share_out1.second()
-    input_grad = grad0[:, :patches]
-    (input_grad,) = settle(
-        (sum_in0, sum_tokens, share_out0, share_in1, share_out1, vector_sum), input_grad
-    )
+    whole = Copies(moves, grad_cin1, grad_cout1)
+    whole.step(1, 2)
+    input_grad = jnp.swapaxes(grad0[:, :patches], 0, 1)
+    (input_grad,) = settle((sum_in0, sum_tokens, share_out0, whole, vector_sum), input_grad)
 
     total = sum_in0.total()
     near = [moves.across(total, bits) for bits in (1, 2, 3)]
     share_out0.second()
-    share_in1.second()
+    whole.add()
+    whole.step(2, 1)
+    vector_sum.step()
+    near = settle((share_out0, whole, vector_sum), *near)
     sum_tokens.along()
     vector_sum.step()
-    (done_out,) = kernels.finish_out(share_out1.parts(), 1, layers)
-    done_out, *near = settle((sum_tokens, share_out0, share_in1, vector_sum), done_out, *near)
-    vector_sum.step()
-    (done_in,) = kernels.finish_in(share_in1.parts(), 1, layers)
-    (grad_out,) = kernels.finish_out(share_out0.parts(), 0, layers, (done_out,))
-    parts = [(part[None], 0) for part in [total] + near]
-    (grad_in,) = kernels.finish_in(parts, 0, layers, (done_in,))
+    whole.add()
+    finished = kernels.finish_last(*whole.values, 1, layers)
+    parts = [(part[None], 0) for part in [total] + list(near)]
+    grad_in, grad_out = kernels.finish_first(parts, share_out0.parts(), 0, layers, finished)
+    output, input_grad = jnp.swapaxes(output, 0, 1), jnp.swapaxes(input_grad, 0, 1)
     near = sum_tokens.total()
 
     near = near.reshape(layers, 2, keys, wide)

time: 405 us -> 384 us (0.948)
  starting transfers between devices: 85.2 us -> 55.6 us
  waiting for transfers between devices: 71.3 us -> 96.4 us
  other arithmetic: 39.3 us -> 25.7 us
  between operations: 2.66 us -> 15.6 us
  Pallas kernels: 164 us -> 153 us
  local copies, waits for them, and re-layouts: 38.1 us -> 33.2 us
    ppermute x35 -> x23, waiting for transfers between devices: 12.4 us -> 35 us  [across(): lax.ppermute(values, 'dp', [(q, q ^ bits) for q in range(self.copies)])]
    ppermute x22 -> x15, starting transfers between devices: 38.2 us -> 21.3 us  [along(): lax.ppermute(values, 'fsdp', [(f, f ^ 2 * bits) for f in range(2 * self.l...]
    all_gather x0 -> x2, waiting for transfers between devices: none -> 11.7 us  [the longest x1 11.7 us: blocked_shards(): w_cout1 = lax.all_gather(shard_out, 'fsdp', axis=0, tiled=True)]
    pallas_call x15 -> x13, Pallas kernels: 164 us -> 153 us  [run(): pl.pallas_call(functools.partial(body, **fixed) if fixed else body, name=...]
    ppermute x35 -> x23, starting transfers between devices: 39.1 us -> 28.5 us  [across(): lax.ppermute(values, 'dp', [(q, q ^ bits) for q in range(self.copies)])]
    add x4 -> x2, other arithmetic: 9.99 us -> 4.74 us  [both(): return self.mine[copies, part] + self.got[copies, part]]
    ppermute x22 -> x15, waiting for transfers between devices: 52.2 us -> 47.1 us  [along(): lax.ppermute(values, 'fsdp', [(f, f ^ 2 * bits) for f in range(2 * self.l...]
    ppermute x5, waiting for transfers between devices: 5.55 us -> 1.11 us  [step(): got = lax.ppermute(self.value, axis, [(i, i ^ bit) for i in range(count)])]
  transfers between devices with their start and end apart: 78 -> 57, of which waited for: 17 -> 21; matrix products, arithmetic and copies ran while one was open for 13% -> 11% of each run, Pallas kernels for 36% -> 40%
where the time goes in v3:
time: 384 us; the launch traced here: 380 us
  Pallas kernels  153 us (40%)
  waiting for transfers between devices  96.4 us (25%)
  starting transfers between devices  55.6 us (14%)
  local copies, waits for them, and re-layouts  33.2 us (9%)
  other arithmetic  25.7 us (7%)
  between operations  15.6 us (4%)
    pallas_call x13, Pallas kernels, run(): pl.pallas_call(functools.partial(body, **fixed) if fixed else body, name=...  153 us
    ppermute x15, waiting for transfers between devices, along(): lax.ppermute(values, 'fsdp', [(f, f ^ 2 * bits) for f in range(2 * self.l...  47.1 us
    ppermute x23, waiting for transfers between devices, across(): lax.ppermute(values, 'dp', [(q, q ^ bits) for q in range(self.copies)])  35 us
    ppermute x23, starting transfers between devices, across(): lax.ppermute(values, 'dp', [(q, q ^ bits) for q in range(self.copies)])  28.5 us
    ppermute x15, starting transfers between devices, along(): lax.ppermute(values, 'fsdp', [(f, f ^ 2 * bits) for f in range(2 * self.l...  21.3 us
    unnamed x94, local copies, waits for them, and re-layouts  15.8 us
    all_gather x1, waiting for transfers between devices, blocked_shards(): w_cout1 = lax.all_gather(shard_out, 'fsdp', axis=0, tiled=True)  11.7 us
  transfers between devices with their start and end apart: 57, of which 21 were waited for; matrix products, arithmetic and copies ran while one was open for 11% of the time, Pallas kernels for 40%

profile of v3, /device:TPU:0, one launch (start us, length us, event | category | flops | bytes accessed | tf_op | source)
XLA Modules:
  0.0 379.5 jit_solution(6918249767308812561)
XLA Ops:
  14.1 5.1 %collective-permute-start.5 = (bf16[96,768]{1,0:T(8,128)(2,1)S(1)}, bf16[96,768]{1,0:T(8,128)(2,1)}, u32[]{:S(2)}, u32[]{:S(2)}) collective-permute-start(bf16[96,768]{1,0:T(8,128)(2,1)S(1)} %bitcast.133), channel_id=1, source_target_pairs={{0,6},{1,7},{2,4},{3,5},{4,2},{5,3},{6,0},{7,1},{8,14},{9,15},{10,... | collective-permute-start | bytes 442376 | tf_op jit(solution)/shard_map/ppermute | solution.py:1002
  19.9 2.2 slice_bitcast_fusion.19
  22.1 1.1 slice_bitcast_fusion.18
  24.1 3.9 %collective-permute-start.2 = (bf16[2,96,768]{2,1,0:T(8,128)(2,1)S(1)}, bf16[2,96,768]{2,1,0:T(8,128)(2,1)S(1)}, u32[]{:S(2)}, u32[]{:S(2)}) collective-permute-start(bf16[2,96,768]{2,1,0:T(8,128)(2,1)S(1)} %pad_maximum_fusion.2), channel_id=1, source_target_pairs={{0,6},{1,7},{2,4},{3,5},{4,2},{5,3},{6,0},{7,1},{8,14},{9,15},{10,... | collective-permute-start | bytes 884744 | tf_op jit(solution)/shard_map/ppermute | solution.py:1002
  28.0 14.3 %collective-permute-done.4 = bf16[96,768]{1,0:T(8,128)(2,1)} collective-permute-done((bf16[96,768]{1,0:T(8,128)(2,1)S(1)}, bf16[96,768]{1,0:T(8,128)(2,1)}, u32[]{:S(2)}, u32[]{:S(2)}) %collective-permute-start.4) | collective-permute-done | bytes 147488 | tf_op jit(solution)/shard_map/ppermute | solution.py:1002
  42.4 14.6 %collective-permute-done.1 = bf16[2,96,768]{2,1,0:T(8,128)(2,1)S(1)} collective-permute-done((bf16[2,96,768]{2,1,0:T(8,128)(2,1)S(1)}, bf16[2,96,768]{2,1,0:T(8,128)(2,1)S(1)}, u32[]{:S(2)}, u32[]{:S(2)}) %collective-permute-start.1) | collective-permute-done | bytes 294944 | tf_op jit(solution)/shard_map/ppermute | solution.py:1002
  59.0 1.6 collective-permute-start.11
  60.6 1.5 collective-permute-start.10
  62.1 1.1 pad_maximum_fusion.1.own
  68.3 3.2 unpack_small.1
  71.5 8.9 %token_forward.2 = (bf16[4,256,768]{2,1,0:T(8,128)(2,1)}, bf16[4,384,768]{2,1,0:T(8,128)(2,1)}, bf16[4,384,768]{2,1,0:T(8,128)(2,1)}, f32[4,208,768]{2,1,0:T(8,128)}, bf16[832,768]{1,0:T(8,128)(2,1)}) custom-call(s32[3]{0:T(128)} %pad_add_fusion.place, f32[4,4]{1,0:T(4,128)} %copy.67.scale, bf16[4,208,768]{2,1,0:T(8,128)(2,1)} %pad.36.x, ...), custom_call_target="tpu_custom_call" | custom-call | flops 1207959552 | bytes 11810880 | tf_op jit(solution)/shard_map/token_forward/pallas_call | solution.py:697
  81.2 1.2 collective-permute-done.10.rest_5_
  85.6 1.5 collective-permute-start.12
  87.1 10.1 %collective-permute-done.13 = bf16[3,1,96,768]{3,2,1,0:T(8,128)(2,1)S(1)} collective-permute-done((bf16[3,1,96,768]{3,2,1,0:T(8,128)(2,1)S(1)}, bf16[3,1,96,768]{3,2,1,0:T(8,128)(2,1)S(1)}, u32[]{:S(2)}, u32[]{:S(2)}) %collective-permute-start.13) | collective-permute-done | bytes 442400 | tf_op jit(solution)/shard_map/ppermute | solution.py:1008
  97.7 1.5 pad.44.grad
  101.1 19.8 %first_forward.1 = (bf16[4,832,768]{2,1,0:T(8,128)(2,1)}, bf16[4,832,768]{2,1,0:T(8,128)(2,1)}, f32[4,208,768]{2,1,0:T(8,128)}) custom-call(s32[3]{0:T(128)} %pad_add_fusion.place, f32[4,4]{1,0:T(4,128)} %copy.67.scale, bf16[832,768]{1,0:T(8,128)(2,1)} %get-tuple-element.167.v, f32[4,208,768]{2,1,0:T(8,128)} %get-tuple-element.168.middle, ...), custom_call_target="tpu_custom_call" | custom-call | flops 7851737088 | bytes 27245632 | tf_op jit(solution)/shard_map/first_forward/pallas_call | solution.py:697
  120.9 9.1 %token_forward.3 = (bf16[4,256,768]{2,1,0:T(8,128)(2,1)}, bf16[4,384,768]{2,1,0:T(8,128)(2,1)}, bf16[4,384,768]{2,1,0:T(8,128)(2,1)}, f32[4,208,768]{2,1,0:T(8,128)}, bf16[832,768]{1,0:T(8,128)(2,1)}) custom-call(s32[3]{0:T(128)} %pad_add_fusion.place, f32[4,4]{1,0:T(4,128)} %copy.67.scale, f32[4,208,768]{2,1,0:T(8,128)} %get-tuple-element.178.x, ...), custom_call_target="tpu_custom_call" | custom-call | flops 1207959552 | bytes 13088832 | tf_op jit(solution)/shard_map/token_forward/pallas_call | solution.py:697
  130.0 19.3 %last_hidden.1 = (bf16[4,832,768]{2,1,0:T(8,128)(2,1)}, bf16[4,832,768]{2,1,0:T(8,128)(2,1)}, bf16[8,768,384]{2,1,0:T(8,128)(2,1)}, bf16[832,768]{1,0:T(8,128)(2,1)}, f32[1,768]{1,0:T(1,128)}) custom-call(s32[3]{0:T(128)} %pad_add_fusion.place, f32[4,4]{1,0:T(4,128)} %copy.67.scale, bf16[832,768]{1,0:T(8,128)(2,1)} %get-tuple-element.185.v, ...), custom_call_target="tpu_custom_call" | custom-call | flops 7851737088 | bytes 23510080 | tf_op jit(solution)/shard_map/last_hidden/pallas_call | solution.py:697
  149.6 11.7 %all-gather.5.cloned.1.call-done.w_out = bf16[3072,768]{1,0:T(8,128)(2,1)} async-done(((bf16[384,768]{1,0:T(8,128)(2,1)}), bf16[3072,768]{1,0:T(8,128)(2,1)}) %all-gather.5.cloned.1.call-update) | async-done | bytes 4718608 | tf_op jit(solution)/shard_map/all_gather | solution.py:1230
  161.3 19.6 %last_backward.1 = (bf16[768,3072]{1,0:T(8,128)(2,1)}, f32[832,768]{1,0:T(8,128)}, f32[4,1,768]{2,1,0:T(1,128)}) custom-call(s32[3]{0:T(128)} %pad_add_fusion.place, bf16[832,768]{1,0:T(8,128)(2,1)} %get-tuple-element.189.low, bf16[832,768]{1,0:T(8,128)(2,1)} %get-tuple-element.185.v, bf16[4,832,768]{2,1,0:T(8,128)(2,1)} %get-tuple-element.190.slope, ...), custom_call_target="tpu_custom_call" | custom-call | flops 11777605632 | bytes 24391680 | tf_op jit(solution)/shard_map/last_backward/pallas_call | solution.py:697
  180.9 12.5 %token_backward.2 = (f32[4,208,768]{2,1,0:T(8,128)}, bf16[4,2,48,256]{3,2,1,0:T(8,128)(2,1)}, bf16[4,2,48,256]{3,2,1,0:T(8,128)(2,1)}, f32[16,768]{1,0:T(8,128)}...) custom-call(s32[3]{0:T(128)} %pad_add_fusion.place, f32[4,4]{1,0:T(4,128)} %copy.67.scale, bf16[4,208,768]{2,1,0:T(8,128)(2,1)} %pad.44.grad, ...), custom_call_target="tpu_custom_call" | custom-call | flops 2415919104 | bytes 19931200 | tf_op jit(solution)/shard_map/token_backward/pallas_call | solution.py:697
  193.4 10.2 %out_weight_grad.1 = (bf16[4,4,96,768]{3,2,1,0:T(8,128)(2,1)}, bf16[4,4,96,768]{3,2,1,0:T(8,128)(2,1)}) custom-call(s32[3]{0:T(128)} %pad_add_fusion.place, bf16[832,768]{1,0:T(8,128)(2,1)} %get-tuple-element.201.low, bf16[4,832,768]{2,1,0:T(8,128)(2,1)} %get-tuple-element.202.hidden), custom_call_target="tpu_custom_call" | custom-call | flops 3925868544 | bytes 11108352 | tf_op jit(solution)/shard_map/out_weight_grad/pallas_call | solution.py:697
  203.9 20.2 %channel_backward.1 = (bf16[4,4,96,768]{3,2,1,0:T(8,128)(2,1)}, bf16[4,4,96,768]{3,2,1,0:T(8,128)(2,1)}, f32[832,768]{1,0:T(8,128)}, f32[4,1,768]{2,1,0:T(1,128)}) custom-call(s32[3]{0:T(128)} %pad_add_fusion.place, bf16[832,768]{1,0:T(8,128)(2,1)} %get-tuple-element.201.low, bf16[832,768]{1,0:T(8,128)(2,1)} %get-tuple-element.167.v, ...), custom_call_target="tpu_custom_call" | custom-call | flops 11777605632 | bytes 25571328 | tf_op jit(solution)/shard_map/channel_backward/pallas_call | solution.py:697
  224.5 2.4 slice_add_fusion.2
  226.9 2.8 collective-permute-start.20
  229.7 2.2 collective-permute-start.19
  231.9 12.6 %token_backward.3 = (f32[4,208,768]{2,1,0:T(8,128)}, bf16[4,4,48,256]{3,2,1,0:T(8,128)(2,1)}, bf16[4,4,48,256]{3,2,1,0:T(8,128)(2,1)}, f32[32,768]{1,0:T(8,128)}) custom-call(s32[3]{0:T(128)} %pad_add_fusion.place, f32[4,4]{1,0:T(4,128)} %copy.67.scale, f32[4,208,768]{2,1,0:T(8,128)} %get-tuple-element.206.grad, f32[832,768]{1,0:T(8,128)} %get-tuple-element.213.back_v, ...), custom_call_target="tpu_custom_call" | custom-call | flops 2415919104 | bytes 19534912 | tf_op jit(solution)/shard_map/token_backward/pallas_call | solution.py:697
  246.1 2.4 slice_add_fusion
  248.7 1.8 collective-permute-start.21
  250.6 2.3 add_bitcast_fusion.2
  253.1 1.8 collective-permute-start.23
  254.8 10.1 %last_out.1 = bf16[4,208,768]{2,1,0:T(8,128)(2,1)} custom-call(s32[3]{0:T(128)} %pad_add_fusion.place, f32[4,4]{1,0:T(4,128)} %copy.67.scale, bf16[4,832,768]{2,1,0:T(8,128)(2,1)} %get-tuple-element.231.hidden, f32[4,208,768]{2,1,0:T(8,128)} %get-tuple-element.193.middle, f32[1,768]{1,0:T(1,128)} %get-tuple-element.232.bias, ...), custom_call_target="tpu_custom_call" | custom-call | flops 3925868544 | bytes 13667392 | tf_op jit(solution)/shard_map/last_out/pallas_call | solution.py:697
  265.9 4.6 %collective-permute-done.24 = bf16[2,96,768]{2,1,0:T(8,128)(2,1)} collective-permute-done((bf16[2,96,768]{2,1,0:T(8,128)(2,1)}, bf16[2,96,768]{2,1,0:T(8,128)(2,1)}, u32[]{:S(2)}, u32[]{:S(2)}) %collective-permute-start.24) | collective-permute-done | bytes 294944 | tf_op jit(solution)/shard_map/ppermute | solution.py:1008
  271.6 1.8 bitcast_add_fusion.2
  273.4 1.8 collective-permute-start.29
  275.3 1.8 collective-permute-start.32
  277.1 2.1 add_bitcast_fusion
  279.5 1.7 collective-permute-start.27
  282.8 1.5 collective-permute-start.30
  285.5 3.7 collective-permute-done.31
  289.1 5.8 %collective-permute-done.30 = bf16[96,768]{1,0:T(8,128)(2,1)} collective-permute-done((bf16[96,768]{1,0:T(8,128)(2,1)}, bf16[96,768]{1,0:T(8,128)(2,1)}, u32[]{:S(2)}, u32[]{:S(2)}) %collective-permute-start.30) | collective-permute-done | bytes 147488 | tf_op jit(solution)/shard_map/ppermute | solution.py:1002
  295.0 1.5 bitcast_add_fusion
  296.8 1.9 collective-permute-start.34
  298.6 2.6 collective-permute-start.36
  302.0 1.7 collective-permute-start.39
  304.8 1.3 collective-permute-start.40
  308.9 5.4 %collective-permute-done.35 = bf16[96,768]{1,0:T(8,128)(2,1)S(1)} collective-permute-done((bf16[96,768]{1,0:T(8,128)(2,1)S(1)}, bf16[96,768]{1,0:T(8,128)(2,1)S(1)}, u32[]{:S(2)}, u32[]{:S(2)}) %collective-permute-start.35) | collective-permute-done | bytes 147488 | tf_op jit(solution)/shard_map/ppermute | solution.py:1002
  314.3 10.8 %collective-permute-done.38 = bf16[96,768]{1,0:T(8,128)(2,1)S(1)} collective-permute-done((bf16[96,768]{1,0:T(8,128)(2,1)S(1)}, bf16[96,768]{1,0:T(8,128)(2,1)S(1)}, u32[]{:S(2)}, u32[]{:S(2)}) %collective-permute-start.38) | collective-permute-done | bytes 147488 | tf_op jit(solution)/shard_map/ppermute | solution.py:1008
  326.3 1.7 collective-permute-start.48
  328.7 1.1 collective-permute-start.46
  330.9 2.1 collective-permute-start.44
  332.9 2.2 collective-permute-start.52
  335.1 1.3 collective-permute-start.51
  337.2 2.3 collective-permute-done.52
  340.9 2.8 copy.72
  343.7 2.4 copy.73
  346.1 1.2 collective-permute-start.43
  347.3 2.4 collective-permute-done.44
  351.5 3.5 collective-permute-done.42
  355.1 1.2 collective-permute-start.49
  357.7 2.0 add.272.grad_out
  359.7 2.2 add.271.grad_in
  361.9 3.6 finish_last.1
  365.5 3.9 %finish_first.1 = (f32[2,96,3072]{2,1,0:T(8,128)}, f32[2,384,768]{2,1,0:T(8,128)}) custom-call(s32[3]{0:T(128)} %pad_add_fusion.place, bf16[1,96,768]{2,1,0:T(8,128)(2,1)} %bitcast.65.refs_0_, bf16[1,96,768]{2,1,0:T(8,128)(2,1)} %bitcast.147, bf16[1,96,768]{2,1,0:T(8,128)(2,1)} %bitcast.146, ...), custom_call_target="tpu_custom_call", output_to_operand_aliasing={{0}: (9, {}), {1}: (10, {})} | custom-call | bytes 10911744 | tf_op jit(solution)/shard_map/finish_first/pallas_call | solution.py:697
  (225 shorter events, 45.7 us)
Async XLA Ops:
  7.2 122.8 %all-gather.3.cloned.1.call-start = ((), (), s32[]{:S(2)}) async-start(), calls=%async_computation.2 | async-start | bytes 5308416 | tf_op jit(solution)/shard_map/all_gather | solution.py:1229
  14.1 10.0 %collective-permute-start.5 = (bf16[96,768]{1,0:T(8,128)(2,1)S(1)}, bf16[96,768]{1,0:T(8,128)(2,1)}, u32[]{:S(2)}, u32[]{:S(2)}) collective-permute-start(bf16[96,768]{1,0:T(8,128)(2,1)S(1)} %bitcast.133), channel_id=1, source_target_pairs={{0,6},{1,7},{2,4},{3,5},{4,2},{5,3},{6,0},{7,1},{8,14},{9,15},{10,... | collective-permute-start | bytes 442376 | tf_op jit(solution)/shard_map/ppermute | solution.py:1002
  19.2 23.0 %collective-permute-start.4 = (bf16[96,768]{1,0:T(8,128)(2,1)S(1)}, bf16[96,768]{1,0:T(8,128)(2,1)}, u32[]{:S(2)}, u32[]{:S(2)}) collective-permute-start(bf16[96,768]{1,0:T(8,128)(2,1)S(1)} %bitcast.134), channel_id=1, source_target_pairs={{0,4},{1,5},{2,6},{3,7},{4,0},{5,1},{6,2},{7,3},{8,12},{9,13},{10,... | collective-permute-start | bytes 442376 | tf_op jit(solution)/shard_map/ppermute | solution.py:1002
  19.3 23.0 %collective-permute-start.3 = (bf16[96,768]{1,0:T(8,128)(2,1)S(1)}, bf16[96,768]{1,0:T(8,128)(2,1)}, u32[]{:S(2)}, u32[]{:S(2)}) collective-permute-start(bf16[96,768]{1,0:T(8,128)(2,1)S(1)} %bitcast.135), channel_id=1, source_target_pairs={{0,2},{1,3},{2,0},{3,1},{4,6},{5,7},{6,4},{7,5},{8,10},{9,11},{10,... | collective-permute-start | bytes 442376 | tf_op jit(solution)/shard_map/ppermute | solution.py:1002
  22.1 34.9 %collective-permute-start.6 = (bf16[96,3072]{1,0:T(8,128)(2,1)S(1)}, bf16[96,3072]{1,0:T(8,128)(2,1)}, u32[]{:S(2)}, u32[]{:S(2)}) collective-permute-start(bf16[96,3072]{1,0:T(8,128)(2,1)S(1)} %get-tuple-element.323), channel_id=1, source_target_pairs={{0,1},{1,0},{2,3},{3,2},{4,5},{5,4},{6,7},{7,6},{8,9},{9,8},{10,11... | collective-permute-start | bytes 1769480 | tf_op jit(solution)/shard_map/ppermute | solution.py:1005
  23.3 33.7 %collective-permute-start.7 = (bf16[384,768]{1,0:T(8,128)(2,1)}, bf16[384,768]{1,0:T(8,128)(2,1)}, u32[]{:S(2)}, u32[]{:S(2)}) collective-permute-start(bf16[384,768]{1,0:T(8,128)(2,1)} %get-tuple-element.320), channel_id=1, source_target_pairs={{0,1},{1,0},{2,3},{3,2},{4,5},{5,4},{6,7},{7,6},{8,9},{9,8},{10,11... | collective-permute-start | bytes 1769480 | tf_op jit(solution)/shard_map/ppermute | solution.py:1005
  23.8 40.2 %copy-start.35 = (s32[4,2,2]{0,2,1:T(2,128)S(1)}, s32[4,2,2]{0,2,1:T(2,128)}, u32[]{:S(2)}) copy-start(s32[4,2,2]{0,2,1:T(2,128)} %param.18) | copy-start | bytes 196
  23.8 40.9 %copy-start.36 = (bf16[2,196]{1,0:T(2,128)(2,1)S(1)}, bf16[2,196]{1,0:T(2,128)(2,1)}, u32[]{:S(2)}) copy-start(bf16[2,196]{1,0:T(2,128)(2,1)} %param.24) | copy-start | bytes 2356
  23.9 41.7 %copy-start.5 = (bf16[4,196,768]{2,0,1:T(4,128)(2,1)S(1)}, bf16[4,196,768]{2,0,1:T(4,128)(2,1)}, u32[]{:S(2)}) copy-start(bf16[4,196,768]{2,0,1:T(4,128)(2,1)} %param.16) | copy-start | bytes 3612676
  24.1 18.3 %collective-permute-start.2 = (bf16[2,96,768]{2,1,0:T(8,128)(2,1)S(1)}, bf16[2,96,768]{2,1,0:T(8,128)(2,1)S(1)}, u32[]{:S(2)}, u32[]{:S(2)}) collective-permute-start(bf16[2,96,768]{2,1,0:T(8,128)(2,1)S(1)} %pad_maximum_fusion.2), channel_id=1, source_target_pairs={{0,6},{1,7},{2,4},{3,5},{4,2},{5,3},{6,0},{7,1},{8,14},{9,15},{10,... | collective-permute-start | bytes 884744 | tf_op jit(solution)/shard_map/ppermute | solution.py:1002
  42.3 14.7 %collective-permute-start.1 = (bf16[2,96,768]{2,1,0:T(8,128)(2,1)S(1)}, bf16[2,96,768]{2,1,0:T(8,128)(2,1)S(1)}, u32[]{:S(2)}, u32[]{:S(2)}) collective-permute-start(bf16[2,96,768]{2,1,0:T(8,128)(2,1)S(1)} %pad_maximum_fusion.2), channel_id=1, source_target_pairs={{0,4},{1,5},{2,6},{3,7},{4,0},{5,1},{6,2},{7,3},{8,12},{9,13},{10,... | collective-permute-start | bytes 884744 | tf_op jit(solution)/shard_map/ppermute | solution.py:1002
  42.3 14.7 %collective-permute-start = (bf16[2,96,768]{2,1,0:T(8,128)(2,1)S(1)}, bf16[2,96,768]{2,1,0:T(8,128)(2,1)S(1)}, u32[]{:S(2)}, u32[]{:S(2)}) collective-permute-start(bf16[2,96,768]{2,1,0:T(8,128)(2,1)S(1)} %pad_maximum_fusion.2), channel_id=1, source_target_pairs={{0,2},{1,3},{2,0},{3,1},{4,6},{5,7},{6,4},{7,5},{8,10},{9,11},{10,... | collective-permute-start | bytes 884744 | tf_op jit(solution)/shard_map/ppermute | solution.py:1002
  57.1 104.2 %all-gather.5.cloned.1.call-start = ((), (), s32[]{:S(2)}) async-start(), calls=%async_computation.3 | async-start | bytes 5308416 | tf_op jit(solution)/shard_map/all_gather | solution.py:1230
  57.8 166.3 %reduce-scatter.3.cloned.1.call-start = ((), (), s32[]{:S(2)}) async-start(), calls=%async_computation.4 | async-start | bytes 5308416 | tf_op jit(solution)/shard_map/reduce_scatter | solution.py:1260
  58.9 8.5 %collective-permute-start.8 = (bf16[3,2,96,768]{3,2,1,0:T(8,128)(2,1)S(1)}, bf16[3,2,96,768]{3,2,1,0:T(8,128)(2,1)}, u32[]{:S(2)}, u32[]{:S(2)}) collective-permute-start(bf16[3,2,96,768]{3,2,1,0:T(8,128)(2,1)S(1)} %pad_maximum_fusion.rest_4_), channel_id=1, source_target_pairs={{0,1},{1,0},{2,3},{3,2},{4,5},{5,4},{6,7},{7,6},{8,9},{9,8},{10,11... | collective-permute-start | bytes 2654216 | tf_op jit(solution)/shard_map/ppermute | solution.py:1005
  59.0 22.2 %collective-permute-start.11 = (bf16[3,2,96,768]{3,2,1,0:T(8,128)(2,1)S(1)}, bf16[3,2,96,768]{3,2,1,0:T(8,128)(2,1)}, u32[]{:S(2)}, u32[]{:S(2)}) collective-permute-start(bf16[3,2,96,768]{3,2,1,0:T(8,128)(2,1)S(1)} %pad_maximum_fusion.rest_4_), channel_id=1, source_target_pairs={{0,16},{8,24},{16,0},{24,8},{1,17},{9,25},{17,1},{25,9},{2,18},{10... | collective-permute-start | bytes 2654216 | tf_op jit(solution)/shard_map/ppermute | solution.py:1008
  60.6 21.8 %collective-permute-start.10 = (bf16[3,2,96,768]{3,2,1,0:T(8,128)(2,1)S(1)}, bf16[3,2,96,768]{3,2,1,0:T(8,128)(2,1)}, u32[]{:S(2)}, u32[]{:S(2)}) collective-permute-start(bf16[3,2,96,768]{3,2,1,0:T(8,128)(2,1)S(1)} %pad_maximum_fusion.rest_4_), channel_id=1, source_target_pairs={{0,8},{8,0},{16,24},{24,16},{1,9},{9,1},{17,25},{25,17},{2,10},{10... | collective-permute-start | bytes 2654216 | tf_op jit(solution)/shard_map/ppermute | solution.py:1008
  63.2 4.2 %collective-permute-start.9 = (bf16[4,96,768]{2,1,0:T(8,128)(2,1)S(1)}, bf16[4,96,768]{2,1,0:T(8,128)(2,1)S(1)}, u32[]{:S(2)}, u32[]{:S(2)}) collective-permute-start(bf16[4,96,768]{2,1,0:T(8,128)(2,1)S(1)} %pad_maximum_fusion.1.own), channel_id=1, source_target_pairs={{0,1},{1,0},{2,3},{3,2},{4,5},{5,4},{6,7},{7,6},{8,9},{9,8},{10,11... | collective-permute-start | bytes 1769480 | tf_op jit(solution)/shard_map/ppermute | solution.py:1005
  82.4 15.0 %collective-permute-start.15 = (bf16[3,2,96,768]{3,2,1,0:T(8,128)(2,1)}, bf16[3,2,96,768]{3,2,1,0:T(8,128)(2,1)S(1)}, u32[]{:S(2)}, u32[]{:S(2)}) collective-permute-start(bf16[3,2,96,768]{3,2,1,0:T(8,128)(2,1)} %collective-permute-done.11.rest_6_), channel_id=1, source_target_pairs={{0,1},{1,0},{2,3},{3,2},{4,5},{5,4},{6,7},{7,6},{8,9},{9,8},{10,11... | collective-permute-start | bytes 2654216 | tf_op jit(solution)/shard_map/ppermute | solution.py:1005
  82.4 15.0 %collective-permute-start.14 = (bf16[3,2,96,768]{3,2,1,0:T(8,128)(2,1)}, bf16[3,2,96,768]{3,2,1,0:T(8,128)(2,1)S(1)}, u32[]{:S(2)}, u32[]{:S(2)}) collective-permute-start(bf16[3,2,96,768]{3,2,1,0:T(8,128)(2,1)} %collective-permute-done.10.rest_5_), channel_id=1, source_target_pairs={{0,1},{1,0},{2,3},{3,2},{4,5},{5,4},{6,7},{7,6},{8,9},{9,8},{10,11... | collective-permute-start | bytes 2654216 | tf_op jit(solution)/shard_map/ppermute | solution.py:1005
  85.0 12.1 %collective-permute-start.13 = (bf16[3,1,96,768]{3,2,1,0:T(8,128)(2,1)S(1)}, bf16[3,1,96,768]{3,2,1,0:T(8,128)(2,1)S(1)}, u32[]{:S(2)}, u32[]{:S(2)}) collective-permute-start(bf16[3,1,96,768]{3,2,1,0:T(8,128)(2,1)S(1)} %slice.190), channel_id=1, source_target_pairs={{0,16},{8,24},{16,0},{24,8},{1,17},{9,25},{17,1},{25,9},{2,18},{10... | collective-permute-start | bytes 1327112 | tf_op jit(solution)/shard_map/ppermute | solution.py:1008
  85.6 11.8 %collective-permute-start.12 = (bf16[3,1,96,768]{3,2,1,0:T(8,128)(2,1)S(1)}, bf16[3,1,96,768]{3,2,1,0:T(8,128)(2,1)S(1)}, u32[]{:S(2)}, u32[]{:S(2)}) collective-permute-start(bf16[3,1,96,768]{3,2,1,0:T(8,128)(2,1)S(1)} %slice.189), channel_id=1, source_target_pairs={{0,8},{8,0},{16,24},{24,16},{1,9},{9,1},{17,25},{25,17},{2,10},{10... | collective-permute-start | bytes 1327112 | tf_op jit(solution)/shard_map/ppermute | solution.py:1008
  97.5 2.7 collective-permute-start.16
  149.3 136.1 %reduce-scatter.5.cloned.1.call-start = ((), (), s32[]{:S(2)}) async-start(), calls=%async_computation.5 | async-start | bytes 5308416 | tf_op jit(solution)/shard_map/reduce_scatter | solution.py:1262
  203.6 20.5 %collective-permute-start.17 = (bf16[4,4,96,768]{3,2,1,0:T(8,128)(2,1)}, bf16[4,4,96,768]{3,2,1,0:T(8,128)(2,1)}, u32[]{:S(2)}, u32[]{:S(2)}) collective-permute-start(bf16[4,4,96,768]{3,2,1,0:T(8,128)(2,1)} %get-tuple-element.212), channel_id=1, source_target_pairs={{0,1},{1,0},{2,3},{3,2},{4,5},{5,4},{6,7},{7,6},{8,9},{9,8},{10,11... | collective-permute-start | bytes 7077896 | tf_op jit(solution)/shard_map/ppermute | solution.py:1005
  203.9 20.6 %copy-start.2 = (bf16[4,4,96,768]{3,2,1,0:T(8,128)(2,1)S(1)}, bf16[4,4,96,768]{3,2,1,0:T(8,128)(2,1)}, u32[]{:S(2)}) copy-start(bf16[4,4,96,768]{3,2,1,0:T(8,128)(2,1)} %get-tuple-element.229) | copy-start | bytes 7077892
  224.1 21.4 %collective-permute-start.18 = (bf16[4,4,96,768]{3,2,1,0:T(8,128)(2,1)}, bf16[4,4,96,768]{3,2,1,0:T(8,128)(2,1)}, u32[]{:S(2)}, u32[]{:S(2)}) collective-permute-start(bf16[4,4,96,768]{3,2,1,0:T(8,128)(2,1)} %get-tuple-element.228), channel_id=1, source_target_pairs={{0,1},{1,0},{2,3},{3,2},{4,5},{5,4},{6,7},{7,6},{8,9},{9,8},{10,11... | collective-permute-start | bytes 7077896 | tf_op jit(solution)/shard_map/ppermute | solution.py:1005
  226.9 17.7 %collective-permute-start.20 = (bf16[2,2,96,768]{3,2,1,0:T(8,128)(2,1)}, bf16[2,2,96,768]{3,2,1,0:T(8,128)(2,1)S(1)}, u32[]{:S(2)}, u32[]{:S(2)}) collective-permute-start(bf16[2,2,96,768]{3,2,1,0:T(8,128)(2,1)} %get-tuple-element.318), channel_id=1, source_target_pairs={{0,16},{8,24},{16,0},{24,8},{1,17},{9,25},{17,1},{25,9},{2,18},{10... | collective-permute-start | bytes 1769480 | tf_op jit(solution)/shard_map/ppermute | solution.py:1008
  229.7 15.9 %collective-permute-start.19 = (bf16[2,2,96,768]{3,2,1,0:T(8,128)(2,1)}, bf16[2,2,96,768]{3,2,1,0:T(8,128)(2,1)S(1)}, u32[]{:S(2)}, u32[]{:S(2)}) collective-permute-start(bf16[2,2,96,768]{3,2,1,0:T(8,128)(2,1)} %get-tuple-element.319), channel_id=1, source_target_pairs={{0,8},{8,0},{16,24},{24,16},{1,9},{9,1},{17,25},{25,17},{2,10},{10... | collective-permute-start | bytes 1769480 | tf_op jit(solution)/shard_map/ppermute | solution.py:1008
  245.6 7.5 %collective-permute-start.26 = (f32[32,768]{1,0:T(8,128)}, f32[32,768]{1,0:T(8,128)S(1)}, u32[]{:S(2)}, u32[]{:S(2)}) collective-permute-start(f32[32,768]{1,0:T(8,128)} %get-tuple-element.238), channel_id=1, source_target_pairs={{0,1},{1,0},{2,3},{3,2},{4,5},{5,4},{6,7},{7,6},{8,9},{9,8},{10,11... | collective-permute-start | bytes 294920 | tf_op jit(solution)/shard_map/ppermute | solution.py:1173
  245.6 24.9 %collective-permute-start.25 = (bf16[4,4,48,256]{3,2,1,0:T(8,128)(2,1)}, bf16[4,4,48,256]{3,2,1,0:T(8,128)(2,1)S(1)}, u32[]{:S(2)}, u32[]{:S(2)}) collective-permute-start(bf16[4,4,48,256]{3,2,1,0:T(8,128)(2,1)} %get-tuple-element.237), channel_id=1, source_target_pairs={{0,1},{1,0},{2,3},{3,2},{4,5},{5,4},{6,7},{7,6},{8,9},{9,8},{10,11... | collective-permute-start | bytes 1179656 | tf_op jit(solution)/shard_map/ppermute | solution.py:1005
  248.4 22.0 %collective-permute-start.22 = (bf16[2,2,96,768]{3,2,1,0:T(8,128)(2,1)}, bf16[2,2,96,768]{3,2,1,0:T(8,128)(2,1)S(1)}, u32[]{:S(2)}, u32[]{:S(2)}) collective-permute-start(bf16[2,2,96,768]{3,2,1,0:T(8,128)(2,1)} %get-tuple-element.316), channel_id=1, source_target_pairs={{0,16},{8,24},{16,0},{24,8},{1,17},{9,25},{17,1},{25,9},{2,18},{10... | collective-permute-start | bytes 1769480 | tf_op jit(solution)/shard_map/ppermute | solution.py:1008
  248.7 21.8 %collective-permute-start.21 = (bf16[2,2,96,768]{3,2,1,0:T(8,128)(2,1)}, bf16[2,2,96,768]{3,2,1,0:T(8,128)(2,1)S(1)}, u32[]{:S(2)}, u32[]{:S(2)}) collective-permute-start(bf16[2,2,96,768]{3,2,1,0:T(8,128)(2,1)} %get-tuple-element.317), channel_id=1, source_target_pairs={{0,8},{8,0},{16,24},{24,16},{1,9},{9,1},{17,25},{25,17},{2,10},{10... | collective-permute-start | bytes 1769480 | tf_op jit(solution)/shard_map/ppermute | solution.py:1008
  252.9 17.6 %collective-permute-start.24 = (bf16[2,96,768]{2,1,0:T(8,128)(2,1)}, bf16[2,96,768]{2,1,0:T(8,128)(2,1)}, u32[]{:S(2)}, u32[]{:S(2)}) collective-permute-start(bf16[2,96,768]{2,1,0:T(8,128)(2,1)} %get-tuple-element.314), channel_id=1, source_target_pairs={{0,8},{8,0},{16,24},{24,16},{1,9},{9,1},{17,25},{25,17},{2,10},{10... | collective-permute-start | bytes 884744 | tf_op jit(solution)/shard_map/ppermute | solution.py:1008
  253.1 17.4 %collective-permute-start.23 = (bf16[2,96,768]{2,1,0:T(8,128)(2,1)}, bf16[2,96,768]{2,1,0:T(8,128)(2,1)}, u32[]{:S(2)}, u32[]{:S(2)}) collective-permute-start(bf16[2,96,768]{2,1,0:T(8,128)(2,1)} %get-tuple-element.315), channel_id=1, source_target_pairs={{0,16},{8,24},{16,0},{24,8},{1,17},{9,25},{17,1},{25,9},{2,18},{10... | collective-permute-start | bytes 884744 | tf_op jit(solution)/shard_map/ppermute | solution.py:1008
  271.3 10.6 %collective-permute-start.33 = (f32[32,768]{1,0:T(8,128)S(1)}, f32[32,768]{1,0:T(8,128)S(1)}, u32[]{:S(2)}, u32[]{:S(2)}) collective-permute-start(f32[32,768]{1,0:T(8,128)S(1)} %add.229), channel_id=1, source_target_pairs={{0,2},{1,3},{2,0},{3,1},{4,6},{5,7},{6,4},{7,5},{8,10},{9,11},{10,... | collective-permute-start | bytes 294920 | tf_op jit(solution)/shard_map/ppermute | solution.py:1173
  273.4 8.7 %collective-permute-start.29 = (bf16[96,768]{1,0:T(8,128)(2,1)S(1)}, bf16[96,768]{1,0:T(8,128)(2,1)S(1)}, u32[]{:S(2)}, u32[]{:S(2)}) collective-permute-start(bf16[96,768]{1,0:T(8,128)(2,1)S(1)} %slice_bitcast_fusion.11), channel_id=1, source_target_pairs={{0,2},{1,3},{2,0},{3,1},{4,6},{5,7},{6,4},{7,5},{8,10},{9,11},{10,... | collective-permute-start | bytes 442376 | tf_op jit(solution)/shard_map/ppermute | solution.py:1002
  275.3 19.7 %collective-permute-start.32 = (bf16[4,4,48,256]{3,2,1,0:T(8,128)(2,1)S(1)}, bf16[4,4,48,256]{3,2,1,0:T(8,128)(2,1)S(1)}, u32[]{:S(2)}, u32[]{:S(2)}) collective-permute-start(bf16[4,4,48,256]{3,2,1,0:T(8,128)(2,1)S(1)} %add.244), channel_id=1, source_target_pairs={{0,8},{8,0},{16,24},{24,16},{1,9},{9,1},{17,25},{25,17},{2,10},{10... | collective-permute-start | bytes 1179656 | tf_op jit(solution)/shard_map/ppermute | solution.py:1008
  279.2 15.8 %collective-permute-start.28 = (bf16[2,96,768]{2,1,0:T(8,128)(2,1)}, bf16[2,96,768]{2,1,0:T(8,128)(2,1)}, u32[]{:S(2)}, u32[]{:S(2)}) collective-permute-start(bf16[2,96,768]{2,1,0:T(8,128)(2,1)} %get-tuple-element.312), channel_id=1, source_target_pairs={{0,8},{8,0},{16,24},{24,16},{1,9},{9,1},{17,25},{25,17},{2,10},{10... | collective-permute-start | bytes 884744 | tf_op jit(solution)/shard_map/ppermute | solution.py:1008
  279.5 15.5 %collective-permute-start.27 = (bf16[2,96,768]{2,1,0:T(8,128)(2,1)}, bf16[2,96,768]{2,1,0:T(8,128)(2,1)}, u32[]{:S(2)}, u32[]{:S(2)}) collective-permute-start(bf16[2,96,768]{2,1,0:T(8,128)(2,1)} %get-tuple-element.313), channel_id=1, source_target_pairs={{0,16},{8,24},{16,0},{24,8},{1,17},{9,25},{17,1},{25,9},{2,18},{10... | collective-permute-start | bytes 884744 | tf_op jit(solution)/shard_map/ppermute | solution.py:1008
  281.9 7.3 %collective-permute-start.31 = (bf16[96,768]{1,0:T(8,128)(2,1)}, bf16[96,768]{1,0:T(8,128)(2,1)}, u32[]{:S(2)}, u32[]{:S(2)}) collective-permute-start(bf16[96,768]{1,0:T(8,128)(2,1)} %get-tuple-element.331), channel_id=1, source_target_pairs={{0,6},{1,7},{2,4},{3,5},{4,2},{5,3},{6,0},{7,1},{8,14},{9,15},{10,... | collective-permute-start | bytes 442376 | tf_op jit(solution)/shard_map/ppermute | solution.py:1002
  282.8 12.2 %collective-permute-start.30 = (bf16[96,768]{1,0:T(8,128)(2,1)}, bf16[96,768]{1,0:T(8,128)(2,1)}, u32[]{:S(2)}, u32[]{:S(2)}) collective-permute-start(bf16[96,768]{1,0:T(8,128)(2,1)} %get-tuple-element.332), channel_id=1, source_target_pairs={{0,4},{1,5},{2,6},{3,7},{4,0},{5,1},{6,2},{7,3},{8,12},{9,13},{10,... | collective-permute-start | bytes 442376 | tf_op jit(solution)/shard_map/ppermute | solution.py:1002
  285.4 20.7 %copy-start.27 = (bf16[96,768]{1,0:T(8,128)(2,1)S(1)}, bf16[96,768]{1,0:T(8,128)(2,1)}, u32[]{:S(2)}) copy-start(bf16[96,768]{1,0:T(8,128)(2,1)} %copy-done.26) | copy-start | bytes 442372
  285.4 23.3 %copy-start = (f32[4,208,768]{2,1,0:T(8,128)S(1)}, f32[4,208,768]{2,1,0:T(8,128)}, u32[]{:S(2)}) copy-start(f32[4,208,768]{2,1,0:T(8,128)} %get-tuple-element.250) | copy-start | bytes 7667716
  296.5 8.3 %collective-permute-start.41 = (f32[32,768]{1,0:T(8,128)S(1)}, f32[32,768]{1,0:T(8,128)S(1)}, u32[]{:S(2)}, u32[]{:S(2)}) collective-permute-start(f32[32,768]{1,0:T(8,128)S(1)} %add.245), channel_id=1, source_target_pairs={{0,4},{1,5},{2,6},{3,7},{4,0},{5,1},{6,2},{7,3},{8,12},{9,13},{10,... | collective-permute-start | bytes 294920 | tf_op jit(solution)/shard_map/ppermute | solution.py:1173
  296.8 10.5 %collective-permute-start.34 = (bf16[96,768]{1,0:T(8,128)(2,1)S(1)}, bf16[96,768]{1,0:T(8,128)(2,1)S(1)}, u32[]{:S(2)}, u32[]{:S(2)}) collective-permute-start(bf16[96,768]{1,0:T(8,128)(2,1)S(1)} %slice_bitcast_fusion.8), channel_id=1, source_target_pairs={{0,2},{1,3},{2,0},{3,1},{4,6},{5,7},{6,4},{7,5},{8,10},{9,11},{10,... | collective-permute-start | bytes 442376 | tf_op jit(solution)/shard_map/ppermute | solution.py:1002
  298.6 9.5 %collective-permute-start.36 = (bf16[96,768]{1,0:T(8,128)(2,1)S(1)}, bf16[96,768]{1,0:T(8,128)(2,1)S(1)}, u32[]{:S(2)}, u32[]{:S(2)}) collective-permute-start(bf16[96,768]{1,0:T(8,128)(2,1)S(1)} %get-tuple-element.329), channel_id=1, source_target_pairs={{0,6},{1,7},{2,4},{3,5},{4,2},{5,3},{6,0},{7,1},{8,14},{9,15},{10,... | collective-permute-start | bytes 442376 | tf_op jit(solution)/shard_map/ppermute | solution.py:1002
  301.2 23.9 %collective-permute-start.37 = (bf16[4,4,48,256]{3,2,1,0:T(8,128)(2,1)S(1)}, bf16[4,4,48,256]{3,2,1,0:T(8,128)(2,1)S(1)}, u32[]{:S(2)}, u32[]{:S(2)}) collective-permute-start(bf16[4,4,48,256]{3,2,1,0:T(8,128)(2,1)S(1)} %add.254), channel_id=1, source_target_pairs={{0,16},{8,24},{16,0},{24,8},{1,17},{9,25},{17,1},{25,9},{2,18},{10... | collective-permute-start | bytes 1179656 | tf_op jit(solution)/shard_map/ppermute | solution.py:1008
  302.0 23.1 %collective-permute-start.39 = (bf16[96,3072]{1,0:T(8,128)(2,1)S(1)}, bf16[96,3072]{1,0:T(8,128)(2,1)S(1)}, u32[]{:S(2)}, u32[]{:S(2)}) collective-permute-start(bf16[96,3072]{1,0:T(8,128)(2,1)S(1)} %copy-done.16), channel_id=1, source_target_pairs={{0,8},{8,0},{16,24},{24,16},{1,9},{9,1},{17,25},{25,17},{2,10},{10... | collective-permute-start | bytes 1769480 | tf_op jit(solution)/shard_map/ppermute | solution.py:1008
  304.8 20.2 %collective-permute-start.40 = (bf16[1,768,384]{2,1,0:T(8,128)(2,1)S(1)}, bf16[1,768,384]{2,1,0:T(8,128)(2,1)S(1)}, u32[]{:S(2)}, u32[]{:S(2)}) collective-permute-start(bf16[1,768,384]{2,1,0:T(8,128)(2,1)S(1)} %copy-done.15), channel_id=1, source_target_pairs={{0,16},{8,24},{16,0},{24,8},{1,17},{9,25},{17,1},{25,9},{2,18},{10... | collective-permute-start | bytes 1769480 | tf_op jit(solution)/shard_map/ppermute | solution.py:1008
  307.2 29.2 %copy-start.4 = (bf16[96,768]{1,0:T(8,128)(2,1)}, bf16[96,768]{1,0:T(8,128)(2,1)S(1)}, u32[]{:S(2)}) copy-start(bf16[96,768]{1,0:T(8,128)(2,1)S(1)} %fusion.5) | copy-start | bytes 442372
  307.3 7.1 %collective-permute-start.35 = (bf16[96,768]{1,0:T(8,128)(2,1)S(1)}, bf16[96,768]{1,0:T(8,128)(2,1)S(1)}, u32[]{:S(2)}, u32[]{:S(2)}) collective-permute-start(bf16[96,768]{1,0:T(8,128)(2,1)S(1)} %get-tuple-element.330), channel_id=1, source_target_pairs={{0,4},{1,5},{2,6},{3,7},{4,0},{5,1},{6,2},{7,3},{8,12},{9,13},{10,... | collective-permute-start | bytes 442376 | tf_op jit(solution)/shard_map/ppermute | solution.py:1002
  308.1 17.0 %collective-permute-start.38 = (bf16[96,768]{1,0:T(8,128)(2,1)S(1)}, bf16[96,768]{1,0:T(8,128)(2,1)S(1)}, u32[]{:S(2)}, u32[]{:S(2)}) collective-permute-start(bf16[96,768]{1,0:T(8,128)(2,1)S(1)} %fusion.5), channel_id=1, source_target_pairs={{0,16},{8,24},{16,0},{24,8},{1,17},{9,25},{17,1},{25,9},{2,18},{10... | collective-permute-start | bytes 442376 | tf_op jit(solution)/shard_map/ppermute | solution.py:1008
  326.3 6.6 %collective-permute-start.48 = (f32[32,768]{1,0:T(8,128)S(1)}, f32[32,768]{1,0:T(8,128)S(1)}, u32[]{:S(2)}, u32[]{:S(2)}) collective-permute-start(f32[32,768]{1,0:T(8,128)S(1)} %add.258), channel_id=1, source_target_pairs={{0,8},{8,0},{16,24},{24,16},{1,9},{9,1},{17,25},{25,17},{2,10},{10... | collective-permute-start | bytes 294920 | tf_op jit(solution)/shard_map/ppermute | solution.py:1173
  328.7 6.4 %collective-permute-start.50 = (bf16[4,48,256]{2,1,0:T(8,128)(2,1)S(1)}, bf16[4,48,256]{2,1,0:T(8,128)(2,1)S(1)}, u32[]{:S(2)}, u32[]{:S(2)}) collective-permute-start(bf16[4,48,256]{2,1,0:T(8,128)(2,1)S(1)} %get-tuple-element.326), channel_id=1, source_target_pairs={{0,2},{1,3},{2,0},{3,1},{4,6},{5,7},{6,4},{7,5},{8,10},{9,11},{10,... | collective-permute-start | bytes 294920 | tf_op jit(solution)/shard_map/ppermute | solution.py:1002
  328.7 26.4 %collective-permute-start.46 = (bf16[96,3072]{1,0:T(8,128)(2,1)}, bf16[96,3072]{1,0:T(8,128)(2,1)}, u32[]{:S(2)}, u32[]{:S(2)}) collective-permute-start(bf16[96,3072]{1,0:T(8,128)(2,1)} %add.262), channel_id=1, source_target_pairs={{0,16},{8,24},{16,0},{24,8},{1,17},{9,25},{17,1},{25,9},{2,18},{10... | collective-permute-start | bytes 1769480 | tf_op jit(solution)/shard_map/ppermute | solution.py:1008
  329.8 25.2 %collective-permute-start.47 = (bf16[1,768,384]{2,1,0:T(8,128)(2,1)S(1)}, bf16[1,768,384]{2,1,0:T(8,128)(2,1)}, u32[]{:S(2)}, u32[]{:S(2)}) collective-permute-start(bf16[1,768,384]{2,1,0:T(8,128)(2,1)S(1)} %add.263), channel_id=1, source_target_pairs={{0,8},{8,0},{16,24},{24,16},{1,9},{9,1},{17,25},{25,17},{2,10},{10... | collective-permute-start | bytes 1769480 | tf_op jit(solution)/shard_map/ppermute | solution.py:1008
  330.9 18.8 %collective-permute-start.44 = (bf16[96,768]{1,0:T(8,128)(2,1)}, bf16[96,768]{1,0:T(8,128)(2,1)}, u32[]{:S(2)}, u32[]{:S(2)}) collective-permute-start(bf16[96,768]{1,0:T(8,128)(2,1)} %fusion.2), channel_id=1, source_target_pairs={{0,24},{8,16},{16,8},{24,0},{1,25},{9,17},{17,9},{25,1},{2,26},{10... | collective-permute-start | bytes 442376 | tf_op jit(solution)/shard_map/ppermute | solution.py:1008
  332.9 6.5 %collective-permute-start.52 = (bf16[4,48,256]{2,1,0:T(8,128)(2,1)S(1)}, bf16[4,48,256]{2,1,0:T(8,128)(2,1)S(1)}, u32[]{:S(2)}, u32[]{:S(2)}) collective-permute-start(bf16[4,48,256]{2,1,0:T(8,128)(2,1)S(1)} %get-tuple-element.327), channel_id=1, source_target_pairs={{0,6},{1,7},{2,4},{3,5},{4,2},{5,3},{6,0},{7,1},{8,14},{9,15},{10,... | collective-permute-start | bytes 294920 | tf_op jit(solution)/shard_map/ppermute | solution.py:1002
  335.1 11.0 %collective-permute-start.51 = (bf16[4,48,256]{2,1,0:T(8,128)(2,1)}, bf16[4,48,256]{2,1,0:T(8,128)(2,1)}, u32[]{:S(2)}, u32[]{:S(2)}) collective-permute-start(bf16[4,48,256]{2,1,0:T(8,128)(2,1)} %get-tuple-element.328), channel_id=1, source_target_pairs={{0,4},{1,5},{2,6},{3,7},{4,0},{5,1},{6,2},{7,3},{8,12},{9,13},{10,... | collective-permute-start | bytes 294920 | tf_op jit(solution)/shard_map/ppermute | solution.py:1002
  340.1 15.0 %collective-permute-start.45 = (bf16[2,96,768]{2,1,0:T(8,128)(2,1)}, bf16[2,96,768]{2,1,0:T(8,128)(2,1)}, u32[]{:S(2)}, u32[]{:S(2)}) collective-permute-start(bf16[2,96,768]{2,1,0:T(8,128)(2,1)} %pad_maximum_fusion.3), channel_id=1, source_target_pairs={{0,8},{8,0},{16,24},{24,16},{1,9},{9,1},{17,25},{25,17},{2,10},{10... | collective-permute-start | bytes 884744 | tf_op jit(solution)/shard_map/ppermute | solution.py:1008
  346.1 5.4 %collective-permute-start.43 = (bf16[96,768]{1,0:T(8,128)(2,1)}, bf16[96,768]{1,0:T(8,128)(2,1)S(1)}, u32[]{:S(2)}, u32[]{:S(2)}) collective-permute-start(bf16[96,768]{1,0:T(8,128)(2,1)} %fusion.2), channel_id=1, source_target_pairs={{0,16},{8,24},{16,0},{24,8},{1,17},{9,25},{17,1},{25,9},{2,18},{10... | collective-permute-start | bytes 442376 | tf_op jit(solution)/shard_map/ppermute | solution.py:1008
  349.7 5.4 %collective-permute-start.42 = (bf16[96,768]{1,0:T(8,128)(2,1)}, bf16[96,768]{1,0:T(8,128)(2,1)S(1)}, u32[]{:S(2)}, u32[]{:S(2)}) collective-permute-start(bf16[96,768]{1,0:T(8,128)(2,1)} %fusion.2), channel_id=1, source_target_pairs={{0,8},{8,0},{16,24},{24,16},{1,9},{9,1},{17,25},{25,17},{2,10},{10... | collective-permute-start | bytes 442376 | tf_op jit(solution)/shard_map/ppermute | solution.py:1008
  355.1 14.3 %collective-permute-start.49 = (f32[32,768]{1,0:T(8,128)S(1)}, f32[32,768]{1,0:T(8,128)S(1)}, u32[]{:S(2)}, u32[]{:S(2)}) collective-permute-start(f32[32,768]{1,0:T(8,128)S(1)} %add.264), channel_id=1, source_target_pairs={{0,16},{8,24},{16,0},{24,8},{1,17},{9,25},{17,1},{25,9},{2,18},{10... | collective-permute-start | bytes 294920 | tf_op jit(solution)/shard_map/ppermute | solution.py:1173
  (33 other events, 214.8 us)
Sparse Core Ops, SparseCore 0:
  57.2 51.8 all-gather.2
  110.7 50.5 all-gather.4
  163.6 53.7 reduce-scatter.2
  219.5 53.2 reduce-scatter.4

commit v4 on v3

--- a/solution.py
+++ b/solution.py
@@ -656,9 +656,9 @@
     back_out[...] += dot(pre[...], w_in[j], 1, 1)
 
 
-def finish_last(place, grad_in, grad_out, in_out, out_out):
-    in_out[0] = grad_in[...].astype(jnp.float32)
-    out_out[0] = grad_out[0].astype(jnp.float32).T
+def finish_last(place, grad_in, got_in, grad_out, got_out, in_out, out_out):
+    in_out[0] = grad_in[...].astype(jnp.float32) + got_in[...].astype(jnp.float32)
+    out_out[0] = (grad_out[0].astype(jnp.float32) + got_out[0].astype(jnp.float32)).T
 
 
 def finish_first(place, *refs):
@@ -970,8 +970,8 @@
         shapes = (layers, self.block, self.hidden), (layers, self.part // 2, self.width)
         return [(shape, jnp.float32, (1,) + shape[1:], lambda i, s: (layer, 0, 0)) for shape in shapes]
 
-    def finish_last(self, grad_in, grad_out, layer, layers):
-        inputs = [self.fixed(grad_in), self.fixed(grad_out)]
+    def finish_last(self, whole, layer, layers):
+        inputs = [self.fixed(a) for a in (whole.values[0], whole.got0, whole.values[1], whole.got1)]
         return self.run(finish_last, 1, inputs, self.shard_outs(layer, layers), [], 0)
 
     def finish_first(self, parts_in, parts_out, layer, layers, earlier):
@@ -1130,22 +1130,26 @@
 class SumSmall(Held):
     def __init__(self, moves, mine, other):
         super().__init__(moves)
-        self.value, self.theirs = mine, other
+        self.mine, self.theirs = mine, other
 
     def core(self):
         self.bring(got=self.moves.core(self.theirs))
 
+    def along(self):
+        both = self.mine + self.got
+        self.value = both[0]
+        self.bring(**{"z%d" % i: self.moves.along(both[i], i) for i in range(1, self.moves.lines)})
+
     def across(self, bits):
-        self.value = self.value + self.got
+        if bits == 1:
+            parts = [self.value] + [getattr(self, "z%d" % i) for i in range(1, self.moves.lines)]
+            self.value = sum(part.astype(jnp.float32) for part in parts).astype(jnp.bfloat16)
+        else:
+            self.value = self.value + self.got
         self.bring(got=self.moves.across(self.value, bits))
 
-    def along(self):
-        self.value = self.value + self.got
-        self.bring(**{"z%d" % i: self.moves.along(self.value[i], i) for i in range(1, self.moves.lines)})
-
     def total(self):
-        parts = [self.value[0]] + [getattr(self, "z%d" % i) for i in range(1, self.moves.lines)]
-        return sum(part.astype(jnp.float32) for part in parts)
+        return self.value.astype(jnp.float32) + self.got.astype(jnp.float32)
 
 
 class Copies(Held):
@@ -1164,14 +1168,19 @@
 class SumAll(Held):
     def __init__(self, moves, value):
         super().__init__(moves)
-        self.value = value
-        self.steps = [(axis, 2**k) for axis in ("fsdp", "dp") for k in range((lax.axis_size(axis) - 1).bit_length())]
+        self.value, self.bit = value, 1
 
     def step(self):
-        axis, bit = self.steps.pop(0)
-        count = lax.axis_size(axis)
-        got = lax.ppermute(self.value, axis, [(i, i ^ bit) for i in range(count)])
+        count = 2 * self.moves.lines
+        got = lax.ppermute(self.value, "fsdp", [(i, i ^ self.bit) for i in range(count)])
+        self.bit *= 2
         self.bring(value=self.value + got)
+
+    def copies(self):
+        self.bring(**{"q%d" % bits: self.moves.across(self.value, bits) for bits in (1, 2, 3)})
+
+    def total(self):
+        return (self.value + self.q1) + (self.q2 + self.q3)
 
 
 def blocked_shards(
@@ -1287,38 +1296,36 @@
     vector_sum = SumAll(moves, vector)
     vector_sum.step()
     output = kernels.last_out(scale, hid1, mid1, b_cout1, w_cout1)
-    (output,) = settle((sum_in0, sum_out0, sum_tokens, vector_sum), output)
+    output, grad_cin1, grad_cout1 = settle(
+        (sum_in0, sum_out0, sum_tokens, vector_sum), output, grad_cin1, grad_cout1
+    )
 
     sum_in0.second()
     sum_out0.once()
+    sum_tokens.along()
+    vector_sum.step()
+    whole = Copies(moves, grad_cin1, grad_cout1)
+    whole.step(1, 2)
+    output = jnp.swapaxes(output[:, :patches], 0, 1)
+    (output,) = settle((sum_in0, sum_out0, sum_tokens, whole, vector_sum), output)
+
+    sum_in0.once()
     sum_tokens.across(1)
-    vector_sum.step()
-    output = jnp.swapaxes(output[:, :patches], 0, 1)
-    output, grad_cin1, grad_cout1 = settle(
-        (sum_in0, sum_out0, sum_tokens, vector_sum), output, grad_cin1, grad_cout1
-    )
-
-    sum_in0.once()
-    sum_tokens.across(2)
     vector_sum.step()
     share_out0 = Share(moves, sum_out0.total(), 2)
     share_out0.first()
-    whole = Copies(moves, grad_cin1, grad_cout1)
-    whole.step(1, 2)
+    whole.add()
+    whole.step(2, 1)
     input_grad = jnp.swapaxes(grad0[:, :patches], 0, 1)
     (input_grad,) = settle((sum_in0, sum_tokens, share_out0, whole, vector_sum), input_grad)
 
     total = sum_in0.total()
     near = [moves.across(total, bits) for bits in (1, 2, 3)]
     share_out0.second()
-    whole.add()
-    whole.step(2, 1)
-    vector_sum.step()
-    near = settle((share_out0, whole, vector_sum), *near)
-    sum_tokens.along()
-    vector_sum.step()
-    whole.add()
-    finished = kernels.finish_last(*whole.values, 1, layers)
+    sum_tokens.across(2)
+    vector_sum.copies()
+    finished = kernels.finish_last(whole, 1, layers)
+    near = settle((share_out0, sum_tokens, vector_sum), *near)
     parts = [(part[None], 0) for part in [total] + list(near)]
     grad_in, grad_out = kernels.finish_first(parts, share_out0.parts(), 0, layers, finished)
     output, input_grad = jnp.swapaxes(output, 0, 1), jnp.swapaxes(input_grad, 0, 1)
@@ -1328,7 +1335,7 @@
     grad_t_in = jnp.swapaxes(near[:, 0, :, :patches], 1, 2)
     grad_b_in = near[:, 0, :, rows]
     grad_t_out = near[:, 1, :, :patches]
-    sums = vector_sum.value.reshape(layers, 16, width)
+    sums = vector_sum.total().reshape(layers, 16, width)
     me = lax.axis_index("fsdp")
 
     def owned(row):

time: 384 us -> 369 us (0.961)
  waiting for transfers between devices: 96.4 us -> 89.5 us
  other arithmetic: 25.7 us -> 20.3 us
    ppermute x23 -> x26, waiting for transfers between devices: 35 us -> 15.1 us  [across(): lax.ppermute(values, 'dp', [(q, q ^ bits) for q in range(self.copies)])]
    reduce_scatter x1, waiting for transfers between devices: 0.02 us -> 7.19 us  [blocked_shards(): lax.psum_scatter(grad_cin1, 'fsdp', scatter_dimension=0, tiled=True)]
    ppermute x15, waiting for transfers between devices: 47.1 us -> 53.8 us  [along(): lax.ppermute(values, 'fsdp', [(f, f ^ 2 * bits) for f in range(2 * self.l...]
    add x4 -> x2, other arithmetic: 5.37 us -> 0.32 us  [add(): self.values = [self.values[0] + self.got0, self.values[1] + self.got1]]
    ppermute x23 -> x26, starting transfers between devices: 28.5 us -> 33.4 us  [across(): lax.ppermute(values, 'dp', [(q, q ^ bits) for q in range(self.copies)])]
    unnamed x94 -> x84, local copies, waits for them, and re-layouts: 15.8 us -> 14.3 us
  transfers between devices with their start and end apart: 57 -> 58, of which waited for: 21 -> 19; matrix products, arithmetic and copies ran while one was open for 11% -> 9% of each run, Pallas kernels for 40% -> 41%
where the time goes in v4:
time: 369 us; the launch traced here: 365 us
  Pallas kernels  154 us (42%)
  waiting for transfers between devices  89.5 us (24%)
  starting transfers between devices  55.5 us (15%)
  local copies, waits for them, and re-layouts  30.4 us (8%)
  other arithmetic  20.3 us (6%)
  between operations  15.6 us (4%)
    pallas_call x13, Pallas kernels, run(): pl.pallas_call(functools.partial(body, **fixed) if fixed else body, name=...  154 us
    ppermute x15, waiting for transfers between devices, along(): lax.ppermute(values, 'fsdp', [(f, f ^ 2 * bits) for f in range(2 * self.l...  53.8 us
    ppermute x26, starting transfers between devices, across(): lax.ppermute(values, 'dp', [(q, q ^ bits) for q in range(self.copies)])  33.4 us
    ppermute x15, starting transfers between devices, along(): lax.ppermute(values, 'fsdp', [(f, f ^ 2 * bits) for f in range(2 * self.l...  19.4 us
    ppermute x26, waiting for transfers between devices, across(): lax.ppermute(values, 'dp', [(q, q ^ bits) for q in range(self.copies)])  15.1 us
    unnamed x84, local copies, waits for them, and re-layouts  14.3 us
    all_gather x1, waiting for transfers between devices, blocked_shards(): w_cout1 = lax.all_gather(shard_out, 'fsdp', axis=0, tiled=True)  11.7 us
  transfers between devices with their start and end apart: 58, of which 19 were waited for; matrix products, arithmetic and copies ran while one was open for 9% of the time, Pallas kernels for 41%

profile of v4, /device:TPU:0, one launch (start us, length us, event | category | flops | bytes accessed | tf_op | source)
XLA Modules:
  0.0 365.0 jit_solution(18004619079153424702)
XLA Ops:
  14.1 5.1 %collective-permute-start.5 = (bf16[96,768]{1,0:T(8,128)(2,1)S(1)}, bf16[96,768]{1,0:T(8,128)(2,1)}, u32[]{:S(2)}, u32[]{:S(2)}) collective-permute-start(bf16[96,768]{1,0:T(8,128)(2,1)S(1)} %bitcast.133), channel_id=1, source_target_pairs={{0,6},{1,7},{2,4},{3,5},{4,2},{5,3},{6,0},{7,1},{8,14},{9,15},{10,... | collective-permute-start | bytes 442376 | tf_op jit(solution)/shard_map/ppermute | solution.py:1002
  19.9 2.2 slice_bitcast_fusion.19
  22.1 1.1 slice_bitcast_fusion.18
  24.1 3.9 %collective-permute-start.2 = (bf16[2,96,768]{2,1,0:T(8,128)(2,1)S(1)}, bf16[2,96,768]{2,1,0:T(8,128)(2,1)S(1)}, u32[]{:S(2)}, u32[]{:S(2)}) collective-permute-start(bf16[2,96,768]{2,1,0:T(8,128)(2,1)S(1)} %pad_maximum_fusion.2), channel_id=1, source_target_pairs={{0,6},{1,7},{2,4},{3,5},{4,2},{5,3},{6,0},{7,1},{8,14},{9,15},{10,... | collective-permute-start | bytes 884744 | tf_op jit(solution)/shard_map/ppermute | solution.py:1002
  28.0 14.3 %collective-permute-done.4 = bf16[96,768]{1,0:T(8,128)(2,1)} collective-permute-done((bf16[96,768]{1,0:T(8,128)(2,1)S(1)}, bf16[96,768]{1,0:T(8,128)(2,1)}, u32[]{:S(2)}, u32[]{:S(2)}) %collective-permute-start.4) | collective-permute-done | bytes 147488 | tf_op jit(solution)/shard_map/ppermute | solution.py:1002
  42.4 14.6 %collective-permute-done.1 = bf16[2,96,768]{2,1,0:T(8,128)(2,1)S(1)} collective-permute-done((bf16[2,96,768]{2,1,0:T(8,128)(2,1)S(1)}, bf16[2,96,768]{2,1,0:T(8,128)(2,1)S(1)}, u32[]{:S(2)}, u32[]{:S(2)}) %collective-permute-start.1) | collective-permute-done | bytes 294944 | tf_op jit(solution)/shard_map/ppermute | solution.py:1002
  59.0 1.6 collective-permute-start.11
  60.6 1.5 collective-permute-start.10
  62.1 1.1 pad_maximum_fusion.1.own
  65.7 1.1 pad.36.x
  68.3 3.2 unpack_small.1
  71.5 8.9 %token_forward.2 = (bf16[4,256,768]{2,1,0:T(8,128)(2,1)}, bf16[4,384,768]{2,1,0:T(8,128)(2,1)}, bf16[4,384,768]{2,1,0:T(8,128)(2,1)}, f32[4,208,768]{2,1,0:T(8,128)}, bf16[832,768]{1,0:T(8,128)(2,1)}) custom-call(s32[3]{0:T(128)} %pad_add_fusion.place, f32[4,4]{1,0:T(4,128)} %copy.67.scale, bf16[4,208,768]{2,1,0:T(8,128)(2,1)} %pad.36.x, ...), custom_call_target="tpu_custom_call" | custom-call | flops 1207959552 | bytes 11810880 | tf_op jit(solution)/shard_map/token_forward/pallas_call | solution.py:697
  81.2 1.2 collective-permute-done.10.rest_5_
  85.6 1.5 collective-permute-start.12
  87.1 10.1 %collective-permute-done.13 = bf16[3,1,96,768]{3,2,1,0:T(8,128)(2,1)S(1)} collective-permute-done((bf16[3,1,96,768]{3,2,1,0:T(8,128)(2,1)S(1)}, bf16[3,1,96,768]{3,2,1,0:T(8,128)(2,1)S(1)}, u32[]{:S(2)}, u32[]{:S(2)}) %collective-permute-start.13) | collective-permute-done | bytes 442400 | tf_op jit(solution)/shard_map/ppermute | solution.py:1008
  97.7 1.5 pad.44.grad
  101.1 19.7 %first_forward.1 = (bf16[4,832,768]{2,1,0:T(8,128)(2,1)}, bf16[4,832,768]{2,1,0:T(8,128)(2,1)}, f32[4,208,768]{2,1,0:T(8,128)}) custom-call(s32[3]{0:T(128)} %pad_add_fusion.place, f32[4,4]{1,0:T(4,128)} %copy.67.scale, bf16[832,768]{1,0:T(8,128)(2,1)} %get-tuple-element.172.v, f32[4,208,768]{2,1,0:T(8,128)} %get-tuple-element.173.middle, ...), custom_call_target="tpu_custom_call" | custom-call | flops 7851737088 | bytes 27245632 | tf_op jit(solution)/shard_map/first_forward/pallas_call | solution.py:697
  120.9 9.1 %token_forward.3 = (bf16[4,256,768]{2,1,0:T(8,128)(2,1)}, bf16[4,384,768]{2,1,0:T(8,128)(2,1)}, bf16[4,384,768]{2,1,0:T(8,128)(2,1)}, f32[4,208,768]{2,1,0:T(8,128)}, bf16[832,768]{1,0:T(8,128)(2,1)}) custom-call(s32[3]{0:T(128)} %pad_add_fusion.place, f32[4,4]{1,0:T(4,128)} %copy.67.scale, f32[4,208,768]{2,1,0:T(8,128)} %get-tuple-element.183.x, ...), custom_call_target="tpu_custom_call" | custom-call | flops 1207959552 | bytes 13088832 | tf_op jit(solution)/shard_map/token_forward/pallas_call | solution.py:697
  130.0 19.3 %last_hidden.1 = (bf16[4,832,768]{2,1,0:T(8,128)(2,1)}, bf16[4,832,768]{2,1,0:T(8,128)(2,1)}, bf16[8,768,384]{2,1,0:T(8,128)(2,1)}, bf16[832,768]{1,0:T(8,128)(2,1)}, f32[1,768]{1,0:T(1,128)}) custom-call(s32[3]{0:T(128)} %pad_add_fusion.place, f32[4,4]{1,0:T(4,128)} %copy.67.scale, bf16[832,768]{1,0:T(8,128)(2,1)} %get-tuple-element.190.v, ...), custom_call_target="tpu_custom_call" | custom-call | flops 7851737088 | bytes 23510080 | tf_op jit(solution)/shard_map/last_hidden/pallas_call | solution.py:697
  149.6 11.7 %all-gather.5.cloned.1.call-done.w_out = bf16[3072,768]{1,0:T(8,128)(2,1)} async-done(((bf16[384,768]{1,0:T(8,128)(2,1)}), bf16[3072,768]{1,0:T(8,128)(2,1)}) %all-gather.5.cloned.1.call-update) | async-done | bytes 4718608 | tf_op jit(solution)/shard_map/all_gather | solution.py:1239
  161.3 19.6 %last_backward.1 = (bf16[768,3072]{1,0:T(8,128)(2,1)}, f32[832,768]{1,0:T(8,128)}, f32[4,1,768]{2,1,0:T(1,128)}) custom-call(s32[3]{0:T(128)} %pad_add_fusion.place, bf16[832,768]{1,0:T(8,128)(2,1)} %get-tuple-element.194.low, bf16[832,768]{1,0:T(8,128)(2,1)} %get-tuple-element.190.v, bf16[4,832,768]{2,1,0:T(8,128)(2,1)} %get-tuple-element.195.slope, ...), custom_call_target="tpu_custom_call" | custom-call | flops 11777605632 | bytes 24391680 | tf_op jit(solution)/shard_map/last_backward/pallas_call | solution.py:697
  180.9 12.5 %token_backward.2 = (f32[4,208,768]{2,1,0:T(8,128)}, bf16[4,2,48,256]{3,2,1,0:T(8,128)(2,1)}, bf16[4,2,48,256]{3,2,1,0:T(8,128)(2,1)}, f32[16,768]{1,0:T(8,128)}...) custom-call(s32[3]{0:T(128)} %pad_add_fusion.place, f32[4,4]{1,0:T(4,128)} %copy.67.scale, bf16[4,208,768]{2,1,0:T(8,128)(2,1)} %pad.44.grad, ...), custom_call_target="tpu_custom_call" | custom-call | flops 2415919104 | bytes 19931200 | tf_op jit(solution)/shard_map/token_backward/pallas_call | solution.py:697
  193.4 10.2 %out_weight_grad.1 = (bf16[4,4,96,768]{3,2,1,0:T(8,128)(2,1)}, bf16[4,4,96,768]{3,2,1,0:T(8,128)(2,1)}) custom-call(s32[3]{0:T(128)} %pad_add_fusion.place, bf16[832,768]{1,0:T(8,128)(2,1)} %get-tuple-element.206.low, bf16[4,832,768]{2,1,0:T(8,128)(2,1)} %get-tuple-element.207.hidden), custom_call_target="tpu_custom_call" | custom-call | flops 3925868544 | bytes 11108352 | tf_op jit(solution)/shard_map/out_weight_grad/pallas_call | solution.py:697
  203.8 20.2 %channel_backward.1 = (bf16[4,4,96,768]{3,2,1,0:T(8,128)(2,1)}, bf16[4,4,96,768]{3,2,1,0:T(8,128)(2,1)}, f32[832,768]{1,0:T(8,128)}, f32[4,1,768]{2,1,0:T(1,128)}) custom-call(s32[3]{0:T(128)} %pad_add_fusion.place, bf16[832,768]{1,0:T(8,128)(2,1)} %get-tuple-element.206.low, bf16[832,768]{1,0:T(8,128)(2,1)} %get-tuple-element.172.v, ...), custom_call_target="tpu_custom_call" | custom-call | flops 11777605632 | bytes 25571328 | tf_op jit(solution)/shard_map/channel_backward/pallas_call | solution.py:697
  224.5 2.4 slice_add_fusion.2
  226.8 2.8 collective-permute-start.20
  229.7 2.2 collective-permute-start.19
  231.8 12.7 %token_backward.3 = (f32[4,208,768]{2,1,0:T(8,128)}, bf16[4,4,48,256]{3,2,1,0:T(8,128)(2,1)}, bf16[4,4,48,256]{3,2,1,0:T(8,128)(2,1)}, f32[32,768]{1,0:T(8,128)}) custom-call(s32[3]{0:T(128)} %pad_add_fusion.place, f32[4,4]{1,0:T(4,128)} %copy.67.scale, f32[4,208,768]{2,1,0:T(8,128)} %get-tuple-element.211.grad, f32[832,768]{1,0:T(8,128)} %get-tuple-element.218.back_v, ...), custom_call_target="tpu_custom_call" | custom-call | flops 2415919104 | bytes 19534912 | tf_op jit(solution)/shard_map/token_backward/pallas_call | solution.py:697
  246.0 2.4 slice_add_fusion
  248.7 1.8 collective-permute-start.21
  250.5 2.3 add_bitcast_fusion.2
  253.0 1.8 collective-permute-start.23
  254.8 10.2 %last_out.1 = bf16[4,208,768]{2,1,0:T(8,128)(2,1)} custom-call(s32[3]{0:T(128)} %pad_add_fusion.place, f32[4,4]{1,0:T(4,128)} %copy.67.scale, bf16[4,832,768]{2,1,0:T(8,128)(2,1)} %get-tuple-element.236.hidden, f32[4,208,768]{2,1,0:T(8,128)} %get-tuple-element.198.middle, f32[1,768]{1,0:T(1,128)} %get-tuple-element.237.bias, ...), custom_call_target="tpu_custom_call" | custom-call | flops 3925868544 | bytes 13667392 | tf_op jit(solution)/shard_map/last_out/pallas_call | solution.py:697
  265.6 7.2 %reduce-scatter.5.cloned.1.call-done = bf16[96,3072]{1,0:T(8,128)(2,1)} async-done(((bf16[768,3072]{1,0:T(8,128)(2,1)}), bf16[96,3072]{1,0:T(8,128)(2,1)}) %reduce-scatter.5.cloned.1.call-update) | async-done | bytes 589840 | tf_op jit(solution)/shard_map/reduce_scatter | solution.py:1271
  272.9 1.8 bitcast_add_fusion.2
  274.9 1.2 add.241
  276.1 1.3 collective-permute-start.34
  277.3 2.2 collective-permute-start.33
  279.5 1.5 collective-permute-start.35
  281.0 1.5 collective-permute-start.36
  283.6 1.3 collective-permute-start.31
  284.8 6.5 %collective-permute-done.33 = bf16[4,48,256]{2,1,0:T(8,128)(2,1)S(1)} collective-permute-done((bf16[4,48,256]{2,1,0:T(8,128)(2,1)S(1)}, bf16[4,48,256]{2,1,0:T(8,128)(2,1)S(1)}, u32[]{:S(2)}, u32[]{:S(2)}) %collective-permute-start.33) | collective-permute-done | bytes 98336 | tf_op jit(solution)/shard_map/ppermute | solution.py:1002
  291.4 1.1 add_bitcast_fusion
  292.5 3.5 collective-permute-done.32
  296.0 1.6 collective-permute-start.28
  297.6 1.5 collective-permute-start.27
  299.1 1.1 slice_bitcast_fusion.1
  300.2 8.1 %collective-permute-done.30 = bf16[96,768]{1,0:T(8,128)(2,1)S(1)} collective-permute-done((bf16[96,768]{1,0:T(8,128)(2,1)S(1)}, bf16[96,768]{1,0:T(8,128)(2,1)S(1)}, u32[]{:S(2)}, u32[]{:S(2)}) %collective-permute-start.30) | collective-permute-done | bytes 147488 | tf_op jit(solution)/shard_map/ppermute | solution.py:1002
  309.4 1.5 bitcast_add_fusion
  311.0 1.3 collective-permute-start.38
  312.7 1.9 collective-permute-start.44
  314.8 2.5 collective-permute-start.40
  317.4 1.3 collective-permute-done.38
  319.8 2.1 collective-permute-done.40
  321.8 3.2 collective-permute-done.39
  325.0 1.8 collective-permute-done.42
  326.8 2.0 collective-permute-start.53
  328.8 1.6 collective-permute-start.52
  332.6 2.8 collective-permute-start.48
  339.0 2.8 copy.72
  341.8 2.4 copy.73
  344.1 4.2 %finish_last.1 = (f32[2,96,3072]{2,1,0:T(8,128)}, f32[2,384,768]{2,1,0:T(8,128)}) custom-call(s32[3]{0:T(128)} %pad_add_fusion.place, bf16[96,3072]{1,0:T(8,128)(2,1)} %copy-done.2, bf16[96,3072]{1,0:T(8,128)(2,1)} %copy-done.17, bf16[1,768,384]{2,1,0:T(8,128)(2,1)} %copy-done.1, bf16[1,768,384]{2,1,0:T(8,128)(2,1)} %copy-done.18), custom_call_target="tpu_custom_call" | custom-call | bytes 7077888 | tf_op jit(solution)/shard_map/finish_last/pallas_call | solution.py:697
  348.4 1.2 add_add_fusion
  354.2 3.9 %finish_first.1 = (f32[2,96,3072]{2,1,0:T(8,128)}, f32[2,384,768]{2,1,0:T(8,128)}) custom-call(s32[3]{0:T(128)} %pad_add_fusion.place, bf16[1,96,768]{2,1,0:T(8,128)(2,1)} %bitcast.65.refs_0_, bf16[1,96,768]{2,1,0:T(8,128)(2,1)} %bitcast.66.refs_1_, bf16[1,96,768]{2,1,0:T(8,128)(2,1)} %bitcast.67.refs_2_, ...), custom_call_target="tpu_custom_call", output_to_operand_aliasing={{0}: (9, {}), {1}: (10, {})} | custom-call | bytes 10911744 | tf_op jit(solution)/shard_map/finish_first/pallas_call | solution.py:697
  (214 shorter events, 37.8 us)
Async XLA Ops:
  7.2 122.8 %all-gather.3.cloned.1.call-start = ((), (), s32[]{:S(2)}) async-start(), calls=%async_computation.2 | async-start | bytes 5308416 | tf_op jit(solution)/shard_map/all_gather | solution.py:1238
  14.1 10.0 %collective-permute-start.5 = (bf16[96,768]{1,0:T(8,128)(2,1)S(1)}, bf16[96,768]{1,0:T(8,128)(2,1)}, u32[]{:S(2)}, u32[]{:S(2)}) collective-permute-start(bf16[96,768]{1,0:T(8,128)(2,1)S(1)} %bitcast.133), channel_id=1, source_target_pairs={{0,6},{1,7},{2,4},{3,5},{4,2},{5,3},{6,0},{7,1},{8,14},{9,15},{10,... | collective-permute-start | bytes 442376 | tf_op jit(solution)/shard_map/ppermute | solution.py:1002
  19.2 23.0 %collective-permute-start.4 = (bf16[96,768]{1,0:T(8,128)(2,1)S(1)}, bf16[96,768]{1,0:T(8,128)(2,1)}, u32[]{:S(2)}, u32[]{:S(2)}) collective-permute-start(bf16[96,768]{1,0:T(8,128)(2,1)S(1)} %bitcast.134), channel_id=1, source_target_pairs={{0,4},{1,5},{2,6},{3,7},{4,0},{5,1},{6,2},{7,3},{8,12},{9,13},{10,... | collective-permute-start | bytes 442376 | tf_op jit(solution)/shard_map/ppermute | solution.py:1002
  19.3 23.0 %collective-permute-start.3 = (bf16[96,768]{1,0:T(8,128)(2,1)S(1)}, bf16[96,768]{1,0:T(8,128)(2,1)}, u32[]{:S(2)}, u32[]{:S(2)}) collective-permute-start(bf16[96,768]{1,0:T(8,128)(2,1)S(1)} %bitcast.135), channel_id=1, source_target_pairs={{0,2},{1,3},{2,0},{3,1},{4,6},{5,7},{6,4},{7,5},{8,10},{9,11},{10,... | collective-permute-start | bytes 442376 | tf_op jit(solution)/shard_map/ppermute | solution.py:1002
  22.1 34.9 %collective-permute-start.6 = (bf16[96,3072]{1,0:T(8,128)(2,1)S(1)}, bf16[96,3072]{1,0:T(8,128)(2,1)}, u32[]{:S(2)}, u32[]{:S(2)}) collective-permute-start(bf16[96,3072]{1,0:T(8,128)(2,1)S(1)} %get-tuple-element.333), channel_id=1, source_target_pairs={{0,1},{1,0},{2,3},{3,2},{4,5},{5,4},{6,7},{7,6},{8,9},{9,8},{10,11... | collective-permute-start | bytes 1769480 | tf_op jit(solution)/shard_map/ppermute | solution.py:1005
  23.3 33.7 %collective-permute-start.7 = (bf16[384,768]{1,0:T(8,128)(2,1)}, bf16[384,768]{1,0:T(8,128)(2,1)}, u32[]{:S(2)}, u32[]{:S(2)}) collective-permute-start(bf16[384,768]{1,0:T(8,128)(2,1)} %get-tuple-element.330), channel_id=1, source_target_pairs={{0,1},{1,0},{2,3},{3,2},{4,5},{5,4},{6,7},{7,6},{8,9},{9,8},{10,11... | collective-permute-start | bytes 1769480 | tf_op jit(solution)/shard_map/ppermute | solution.py:1005
  23.8 40.2 %copy-start.30 = (s32[4,2,2]{0,2,1:T(2,128)S(1)}, s32[4,2,2]{0,2,1:T(2,128)}, u32[]{:S(2)}) copy-start(s32[4,2,2]{0,2,1:T(2,128)} %param.18) | copy-start | bytes 196
  23.8 40.9 %copy-start.31 = (bf16[2,196]{1,0:T(2,128)(2,1)S(1)}, bf16[2,196]{1,0:T(2,128)(2,1)}, u32[]{:S(2)}) copy-start(bf16[2,196]{1,0:T(2,128)(2,1)} %param.24) | copy-start | bytes 2356
  23.9 41.7 %copy-start.7 = (bf16[4,196,768]{2,0,1:T(4,128)(2,1)S(1)}, bf16[4,196,768]{2,0,1:T(4,128)(2,1)}, u32[]{:S(2)}) copy-start(bf16[4,196,768]{2,0,1:T(4,128)(2,1)} %param.16) | copy-start | bytes 3612676
  24.1 18.3 %collective-permute-start.2 = (bf16[2,96,768]{2,1,0:T(8,128)(2,1)S(1)}, bf16[2,96,768]{2,1,0:T(8,128)(2,1)S(1)}, u32[]{:S(2)}, u32[]{:S(2)}) collective-permute-start(bf16[2,96,768]{2,1,0:T(8,128)(2,1)S(1)} %pad_maximum_fusion.2), channel_id=1, source_target_pairs={{0,6},{1,7},{2,4},{3,5},{4,2},{5,3},{6,0},{7,1},{8,14},{9,15},{10,... | collective-permute-start | bytes 884744 | tf_op jit(solution)/shard_map/ppermute | solution.py:1002
  42.3 14.7 %collective-permute-start.1 = (bf16[2,96,768]{2,1,0:T(8,128)(2,1)S(1)}, bf16[2,96,768]{2,1,0:T(8,128)(2,1)S(1)}, u32[]{:S(2)}, u32[]{:S(2)}) collective-permute-start(bf16[2,96,768]{2,1,0:T(8,128)(2,1)S(1)} %pad_maximum_fusion.2), channel_id=1, source_target_pairs={{0,4},{1,5},{2,6},{3,7},{4,0},{5,1},{6,2},{7,3},{8,12},{9,13},{10,... | collective-permute-start | bytes 884744 | tf_op jit(solution)/shard_map/ppermute | solution.py:1002
  42.3 14.7 %collective-permute-start = (bf16[2,96,768]{2,1,0:T(8,128)(2,1)S(1)}, bf16[2,96,768]{2,1,0:T(8,128)(2,1)S(1)}, u32[]{:S(2)}, u32[]{:S(2)}) collective-permute-start(bf16[2,96,768]{2,1,0:T(8,128)(2,1)S(1)} %pad_maximum_fusion.2), channel_id=1, source_target_pairs={{0,2},{1,3},{2,0},{3,1},{4,6},{5,7},{6,4},{7,5},{8,10},{9,11},{10,... | collective-permute-start | bytes 884744 | tf_op jit(solution)/shard_map/ppermute | solution.py:1002
  57.1 104.2 %all-gather.5.cloned.1.call-start = ((), (), s32[]{:S(2)}) async-start(), calls=%async_computation.3 | async-start | bytes 5308416 | tf_op jit(solution)/shard_map/all_gather | solution.py:1239
  57.8 166.3 %reduce-scatter.3.cloned.1.call-start = ((), (), s32[]{:S(2)}) async-start(), calls=%async_computation.4 | async-start | bytes 5308416 | tf_op jit(solution)/shard_map/reduce_scatter | solution.py:1269
  58.9 8.6 %collective-permute-start.8 = (bf16[3,2,96,768]{3,2,1,0:T(8,128)(2,1)S(1)}, bf16[3,2,96,768]{3,2,1,0:T(8,128)(2,1)}, u32[]{:S(2)}, u32[]{:S(2)}) collective-permute-start(bf16[3,2,96,768]{3,2,1,0:T(8,128)(2,1)S(1)} %pad_maximum_fusion.rest_4_), channel_id=1, source_target_pairs={{0,1},{1,0},{2,3},{3,2},{4,5},{5,4},{6,7},{7,6},{8,9},{9,8},{10,11... | collective-permute-start | bytes 2654216 | tf_op jit(solution)/shard_map/ppermute | solution.py:1005
  59.0 22.2 %collective-permute-start.11 = (bf16[3,2,96,768]{3,2,1,0:T(8,128)(2,1)S(1)}, bf16[3,2,96,768]{3,2,1,0:T(8,128)(2,1)}, u32[]{:S(2)}, u32[]{:S(2)}) collective-permute-start(bf16[3,2,96,768]{3,2,1,0:T(8,128)(2,1)S(1)} %pad_maximum_fusion.rest_4_), channel_id=1, source_target_pairs={{0,16},{8,24},{16,0},{24,8},{1,17},{9,25},{17,1},{25,9},{2,18},{10... | collective-permute-start | bytes 2654216 | tf_op jit(solution)/shard_map/ppermute | solution.py:1008
  60.6 21.8 %collective-permute-start.10 = (bf16[3,2,96,768]{3,2,1,0:T(8,128)(2,1)S(1)}, bf16[3,2,96,768]{3,2,1,0:T(8,128)(2,1)}, u32[]{:S(2)}, u32[]{:S(2)}) collective-permute-start(bf16[3,2,96,768]{3,2,1,0:T(8,128)(2,1)S(1)} %pad_maximum_fusion.rest_4_), channel_id=1, source_target_pairs={{0,8},{8,0},{16,24},{24,16},{1,9},{9,1},{17,25},{25,17},{2,10},{10... | collective-permute-start | bytes 2654216 | tf_op jit(solution)/shard_map/ppermute | solution.py:1008
  63.2 4.3 %collective-permute-start.9 = (bf16[4,96,768]{2,1,0:T(8,128)(2,1)S(1)}, bf16[4,96,768]{2,1,0:T(8,128)(2,1)S(1)}, u32[]{:S(2)}, u32[]{:S(2)}) collective-permute-start(bf16[4,96,768]{2,1,0:T(8,128)(2,1)S(1)} %pad_maximum_fusion.1.own), channel_id=1, source_target_pairs={{0,1},{1,0},{2,3},{3,2},{4,5},{5,4},{6,7},{7,6},{8,9},{9,8},{10,11... | collective-permute-start | bytes 1769480 | tf_op jit(solution)/shard_map/ppermute | solution.py:1005
  82.4 15.0 %collective-permute-start.15 = (bf16[3,2,96,768]{3,2,1,0:T(8,128)(2,1)}, bf16[3,2,96,768]{3,2,1,0:T(8,128)(2,1)S(1)}, u32[]{:S(2)}, u32[]{:S(2)}) collective-permute-start(bf16[3,2,96,768]{3,2,1,0:T(8,128)(2,1)} %collective-permute-done.11.rest_6_), channel_id=1, source_target_pairs={{0,1},{1,0},{2,3},{3,2},{4,5},{5,4},{6,7},{7,6},{8,9},{9,8},{10,11... | collective-permute-start | bytes 2654216 | tf_op jit(solution)/shard_map/ppermute | solution.py:1005
  82.4 15.0 %collective-permute-start.14 = (bf16[3,2,96,768]{3,2,1,0:T(8,128)(2,1)}, bf16[3,2,96,768]{3,2,1,0:T(8,128)(2,1)S(1)}, u32[]{:S(2)}, u32[]{:S(2)}) collective-permute-start(bf16[3,2,96,768]{3,2,1,0:T(8,128)(2,1)} %collective-permute-done.10.rest_5_), channel_id=1, source_target_pairs={{0,1},{1,0},{2,3},{3,2},{4,5},{5,4},{6,7},{7,6},{8,9},{9,8},{10,11... | collective-permute-start | bytes 2654216 | tf_op jit(solution)/shard_map/ppermute | solution.py:1005
  85.0 12.1 %collective-permute-start.13 = (bf16[3,1,96,768]{3,2,1,0:T(8,128)(2,1)S(1)}, bf16[3,1,96,768]{3,2,1,0:T(8,128)(2,1)S(1)}, u32[]{:S(2)}, u32[]{:S(2)}) collective-permute-start(bf16[3,1,96,768]{3,2,1,0:T(8,128)(2,1)S(1)} %slice.190), channel_id=1, source_target_pairs={{0,16},{8,24},{16,0},{24,8},{1,17},{9,25},{17,1},{25,9},{2,18},{10... | collective-permute-start | bytes 1327112 | tf_op jit(solution)/shard_map/ppermute | solution.py:1008
  85.6 11.8 %collective-permute-start.12 = (bf16[3,1,96,768]{3,2,1,0:T(8,128)(2,1)S(1)}, bf16[3,1,96,768]{3,2,1,0:T(8,128)(2,1)S(1)}, u32[]{:S(2)}, u32[]{:S(2)}) collective-permute-start(bf16[3,1,96,768]{3,2,1,0:T(8,128)(2,1)S(1)} %slice.189), channel_id=1, source_target_pairs={{0,8},{8,0},{16,24},{24,16},{1,9},{9,1},{17,25},{25,17},{2,10},{10... | collective-permute-start | bytes 1327112 | tf_op jit(solution)/shard_map/ppermute | solution.py:1008
  97.5 2.7 collective-permute-start.16
  149.3 123.5 %reduce-scatter.5.cloned.1.call-start = ((), (), s32[]{:S(2)}) async-start(), calls=%async_computation.5 | async-start | bytes 5308416 | tf_op jit(solution)/shard_map/reduce_scatter | solution.py:1271
  203.6 20.4 %collective-permute-start.17 = (bf16[4,4,96,768]{3,2,1,0:T(8,128)(2,1)}, bf16[4,4,96,768]{3,2,1,0:T(8,128)(2,1)}, u32[]{:S(2)}, u32[]{:S(2)}) collective-permute-start(bf16[4,4,96,768]{3,2,1,0:T(8,128)(2,1)} %get-tuple-element.217), channel_id=1, source_target_pairs={{0,1},{1,0},{2,3},{3,2},{4,5},{5,4},{6,7},{7,6},{8,9},{9,8},{10,11... | collective-permute-start | bytes 7077896 | tf_op jit(solution)/shard_map/ppermute | solution.py:1005
  203.8 20.6 %copy-start.4 = (bf16[4,4,96,768]{3,2,1,0:T(8,128)(2,1)S(1)}, bf16[4,4,96,768]{3,2,1,0:T(8,128)(2,1)}, u32[]{:S(2)}) copy-start(bf16[4,4,96,768]{3,2,1,0:T(8,128)(2,1)} %get-tuple-element.234) | copy-start | bytes 7077892
  224.1 21.4 %collective-permute-start.18 = (bf16[4,4,96,768]{3,2,1,0:T(8,128)(2,1)}, bf16[4,4,96,768]{3,2,1,0:T(8,128)(2,1)}, u32[]{:S(2)}, u32[]{:S(2)}) collective-permute-start(bf16[4,4,96,768]{3,2,1,0:T(8,128)(2,1)} %get-tuple-element.233), channel_id=1, source_target_pairs={{0,1},{1,0},{2,3},{3,2},{4,5},{5,4},{6,7},{7,6},{8,9},{9,8},{10,11... | collective-permute-start | bytes 7077896 | tf_op jit(solution)/shard_map/ppermute | solution.py:1005
  226.8 17.7 %collective-permute-start.20 = (bf16[2,2,96,768]{3,2,1,0:T(8,128)(2,1)}, bf16[2,2,96,768]{3,2,1,0:T(8,128)(2,1)S(1)}, u32[]{:S(2)}, u32[]{:S(2)}) collective-permute-start(bf16[2,2,96,768]{3,2,1,0:T(8,128)(2,1)} %get-tuple-element.328), channel_id=1, source_target_pairs={{0,16},{8,24},{16,0},{24,8},{1,17},{9,25},{17,1},{25,9},{2,18},{10... | collective-permute-start | bytes 1769480 | tf_op jit(solution)/shard_map/ppermute | solution.py:1008
  229.7 15.9 %collective-permute-start.19 = (bf16[2,2,96,768]{3,2,1,0:T(8,128)(2,1)}, bf16[2,2,96,768]{3,2,1,0:T(8,128)(2,1)S(1)}, u32[]{:S(2)}, u32[]{:S(2)}) collective-permute-start(bf16[2,2,96,768]{3,2,1,0:T(8,128)(2,1)} %get-tuple-element.329), channel_id=1, source_target_pairs={{0,8},{8,0},{16,24},{24,16},{1,9},{9,1},{17,25},{25,17},{2,10},{10... | collective-permute-start | bytes 1769480 | tf_op jit(solution)/shard_map/ppermute | solution.py:1008
  245.5 7.5 %collective-permute-start.26 = (f32[32,768]{1,0:T(8,128)}, f32[32,768]{1,0:T(8,128)S(1)}, u32[]{:S(2)}, u32[]{:S(2)}) collective-permute-start(f32[32,768]{1,0:T(8,128)} %get-tuple-element.245), channel_id=1, source_target_pairs={{0,1},{1,0},{2,3},{3,2},{4,5},{5,4},{6,7},{7,6},{8,9},{9,8},{10,11... | collective-permute-start | bytes 294920 | tf_op jit(solution)/shard_map/ppermute | solution.py:1175
  245.5 27.3 %collective-permute-start.25 = (bf16[4,4,48,256]{3,2,1,0:T(8,128)(2,1)}, bf16[4,4,48,256]{3,2,1,0:T(8,128)(2,1)}, u32[]{:S(2)}, u32[]{:S(2)}) collective-permute-start(bf16[4,4,48,256]{3,2,1,0:T(8,128)(2,1)} %get-tuple-element.244), channel_id=1, source_target_pairs={{0,1},{1,0},{2,3},{3,2},{4,5},{5,4},{6,7},{7,6},{8,9},{9,8},{10,11... | collective-permute-start | bytes 1179656 | tf_op jit(solution)/shard_map/ppermute | solution.py:1005
  248.4 24.5 %collective-permute-start.22 = (bf16[2,2,96,768]{3,2,1,0:T(8,128)(2,1)}, bf16[2,2,96,768]{3,2,1,0:T(8,128)(2,1)S(1)}, u32[]{:S(2)}, u32[]{:S(2)}) collective-permute-start(bf16[2,2,96,768]{3,2,1,0:T(8,128)(2,1)} %get-tuple-element.326), channel_id=1, source_target_pairs={{0,16},{8,24},{16,0},{24,8},{1,17},{9,25},{17,1},{25,9},{2,18},{10... | collective-permute-start | bytes 1769480 | tf_op jit(solution)/shard_map/ppermute | solution.py:1008
  248.7 24.2 %collective-permute-start.21 = (bf16[2,2,96,768]{3,2,1,0:T(8,128)(2,1)}, bf16[2,2,96,768]{3,2,1,0:T(8,128)(2,1)S(1)}, u32[]{:S(2)}, u32[]{:S(2)}) collective-permute-start(bf16[2,2,96,768]{3,2,1,0:T(8,128)(2,1)} %get-tuple-element.327), channel_id=1, source_target_pairs={{0,8},{8,0},{16,24},{24,16},{1,9},{9,1},{17,25},{25,17},{2,10},{10... | collective-permute-start | bytes 1769480 | tf_op jit(solution)/shard_map/ppermute | solution.py:1008
  252.8 20.0 %collective-permute-start.24 = (bf16[2,96,768]{2,1,0:T(8,128)(2,1)}, bf16[2,96,768]{2,1,0:T(8,128)(2,1)}, u32[]{:S(2)}, u32[]{:S(2)}) collective-permute-start(bf16[2,96,768]{2,1,0:T(8,128)(2,1)} %get-tuple-element.324), channel_id=1, source_target_pairs={{0,8},{8,0},{16,24},{24,16},{1,9},{9,1},{17,25},{25,17},{2,10},{10... | collective-permute-start | bytes 884744 | tf_op jit(solution)/shard_map/ppermute | solution.py:1008
  253.0 19.8 %collective-permute-start.23 = (bf16[2,96,768]{2,1,0:T(8,128)(2,1)}, bf16[2,96,768]{2,1,0:T(8,128)(2,1)}, u32[]{:S(2)}, u32[]{:S(2)}) collective-permute-start(bf16[2,96,768]{2,1,0:T(8,128)(2,1)} %get-tuple-element.325), channel_id=1, source_target_pairs={{0,16},{8,24},{16,0},{24,8},{1,17},{9,25},{17,1},{25,9},{2,18},{10... | collective-permute-start | bytes 884744 | tf_op jit(solution)/shard_map/ppermute | solution.py:1008
  274.7 24.3 %copy-start.9 = (bf16[4,208,768]{2,1,0:T(8,128)(2,1)S(1)}, bf16[4,208,768]{2,1,0:T(8,128)(2,1)}, u32[]{:S(2)}) copy-start(bf16[4,208,768]{2,1,0:T(8,128)(2,1)} %last_out.1) | copy-start | bytes 3833860
  274.8 7.7 %collective-permute-start.37 = (f32[32,768]{1,0:T(8,128)S(1)}, f32[32,768]{1,0:T(8,128)S(1)}, u32[]{:S(2)}, u32[]{:S(2)}) collective-permute-start(f32[32,768]{1,0:T(8,128)S(1)} %copy-done.22), channel_id=1, source_target_pairs={{0,2},{1,3},{2,0},{3,1},{4,6},{5,7},{6,4},{7,5},{8,10},{9,11},{10,... | collective-permute-start | bytes 294920 | tf_op jit(solution)/shard_map/ppermute | solution.py:1175
  276.1 7.5 %collective-permute-start.34 = (bf16[4,48,256]{2,1,0:T(8,128)(2,1)S(1)}, bf16[4,48,256]{2,1,0:T(8,128)(2,1)S(1)}, u32[]{:S(2)}, u32[]{:S(2)}) collective-permute-start(bf16[4,48,256]{2,1,0:T(8,128)(2,1)S(1)} %get-tuple-element.336), channel_id=1, source_target_pairs={{0,6},{1,7},{2,4},{3,5},{4,2},{5,3},{6,0},{7,1},{8,14},{9,15},{10,... | collective-permute-start | bytes 294920 | tf_op jit(solution)/shard_map/ppermute | solution.py:1002
  277.3 14.0 %collective-permute-start.33 = (bf16[4,48,256]{2,1,0:T(8,128)(2,1)S(1)}, bf16[4,48,256]{2,1,0:T(8,128)(2,1)S(1)}, u32[]{:S(2)}, u32[]{:S(2)}) collective-permute-start(bf16[4,48,256]{2,1,0:T(8,128)(2,1)S(1)} %get-tuple-element.337), channel_id=1, source_target_pairs={{0,4},{1,5},{2,6},{3,7},{4,0},{5,1},{6,2},{7,3},{8,12},{9,13},{10,... | collective-permute-start | bytes 294920 | tf_op jit(solution)/shard_map/ppermute | solution.py:1002
  279.5 28.8 %collective-permute-start.35 = (bf16[96,3072]{1,0:T(8,128)(2,1)S(1)}, bf16[96,3072]{1,0:T(8,128)(2,1)S(1)}, u32[]{:S(2)}, u32[]{:S(2)}) collective-permute-start(bf16[96,3072]{1,0:T(8,128)(2,1)S(1)} %copy-done.16), channel_id=1, source_target_pairs={{0,8},{8,0},{16,24},{24,16},{1,9},{9,1},{17,25},{25,17},{2,10},{10... | collective-permute-start | bytes 1769480 | tf_op jit(solution)/shard_map/ppermute | solution.py:1008
  281.0 27.4 %collective-permute-start.36 = (bf16[1,768,384]{2,1,0:T(8,128)(2,1)S(1)}, bf16[1,768,384]{2,1,0:T(8,128)(2,1)S(1)}, u32[]{:S(2)}, u32[]{:S(2)}) collective-permute-start(bf16[1,768,384]{2,1,0:T(8,128)(2,1)S(1)} %copy-done.15), channel_id=1, source_target_pairs={{0,16},{8,24},{16,0},{24,8},{1,17},{9,25},{17,1},{25,9},{2,18},{10... | collective-permute-start | bytes 1769480 | tf_op jit(solution)/shard_map/ppermute | solution.py:1008
  282.5 15.1 %collective-permute-start.29 = (bf16[96,768]{1,0:T(8,128)(2,1)S(1)}, bf16[96,768]{1,0:T(8,128)(2,1)S(1)}, u32[]{:S(2)}, u32[]{:S(2)}) collective-permute-start(bf16[96,768]{1,0:T(8,128)(2,1)S(1)} %slice_bitcast_fusion.11), channel_id=1, source_target_pairs={{0,2},{1,3},{2,0},{3,1},{4,6},{5,7},{6,4},{7,5},{8,10},{9,11},{10,... | collective-permute-start | bytes 442376 | tf_op jit(solution)/shard_map/ppermute | solution.py:1002
  283.6 15.5 %collective-permute-start.31 = (bf16[96,768]{1,0:T(8,128)(2,1)S(1)}, bf16[96,768]{1,0:T(8,128)(2,1)S(1)}, u32[]{:S(2)}, u32[]{:S(2)}) collective-permute-start(bf16[96,768]{1,0:T(8,128)(2,1)S(1)} %get-tuple-element.341), channel_id=1, source_target_pairs={{0,6},{1,7},{2,4},{3,5},{4,2},{5,3},{6,0},{7,1},{8,14},{9,15},{10,... | collective-permute-start | bytes 442376 | tf_op jit(solution)/shard_map/ppermute | solution.py:1002
  291.4 4.6 %collective-permute-start.32 = (bf16[4,48,256]{2,1,0:T(8,128)(2,1)S(1)}, bf16[4,48,256]{2,1,0:T(8,128)(2,1)S(1)}, u32[]{:S(2)}, u32[]{:S(2)}) collective-permute-start(bf16[4,48,256]{2,1,0:T(8,128)(2,1)S(1)} %get-tuple-element.338), channel_id=1, source_target_pairs={{0,2},{1,3},{2,0},{3,1},{4,6},{5,7},{6,4},{7,5},{8,10},{9,11},{10,... | collective-permute-start | bytes 294920 | tf_op jit(solution)/shard_map/ppermute | solution.py:1002
  296.0 12.4 %collective-permute-start.28 = (bf16[2,96,768]{2,1,0:T(8,128)(2,1)S(1)}, bf16[2,96,768]{2,1,0:T(8,128)(2,1)S(1)}, u32[]{:S(2)}, u32[]{:S(2)}) collective-permute-start(bf16[2,96,768]{2,1,0:T(8,128)(2,1)S(1)} %get-tuple-element.322), channel_id=1, source_target_pairs={{0,8},{8,0},{16,24},{24,16},{1,9},{9,1},{17,25},{25,17},{2,10},{10... | collective-permute-start | bytes 884744 | tf_op jit(solution)/shard_map/ppermute | solution.py:1008
  297.6 10.8 %collective-permute-start.27 = (bf16[2,96,768]{2,1,0:T(8,128)(2,1)S(1)}, bf16[2,96,768]{2,1,0:T(8,128)(2,1)S(1)}, u32[]{:S(2)}, u32[]{:S(2)}) collective-permute-start(bf16[2,96,768]{2,1,0:T(8,128)(2,1)S(1)} %get-tuple-element.323), channel_id=1, source_target_pairs={{0,16},{8,24},{16,0},{24,8},{1,17},{9,25},{17,1},{25,9},{2,18},{10... | collective-permute-start | bytes 884744 | tf_op jit(solution)/shard_map/ppermute | solution.py:1008
  299.1 9.3 %collective-permute-start.30 = (bf16[96,768]{1,0:T(8,128)(2,1)S(1)}, bf16[96,768]{1,0:T(8,128)(2,1)S(1)}, u32[]{:S(2)}, u32[]{:S(2)}) collective-permute-start(bf16[96,768]{1,0:T(8,128)(2,1)S(1)} %get-tuple-element.342), channel_id=1, source_target_pairs={{0,4},{1,5},{2,6},{3,7},{4,0},{5,1},{6,2},{7,3},{8,12},{9,13},{10,... | collective-permute-start | bytes 442376 | tf_op jit(solution)/shard_map/ppermute | solution.py:1002
  308.8 6.0 %collective-permute-start.41 = (bf16[4,48,256]{2,1,0:T(8,128)(2,1)S(1)}, bf16[4,48,256]{2,1,0:T(8,128)(2,1)S(1)}, u32[]{:S(2)}, u32[]{:S(2)}) collective-permute-start(bf16[4,48,256]{2,1,0:T(8,128)(2,1)S(1)} %fusion.8), channel_id=1, source_target_pairs={{0,8},{8,0},{16,24},{24,16},{1,9},{9,1},{17,25},{25,17},{2,10},{10... | collective-permute-start | bytes 294920 | tf_op jit(solution)/shard_map/ppermute | solution.py:1008
  309.4 8.0 %collective-permute-start.45 = (f32[32,768]{1,0:T(8,128)S(1)}, f32[32,768]{1,0:T(8,128)S(1)}, u32[]{:S(2)}, u32[]{:S(2)}) collective-permute-start(f32[32,768]{1,0:T(8,128)S(1)} %add.242), channel_id=1, source_target_pairs={{0,4},{1,5},{2,6},{3,7},{4,0},{5,1},{6,2},{7,3},{8,12},{9,13},{10,... | collective-permute-start | bytes 294920 | tf_op jit(solution)/shard_map/ppermute | solution.py:1175
  311.0 7.7 %collective-permute-start.38 = (bf16[96,768]{1,0:T(8,128)(2,1)S(1)}, bf16[96,768]{1,0:T(8,128)(2,1)S(1)}, u32[]{:S(2)}, u32[]{:S(2)}) collective-permute-start(bf16[96,768]{1,0:T(8,128)(2,1)S(1)} %slice_bitcast_fusion.8), channel_id=1, source_target_pairs={{0,2},{1,3},{2,0},{3,1},{4,6},{5,7},{6,4},{7,5},{8,10},{9,11},{10,... | collective-permute-start | bytes 442376 | tf_op jit(solution)/shard_map/ppermute | solution.py:1002
  312.3 14.5 %collective-permute-start.43 = (bf16[96,3072]{1,0:T(8,128)(2,1)S(1)}, bf16[96,3072]{1,0:T(8,128)(2,1)S(1)}, u32[]{:S(2)}, u32[]{:S(2)}) collective-permute-start(bf16[96,3072]{1,0:T(8,128)(2,1)S(1)} %add.257.grad_in), channel_id=1, source_target_pairs={{0,16},{8,24},{16,0},{24,8},{1,17},{9,25},{17,1},{25,9},{2,18},{10... | collective-permute-start | bytes 1769480 | tf_op jit(solution)/shard_map/ppermute | solution.py:1008
  312.7 14.1 %collective-permute-start.44 = (bf16[1,768,384]{2,1,0:T(8,128)(2,1)S(1)}, bf16[1,768,384]{2,1,0:T(8,128)(2,1)S(1)}, u32[]{:S(2)}, u32[]{:S(2)}) collective-permute-start(bf16[1,768,384]{2,1,0:T(8,128)(2,1)S(1)} %add.258.grad_out), channel_id=1, source_target_pairs={{0,8},{8,0},{16,24},{24,16},{1,9},{9,1},{17,25},{25,17},{2,10},{10... | collective-permute-start | bytes 1769480 | tf_op jit(solution)/shard_map/ppermute | solution.py:1008
  314.8 7.0 %collective-permute-start.40 = (bf16[96,768]{1,0:T(8,128)(2,1)S(1)}, bf16[96,768]{1,0:T(8,128)(2,1)S(1)}, u32[]{:S(2)}, u32[]{:S(2)}) collective-permute-start(bf16[96,768]{1,0:T(8,128)(2,1)S(1)} %get-tuple-element.339), channel_id=1, source_target_pairs={{0,6},{1,7},{2,4},{3,5},{4,2},{5,3},{6,0},{7,1},{8,14},{9,15},{10,... | collective-permute-start | bytes 442376 | tf_op jit(solution)/shard_map/ppermute | solution.py:1002
  317.4 7.6 %collective-permute-start.39 = (bf16[96,768]{1,0:T(8,128)(2,1)S(1)}, bf16[96,768]{1,0:T(8,128)(2,1)S(1)}, u32[]{:S(2)}, u32[]{:S(2)}) collective-permute-start(bf16[96,768]{1,0:T(8,128)(2,1)S(1)} %get-tuple-element.340), channel_id=1, source_target_pairs={{0,4},{1,5},{2,6},{3,7},{4,0},{5,1},{6,2},{7,3},{8,12},{9,13},{10,... | collective-permute-start | bytes 442376 | tf_op jit(solution)/shard_map/ppermute | solution.py:1002
  318.7 8.1 %collective-permute-start.42 = (bf16[96,768]{1,0:T(8,128)(2,1)S(1)}, bf16[96,768]{1,0:T(8,128)(2,1)S(1)}, u32[]{:S(2)}, u32[]{:S(2)}) collective-permute-start(bf16[96,768]{1,0:T(8,128)(2,1)S(1)} %fusion.5), channel_id=1, source_target_pairs={{0,16},{8,24},{16,0},{24,8},{1,17},{9,25},{17,1},{25,9},{2,18},{10... | collective-permute-start | bytes 442376 | tf_op jit(solution)/shard_map/ppermute | solution.py:1008
  326.8 17.3 %copy-start.19 = (bf16[96,768]{1,0:T(8,128)(2,1)}, bf16[96,768]{1,0:T(8,128)(2,1)S(1)}, u32[]{:S(2)}) copy-start(bf16[96,768]{1,0:T(8,128)(2,1)S(1)} %collective-permute-done.42) | copy-start | bytes 442372
  326.8 10.1 %collective-permute-start.53 = (f32[32,768]{1,0:T(8,128)}, f32[32,768]{1,0:T(8,128)}, u32[]{:S(2)}, u32[]{:S(2)}) collective-permute-start(f32[32,768]{1,0:T(8,128)} %add.259), channel_id=1, source_target_pairs={{0,24},{8,16},{16,8},{24,0},{1,25},{9,17},{17,9},{25,1},{2,26},{10... | collective-permute-start | bytes 294920 | tf_op jit(solution)/shard_map/ppermute | solution.py:1008
  328.8 9.1 %collective-permute-start.52 = (f32[32,768]{1,0:T(8,128)}, f32[32,768]{1,0:T(8,128)}, u32[]{:S(2)}, u32[]{:S(2)}) collective-permute-start(f32[32,768]{1,0:T(8,128)} %add.259), channel_id=1, source_target_pairs={{0,16},{8,24},{16,0},{24,8},{1,17},{9,25},{17,1},{25,9},{2,18},{10... | collective-permute-start | bytes 294920 | tf_op jit(solution)/shard_map/ppermute | solution.py:1008
  330.4 5.0 %collective-permute-start.50 = (bf16[4,48,256]{2,1,0:T(8,128)(2,1)S(1)}, bf16[4,48,256]{2,1,0:T(8,128)(2,1)S(1)}, u32[]{:S(2)}, u32[]{:S(2)}) collective-permute-start(bf16[4,48,256]{2,1,0:T(8,128)(2,1)S(1)} %add.263), channel_id=1, source_target_pairs={{0,16},{8,24},{16,0},{24,8},{1,17},{9,25},{17,1},{25,9},{2,18},{10... | collective-permute-start | bytes 294920 | tf_op jit(solution)/shard_map/ppermute | solution.py:1008
  331.7 16.7 %collective-permute-start.49 = (bf16[2,96,768]{2,1,0:T(8,128)(2,1)}, bf16[2,96,768]{2,1,0:T(8,128)(2,1)S(1)}, u32[]{:S(2)}, u32[]{:S(2)}) collective-permute-start(bf16[2,96,768]{2,1,0:T(8,128)(2,1)} %pad_maximum_fusion.3), channel_id=1, source_target_pairs={{0,8},{8,0},{16,24},{24,16},{1,9},{9,1},{17,25},{25,17},{2,10},{10... | collective-permute-start | bytes 884744 | tf_op jit(solution)/shard_map/ppermute | solution.py:1008
  332.6 15.7 %collective-permute-start.48 = (bf16[96,768]{1,0:T(8,128)(2,1)}, bf16[96,768]{1,0:T(8,128)(2,1)}, u32[]{:S(2)}, u32[]{:S(2)}) collective-permute-start(bf16[96,768]{1,0:T(8,128)(2,1)} %fusion.2), channel_id=1, source_target_pairs={{0,24},{8,16},{16,8},{24,0},{1,25},{9,17},{17,9},{25,1},{2,26},{10... | collective-permute-start | bytes 442376 | tf_op jit(solution)/shard_map/ppermute | solution.py:1008
  336.1 12.2 %collective-permute-start.47 = (bf16[96,768]{1,0:T(8,128)(2,1)}, bf16[96,768]{1,0:T(8,128)(2,1)}, u32[]{:S(2)}, u32[]{:S(2)}) collective-permute-start(bf16[96,768]{1,0:T(8,128)(2,1)} %fusion.2), channel_id=1, source_target_pairs={{0,16},{8,24},{16,0},{24,8},{1,17},{9,25},{17,1},{25,9},{2,18},{10... | collective-permute-start | bytes 442376 | tf_op jit(solution)/shard_map/ppermute | solution.py:1008
  337.0 11.4 %collective-permute-start.46 = (bf16[96,768]{1,0:T(8,128)(2,1)}, bf16[96,768]{1,0:T(8,128)(2,1)}, u32[]{:S(2)}, u32[]{:S(2)}) collective-permute-start(bf16[96,768]{1,0:T(8,128)(2,1)} %fusion.2), channel_id=1, source_target_pairs={{0,8},{8,0},{16,24},{24,16},{1,9},{9,1},{17,25},{25,17},{2,10},{10... | collective-permute-start | bytes 442376 | tf_op jit(solution)/shard_map/ppermute | solution.py:1008
  338.0 10.3 %collective-permute-start.51 = (f32[32,768]{1,0:T(8,128)}, f32[32,768]{1,0:T(8,128)}, u32[]{:S(2)}, u32[]{:S(2)}) collective-permute-start(f32[32,768]{1,0:T(8,128)} %add.259), channel_id=1, source_target_pairs={{0,8},{8,0},{16,24},{24,16},{1,9},{9,1},{17,25},{25,17},{2,10},{10... | collective-permute-start | bytes 294920 | tf_op jit(solution)/shard_map/ppermute | solution.py:1008
  (29 other events, 184.0 us)
Sparse Core Ops, SparseCore 0:
  57.2 51.8 all-gather.2
  110.7 50.5 all-gather.4
  163.6 53.7 reduce-scatter.2
  219.5 53.2 reduce-scatter.4
